TPU v7x, 1024 devices: a whole 8x8x8 slice. The times are simulated.
1024 devices in a mesh: slab: 64 (over x, z), layer: 16 (over y, core).
Axes of the slice: x: 8, y: 8, z: 8, core: 2. Of those that a mesh axis runs over, the one named last changes fastest.
Arguments:
- adjoint_source: float32 [16, 1024, 4096], P('layer', 'slab')
- conductivity: float32 [16, 1024, 4096], P('layer', 'slab'), may hold values from 0.3 to 3
- tile_owner: int32 [8, 32], replicated, may hold values from 0 to 63, as said below
Outputs:
- adjoint: float32 [16, 1024, 4096], P('layer', 'slab')
- owned_grad: float32 [256, 128, 128], P('slab', 'layer')
Inputs may be any that keep to these rules, and one draw needn't show every extreme that they name: `tile_owner`: every owner holds exactly 4 tiles, and in every row of tiles each owner holds at most 1 tile; in every row some owner holds 1 tile.
All inputs are finite; a program needn't handle non-finite values.
Results may differ from a plain program's by a relative error of at most 0.0003.
Values sent between devices are 32-bit elements; how exact they have to be, the bound alone decides.
No kernel may reach another device: no remote copies, remote signals or barrier semaphores. Data moves between devices by JAX's collectives and lax.ppermute only.
A program may use at most 32 MiB of HBM per device.

v0:
```python
import jax
import jax.numpy as jnp
from jax import lax
from jax.sharding import PartitionSpec as P

TILE = 128
ITERS = 3


def padded_2(block, sides, width):
    for axis, dim in sides:
        count = lax.axis_size(axis)
        forward = [(i, i + 1) for i in range(count - 1)]
        backward = [(target, source) for source, target in forward]
        low = lax.ppermute(
            lax.slice_in_dim(block, block.shape[dim] - width, None, axis=dim), axis, forward
        )
        high = lax.ppermute(lax.slice_in_dim(block, 0, width, axis=dim), axis, backward)
        block = jnp.concatenate([low, block, high], axis=dim)
    return block


def neighbours(padded):
    return [
        padded[2:, 1:-1, 1:-1],
        padded[:-2, 1:-1, 1:-1],
        padded[1:-1, 2:, 1:-1],
        padded[1:-1, :-2, 1:-1],
        padded[1:-1, 1:-1, 2:],
        padded[1:-1, 1:-1, :-2],
    ]


def extend(field):
    framed = padded_2(field, (("slab", 1), ("layer", 0)), 1)
    return jnp.pad(framed, ((0, 0), (0, 0), (1, 1)))


def per_device(adjoint_source, conductivity, tile_owner):
    layer_depth, row_count, column_count = adjoint_source.shape
    slab_count = lax.axis_size("slab")
    face_conds = [
        0.5 * (conductivity + near_cond) for near_cond in neighbours(extend(conductivity))
    ]
    diagonal = jnp.zeros_like(conductivity)
    for face_cond in face_conds:
        diagonal = diagonal + face_cond
    inverse = 1.0 / diagonal
    solution = jnp.zeros_like(adjoint_source)
    residual = adjoint_source

    def combined(value):
        slab_total = lax.psum(value, "slab")
        return lax.psum(slab_total, "layer")

    precond = inverse * residual
    direction = precond
    inner_now = combined(jnp.sum(residual * precond))
    for iteration in range(ITERS):
        result = jnp.zeros_like(direction)
        for apply_face_cond, near_field in zip(face_conds, neighbours(extend(direction))):
            result = result + apply_face_cond * (direction - near_field)
        step_size = inner_now / combined(jnp.sum(direction * result))
        solution = solution + step_size * direction
        residual = residual - step_size * result
        if iteration + 1 < ITERS:
            precond = inverse * residual
            inner_next = combined(jnp.sum(residual * precond))
            direction = precond + inner_next / inner_now * direction
            inner_now = inner_next
    partial_map = jnp.sum(solution, axis=0)
    tiles_across = tile_owner.shape[1]
    tile_rows = tile_owner.shape[0]
    blocks = partial_map.reshape(row_count, tiles_across, TILE)
    owner_index = lax.axis_index("slab")
    per_tile = TILE // row_count
    capacity = max(1, tiles_across // slab_count)
    owned_count = tile_rows * tiles_across // slab_count
    same_owner = tile_owner[:, :, None] == tile_owner[:, None, :]
    earlier = jnp.arange(tiles_across)[None, :] < jnp.arange(tiles_across)[:, None]
    slot_table = jnp.sum((same_owner & earlier[None, :, :]).astype(jnp.int32), axis=2)
    my_row = owner_index // per_tile
    row_owner = lax.dynamic_index_in_dim(tile_owner, my_row, 0, keepdims=False)
    row_slot = lax.dynamic_index_in_dim(slot_table, my_row, 0, keepdims=False)
    select = (
        (row_owner[None, None, :] == jnp.arange(slab_count, dtype=jnp.int32)[:, None, None])
        & (row_slot[None, None, :] == jnp.arange(capacity, dtype=jnp.int32)[None, :, None])
    ).astype(jnp.float32)
    flat_owner = tile_owner.reshape(-1)
    flat_slot = slot_table.reshape(-1)
    flat_row = jnp.arange(tile_rows * tiles_across, dtype=jnp.int32) // tiles_across
    owned_flag = flat_owner == owner_index
    owned_rank = jnp.cumsum(owned_flag.astype(jnp.int32)) - 1
    picked = owned_flag[None, :] & (
        owned_rank[None, :] == jnp.arange(owned_count, dtype=jnp.int32)[:, None]
    )
    tile_row_of = jnp.sum(jnp.where(picked, flat_row[None, :], 0), axis=1)
    tile_slot_of = jnp.sum(jnp.where(picked, flat_slot[None, :], 0), axis=1)
    sender = tile_row_of[:, None] * per_tile + jnp.arange(per_tile, dtype=jnp.int32)[None, :]
    gather_sel = (
        (sender[:, :, None, None] == jnp.arange(slab_count, dtype=jnp.int32)[None, None, :, None])
        & (
            tile_slot_of[:, None, None, None]
            == jnp.arange(capacity, dtype=jnp.int32)[None, None, None, :]
        )
    ).astype(jnp.float32)
    strips = lax.psum_scatter(blocks, "layer", scatter_dimension=2, tiled=True)
    strip_width = strips.shape[2]
    outgoing = jnp.einsum("ojc,xcw->ojwx", select, strips, precision=lax.Precision.HIGHEST)
    outgoing = outgoing.reshape(slab_count, capacity, strip_width * row_count)
    received = lax.all_to_all(outgoing, "slab", split_axis=0, concat_axis=0, tiled=True)
    shaped = received.reshape(slab_count, capacity, strip_width, row_count)
    placed = jnp.einsum("kqsj,sjwx->kwqx", gather_sel, shaped, precision=lax.Precision.HIGHEST)
    owned_tiles = placed.reshape(owned_count, strip_width, TILE)
    return (solution, owned_tiles)


def solution(mesh):
    placed = (P("layer", "slab", None), P("layer", "slab", None), P())
    return jax.shard_map(
        per_device,
        mesh=mesh,
        in_specs=placed,
        out_specs=(P("layer", "slab", None), P("slab", "layer", None)),
        check_vma=False,
    )
```

profile of v0, /device:TPU:1, one launch (start us, length us, event | category | flops | bytes accessed | tf_op | source)
XLA Modules:
  0.0 1058.0 jit_solution(12654339260225229527)
XLA Ops:
  8.2 5.7 collective-permute-start
  15.3 4.7 collective-permute-done.1
  21.0 11.3 %collective-permute-start.2 = (f32[1,18,4096]{2,1,0:T(8,128)S(1)}, f32[1,18,4096]{2,1,0:T(8,128)S(1)}, u32[]{:S(2)}, u32[]{:S(2)}) collective-permute-start(f32[1,18,4096]{2,1,0:T(8,128)S(1)} %pad_maximum_fusion), channel_id=1, source_target_pairs={{1,0},{2,1},{3,2},{4,3},{5,4},{6,5},{7,6},{8,7},{9,8},{10,9},{11,1... | collective-permute-start | bytes 884744 | tf_op jit(solution)/shard_map/ppermute | solution.py:18
  34.3 4.7 collective-permute-done.3
  43.5 3.3 collective-permute-done.5
  48.7 5.7 collective-permute-start.7
  54.4 3.5 collective-permute-done.6
  60.8 117.7 %all-reduce.4 = (f32[]{:T(128)}, f32[]{:T(128)}) all-reduce(f32[]{:T(128)} %get-tuple-element.11, f32[]{:T(128)} %get-tuple-element.10), channel_id=1, replica_groups=mesh['slab'=64,'layer'=16] {'slab'}, use_global_device_ids=true, to_apply=%region_1.2 | all-reduce | flops 2 | bytes 16 | tf_op jit(solution)/shard_map/psum | solution.py:53
  178.5 54.0 %all-reduce.5 = (f32[]{:T(128)}, f32[]{:T(128)}) all-reduce(f32[]{:T(128)} %get-tuple-element.14, f32[]{:T(128)} %get-tuple-element.15), channel_id=1, replica_groups=mesh['slab'=64,'layer'=16] {'layer'}, use_global_device_ids=true, to_apply=%region_2.3 | all-reduce | flops 2 | bytes 16 | tf_op jit(solution)/shard_map/psum | solution.py:54
  235.4 111.2 %psum.88 = f32[]{:T(128)} all-reduce(f32[]{:T(128)} %get-tuple-element.22), channel_id=1, replica_groups=mesh['slab'=64,'layer'=16] {'slab'}, use_global_device_ids=true, to_apply=%region_7.8 | all-reduce | flops 1 | bytes 8 | tf_op jit(solution)/shard_map/psum | solution.py:53
  346.6 51.0 %psum.89 = f32[]{:T(128)} all-reduce(f32[]{:T(128)} %psum.88), channel_id=1, replica_groups=mesh['slab'=64,'layer'=16] {'layer'}, use_global_device_ids=true, to_apply=%region_8.9 | all-reduce | flops 1 | bytes 8 | tf_op jit(solution)/shard_map/psum | solution.py:54
  400.1 3.6 collective-permute-start.8
  409.0 4.0 collective-permute-start.10
  423.7 111.0 %psum.90 = f32[]{:T(128)} all-reduce(f32[]{:T(128)} %get-tuple-element.20), channel_id=1, replica_groups=mesh['slab'=64,'layer'=16] {'slab'}, use_global_device_ids=true, to_apply=%region_10.11 | all-reduce | flops 1 | bytes 8 | tf_op jit(solution)/shard_map/psum | solution.py:53
  534.8 51.4 %psum.91 = f32[]{:T(128)} all-reduce(f32[]{:T(128)} %psum.90), channel_id=1, replica_groups=mesh['slab'=64,'layer'=16] {'layer'}, use_global_device_ids=true, to_apply=%region_11.12 | all-reduce | flops 1 | bytes 8 | tf_op jit(solution)/shard_map/psum | solution.py:54
  589.2 113.1 %psum.92 = f32[]{:T(128)} all-reduce(f32[]{:T(128)} %multiply_reduce_fusion), channel_id=1, replica_groups=mesh['slab'=64,'layer'=16] {'slab'}, use_global_device_ids=true, to_apply=%region_13.14 | all-reduce | flops 1 | bytes 8 | tf_op jit(solution)/shard_map/psum | solution.py:53
  702.4 51.1 %psum.93 = f32[]{:T(128)} all-reduce(f32[]{:T(128)} %psum.92), channel_id=1, replica_groups=mesh['slab'=64,'layer'=16] {'layer'}, use_global_device_ids=true, to_apply=%region_14.15 | all-reduce | flops 1 | bytes 8 | tf_op jit(solution)/shard_map/psum | solution.py:54
  762.2 4.0 collective-permute-start.14
  766.2 3.8 collective-permute-start.15
  776.3 111.4 %psum.94 = f32[]{:T(128)} all-reduce(f32[]{:T(128)} %fusion.4), channel_id=1, replica_groups=mesh['slab'=64,'layer'=16] {'slab'}, use_global_device_ids=true, to_apply=%region_16.17 | all-reduce | flops 1 | bytes 8 | tf_op jit(solution)/shard_map/psum | solution.py:53
  887.7 53.1 %psum.95 = f32[]{:T(128)} all-reduce(f32[]{:T(128)} %psum.94), channel_id=1, replica_groups=mesh['slab'=64,'layer'=16] {'layer'}, use_global_device_ids=true, to_apply=%region_17.18 | all-reduce | flops 1 | bytes 8 | tf_op jit(solution)/shard_map/psum | solution.py:54
  944.9 81.0 %reduce-scatter.2.cloned.1.call-done = f32[16,32,8]{1,0,2:T(8,128)} async-done(((f32[16,32,128]{1,0,2:T(8,128)}), f32[16,32,8]{1,0,2:T(8,128)}) %reduce-scatter.2.cloned.1.call-update) | async-done | bytes 16400 | tf_op jit(solution)/shard_map/reduce_scatter | solution.py:107
  1027.7 11.4 %all-to-all-start = ((f32[64,1,128]{2,1,0:T(1,128)}), f32[64,1,128]{2,1,0:T(1,128)S(1)}, u32[]{:S(2)}, u32[]{:S(2)}) async-start(f32[64,1,128]{2,1,0:T(1,128)} %copy.14), calls=%async_computation.1 | async-start | bytes 65536 | tf_op jit(solution)/shard_map/all_to_all | solution.py:111
  1039.1 10.8 %all-to-all-done = f32[64,1,128]{2,1,0:T(1,128)S(1)} async-done(((f32[64,1,128]{2,1,0:T(1,128)}), f32[64,1,128]{2,1,0:T(1,128)S(1)}, u32[]{:S(2)}, u32[]{:S(2)}) %all-to-all-start) | async-done | bytes 32800 | tf_op jit(solution)/shard_map/all_to_all | solution.py:111
  (82 shorter events, 54.1 us)
Async XLA Ops:
  7.2 1018.7 %reduce-scatter.2.cloned.1.call-start = ((), (), s32[]{:S(2)}) async-start(), calls=%async_computation.2 | async-start | bytes 1114112 | tf_op jit(solution)/shard_map/reduce_scatter | solution.py:107
  8.2 7.0 collective-permute-start
  13.9 6.0 collective-permute-start.1
  21.0 19.4 %copy-start = (f32[1,16,4096]{2,1,0:T(8,128)S(1)}, f32[1,16,4096]{2,1,0:T(8,128)}, u32[]{:S(2)}) copy-start(f32[1,16,4096]{2,1,0:T(8,128)} %param.4) | copy-start | bytes 786436
  21.0 19.4 %copy-start.2 = (f32[1,16,4096]{2,1,0:T(8,128)S(1)}, f32[1,16,4096]{2,1,0:T(8,128)}, u32[]{:S(2)}) copy-start(f32[1,16,4096]{2,1,0:T(8,128)} %param.3) | copy-start | bytes 786436
  21.0 13.3 %collective-permute-start.2 = (f32[1,18,4096]{2,1,0:T(8,128)S(1)}, f32[1,18,4096]{2,1,0:T(8,128)S(1)}, u32[]{:S(2)}, u32[]{:S(2)}) collective-permute-start(f32[1,18,4096]{2,1,0:T(8,128)S(1)} %pad_maximum_fusion), channel_id=1, source_target_pairs={{1,0},{2,1},{3,2},{4,3},{5,4},{6,5},{7,6},{8,7},{9,8},{10,9},{11,1... | collective-permute-start | bytes 884744 | tf_op jit(solution)/shard_map/ppermute | solution.py:18
  32.4 6.6 collective-permute-start.3
  40.8 2.7 collective-permute-start.4
  42.1 4.6 collective-permute-start.5
  46.8 11.1 %collective-permute-start.6 = (f32[1,18,4096]{2,1,0:T(8,128)S(1)}, f32[1,18,4096]{2,1,0:T(8,128)S(1)}, u32[]{:S(2)}, u32[]{:S(2)}) collective-permute-start(f32[1,18,4096]{2,1,0:T(8,128)S(1)} %pad_maximum_fusion.1), channel_id=1, source_target_pairs={{1,0},{2,1},{3,2},{4,3},{5,4},{6,5},{7,6},{8,7},{9,8},{10,9},{11,1... | collective-permute-start | bytes 884744 | tf_op jit(solution)/shard_map/ppermute | solution.py:18
  48.7 10.4 collective-permute-start.7
  234.0 180.9 %copy-start.5 = (s32[8,32]{1,0:T(8,128)S(1)}, s32[8,32]{1,0:T(8,128)}, u32[]{:S(2)}) copy-start(s32[8,32]{1,0:T(8,128)} %param.5) | copy-start | bytes 3076
  400.1 4.9 collective-permute-start.8
  403.7 4.5 collective-permute-start.9
  409.0 9.3 collective-permute-start.10
  413.0 6.9 collective-permute-start.11
  418.3 1.6 copy-start.3
  423.7 329.8 %copy-start.1 = (f32[1,16,4096]{2,1,0:T(8,128)}, f32[1,16,4096]{2,1,0:T(8,128)S(1)}, u32[]{:S(2)}) copy-start(f32[1,16,4096]{2,1,0:T(8,128)S(1)} %get-tuple-element.21) | copy-start | bytes 786436
  756.1 3.1 collective-permute-start.12
  757.7 4.5 collective-permute-start.13
  762.2 11.3 %collective-permute-start.14 = (f32[1,18,4096]{2,1,0:T(8,128)S(1)}, f32[1,18,4096]{2,1,0:T(8,128)S(1)}, u32[]{:S(2)}, u32[]{:S(2)}) collective-permute-start(f32[1,18,4096]{2,1,0:T(8,128)S(1)} %pad_maximum_fusion.3), channel_id=1, source_target_pairs={{1,0},{2,1},{3,2},{4,3},{5,4},{6,5},{7,6},{8,7},{9,8},{10,9},{11,1... | collective-permute-start | bytes 884744 | tf_op jit(solution)/shard_map/ppermute | solution.py:18
  766.2 8.5 collective-permute-start.15
  943.3 1.5 copy-start.4
  1027.7 22.2 %all-to-all-start = ((f32[64,1,128]{2,1,0:T(1,128)}), f32[64,1,128]{2,1,0:T(1,128)S(1)}, u32[]{:S(2)}, u32[]{:S(2)}) async-start(f32[64,1,128]{2,1,0:T(1,128)} %copy.14), calls=%async_computation.1 | async-start | bytes 65536 | tf_op jit(solution)/shard_map/all_to_all | solution.py:111
Sparse Core Ops, SparseCore 0:
  944.9 80.9 reduce-scatter.1
where the time goes:
time: 1060 us
  blocking collectives  825 us (78%)
  waiting for transfers between devices  124 us (12%)
  starting transfers between devices  63.4 us (6%)
  between operations  21.2 us (2%)
  other arithmetic  18.1 us (2%)
    psum x5, blocking collectives, combined(): slab_total = lax.psum(value, 'slab')  564 us
    psum x5, blocking collectives, combined(): return lax.psum(slab_total, 'layer')  261 us
    reduce_scatter x1, waiting for transfers between devices, per_device(): strips = lax.psum_scatter(blocks, 'layer', scatter_dimension=2, tiled=True)  81 us
    ppermute x8, starting transfers between devices, padded_2(): lax.ppermute(lax.slice_in_dim(block, 0, width, axis=dim), axis, backward)  26.4 us
    ppermute x8, starting transfers between devices, padded_2(): lax.ppermute(lax.slice_in_dim(block, block.shape[dim] - width, None, axis...  25.6 us
    ppermute x8, waiting for transfers between devices, padded_2(): lax.ppermute(lax.slice_in_dim(block, 0, width, axis=dim), axis, backward)  23.7 us
  transfers between devices with their start and end apart: 18, of which 13 were waited for; matrix products, arithmetic and copies ran while one was open for 0% of the time, Pallas kernels for 0%

commit v1 on v0

v1 whole, which is shorter than its diff:
```python
import jax
import jax.numpy as jnp
from jax import lax
from jax.experimental import pallas as pl
from jax.experimental.pallas import tpu as pltpu
from jax.sharding import PartitionSpec as P

F32 = jnp.float32
LAYERS = 16
ROWS = 16
COLS = 4096
WIDTH = COLS // LAYERS
SLABS = 64
TILE_COLS = 32
PER_TILE = 8
OWNED = 4
EXT_ROWS = 24
EXT_COLS = 384
VMEM_LIMIT = 48 * 1024 * 1024


def lanes():
    return lax.broadcasted_iota(jnp.int32, (8, 128), 1)


def sublanes():
    return lax.broadcasted_iota(jnp.int32, (8, 128), 0)


def pack_kernel(cond_ref, src_ref, out_ref):
    lane = lanes()
    zero = jnp.zeros((8, 128), F32)
    for j in range(LAYERS):
        edge = zero
        for q, ref in enumerate((cond_ref, src_ref)):
            for g in range(2):
                rows = slice(8 * g, 8 * g + 8)
                base = WIDTH * j
                for t in range(2):
                    out_ref[j, 4 * q + 2 * g + t] = ref[0, rows, base + 128 * t : base + 128 * t + 128]
                before = ref[0, rows, base - 128 : base] if j > 0 else zero
                after = ref[0, rows, base + 256 : base + 384] if j < LAYERS - 1 else zero
                both = jnp.where(lane < 4, after, jnp.where(lane >= 124, before, 0.0))
                edge = edge + pltpu.roll(both, 4 + 8 * (2 * q + g), axis=1)
        out_ref[j, 8] = edge


def halo_kernel(recv_ref, up_ref, down_ref):
    sub = sublanes()
    for l in range(LAYERS):
        for t in range(2):
            up_ref[l, t] = jnp.where(sub >= 4, recv_ref[l, 2 + t], pltpu.roll(recv_ref[l, 6 + t], 4, axis=0))
            down_ref[l, t] = jnp.where(sub < 4, recv_ref[l, t], pltpu.roll(recv_ref[l, 4 + t], 4, axis=0))
        edge = recv_ref[l, 8]
        up_ref[l, 2] = edge
        down_ref[l, 2] = edge


def own(value):
    return value[:ROWS, :WIDTH]


def folded(value):
    return (value[:8, :128] + value[8:, :128]) + (value[:8, 128:] + value[8:, 128:])


def krylov_kernel(
    recv_ref, low_ref, high_ref, msg_ref, ret_ref, k_ref, v0_ref, v1_ref, v2_ref, inv_ref, cc_ref, cr_ref, cz_ref, square_ref
):
    lane = lanes()
    sub = sublanes()
    rim = (lane < 4) | (lane >= 124)
    blank = jnp.zeros((EXT_ROWS, EXT_COLS), F32)
    for ref in (k_ref, v0_ref, v1_ref, v2_ref):
        ref[LAYERS] = blank

    def spread(tile, index):
        return jnp.where(rim, pltpu.roll(tile, 128 - (4 + 8 * index), axis=1), 0.0)

    def unpack(l, _):
        edge = recv_ref[l, 8]
        high_edge = high_ref[l, 2]
        low_edge = pltpu.roll(low_ref[l, 2], 120, axis=1)
        halo_edge = jnp.where(sub < 4, high_edge, low_edge)
        for q, ref in enumerate((k_ref, v0_ref)):
            for g in range(2):
                for t in range(2):
                    ref[l, 8 * g : 8 * g + 8, 128 * t : 128 * t + 128] = recv_ref[l, 4 * q + 2 * g + t]
                ref[l, 8 * g : 8 * g + 8, 256:384] = spread(edge, 2 * q + g)
            ref[l, 16:24, 256:384] = spread(halo_edge, 2 * q)
        for t in range(2):
            cols = slice(128 * t, 128 * t + 128)
            high = high_ref[l, t]
            low = low_ref[l, t]
            k_ref[l, 16:24, cols] = jnp.where(sub < 4, high, low)
            v0_ref[l, 16:24, cols] = pltpu.roll(jnp.where(sub < 4, low, high), 4, axis=0)
        return 0

    lax.fori_loop(0, LAYERS, unpack, 0)

    def setup(l, carry):
        cz_before, s0, m0 = carry
        k = k_ref[l]
        cc = k + pltpu.roll(k, EXT_COLS - 1, axis=1)
        cr = k + pltpu.roll(k, EXT_ROWS - 1, axis=0)
        cz = k + k_ref[l + 1]
        diag = (cc + pltpu.roll(cc, 1, axis=1)) + (cr + pltpu.roll(cr, 1, axis=0)) + (cz + cz_before)
        inv = jnp.where(k > 0.0, 1.0 / diag, 0.0)
        twice = v0_ref[l] * 2.0
        v0 = twice * inv
        cc_ref[l] = cc
        cr_ref[l] = cr
        cz_ref[l] = cz
        inv_ref[l] = inv
        v0_ref[l] = v0
        mine = own(v0)
        for g in range(2):
            for t in range(2):
                ret_ref[l, 2 * g + t] = mine[8 * g : 8 * g + 8, 128 * t : 128 * t + 128]
        return cz, s0 + folded(mine * own(twice)), m0 + mine

    none = jnp.zeros((8, 128), F32)
    no_map = jnp.zeros((ROWS, WIDTH), F32)
    _, s0, m0 = lax.fori_loop(0, LAYERS, setup, (k_ref[0], none, no_map))

    def image(l, v_ref, fz_before):
        v = v_ref[l]
        fc = cc_ref[l] * (v - pltpu.roll(v, EXT_COLS - 1, axis=1))
        fr = cr_ref[l] * (v - pltpu.roll(v, EXT_ROWS - 1, axis=0))
        fz = cz_ref[l] * (v - v_ref[l + 1])
        result = (fc - pltpu.roll(fc, 1, axis=1)) + (fr - pltpu.roll(fr, 1, axis=0)) + (fz - fz_before)
        return v, result, fz

    def step(v_ref, out_ref, slot):
        def body(l, carry):
            fz_before, odd, even, total = carry
            v, result, fz = image(l, v_ref, fz_before)
            after = inv_ref[l] * result
            out_ref[l] = after
            mine = own(after)
            for g in range(2):
                for t in range(2):
                    ret_ref[l, 4 * slot + 2 * g + t] = mine[8 * g : 8 * g + 8, 128 * t : 128 * t + 128]
            got = own(result)
            return fz, odd + folded(own(v) * got), even + folded(mine * got), total + mine

        start = (-(k_ref[0] * v_ref[0]), none, none, no_map)
        return lax.fori_loop(0, LAYERS, body, start)[1:]

    s1, s2, m1 = step(v0_ref, v1_ref, 1)
    s3, s4, m2 = step(v1_ref, v2_ref, 2)

    def last(l, carry):
        fz_before, odd = carry
        v, result, fz = image(l, v2_ref, fz_before)
        return fz, odd + folded(own(v) * own(result))

    _, s5 = lax.fori_loop(0, LAYERS, last, (-(k_ref[0] * v2_ref[0]), none))

    sums = none
    for n, part in enumerate((s0, s1, s2, s3, s4, s5)):
        sums = jnp.where(sub == n, jnp.sum(part), sums)
    for t in range(2):
        for f, total in enumerate((m0, m1, m2)):
            square_ref[48 * t + 16 * f : 48 * t + 16 * f + 16, :] = total[:, 128 * t : 128 * t + 128]
    square_ref[96:104, :] = sums
    square_ref[104:128, :] = jnp.zeros((24, 128), F32)
    turned = square_ref[...].T
    for j in range(LAYERS):
        msg_ref[j] = turned[8 * j : 8 * j + 8, :]


def tree(values):
    while len(values) > 1:
        values = [a + b for a, b in zip(values[::2], values[1::2])]
    return values[0]


def route_kernel(owner_ref, index_ref, recv_ref, msg_ref):
    lane = lanes()
    total = tree([recv_ref[j] for j in range(LAYERS)])
    common = pltpu.roll(total, 80, axis=1)
    for o in range(SLABS):
        msg_ref[o] = common
    row = index_ref[0] // PER_TILE
    for c in range(TILE_COLS):
        strip = recv_ref[c // 2]
        if c % 2:
            strip = pltpu.roll(strip, 80, axis=1)
        msg_ref[owner_ref[row, c]] = jnp.where(lane < 48, strip, common)


def weights(s):
    s0, s1, s2, s3, s4, s5 = s
    a0 = s0 / s1
    z1 = -a0
    n1 = s0 + z1 * (2.0 * s1 + z1 * s2)
    b0 = n1 / s0
    p0, p1 = 1.0 + b0, z1
    a1 = n1 / (p0 * p0 * s1 + p1 * (2.0 * p0 * s2 + p1 * s3))
    x0, x1 = a0 + a1 * p0, a1 * p1
    z1, z2 = z1 - a1 * p0, -(a1 * p1)
    n2 = s0 + z1 * (2.0 * s1 + z1 * s2) + z2 * (2.0 * (s2 + z1 * s3) + z2 * s4)
    b1 = n2 / n1
    p0, p1, p2 = 1.0 + b1 * p0, z1 + b1 * p1, z2
    energy = p0 * p0 * s1 + p1 * (2.0 * p0 * s2 + p1 * s3) + p2 * (2.0 * (p0 * s3 + p1 * s4) + p2 * s5)
    a2 = n2 / energy
    return x0 + a2 * p0, x1 + a2 * p1, a2 * p2


def finish_kernel(rows_ref, recv_ref, ret_ref, adjoint_ref, owned_ref):
    lane = lanes()
    total = tree([recv_ref[s] for s in range(SLABS)])
    moments = [jnp.broadcast_to(total[:, 48 + n : 49 + n], (8, 128)) for n in range(6)]
    w0, w1, w2 = weights(moments)
    for j in range(LAYERS):
        for g in range(2):
            for t in range(2):
                n = 2 * g + t
                value = w0 * ret_ref[j, n] + w1 * ret_ref[j, 4 + n] + w2 * ret_ref[j, 8 + n]
                col = WIDTH * j + 128 * t
                adjoint_ref[0, 8 * g : 8 * g + 8, col : col + 128] = value
    for k in range(OWNED):
        row = rows_ref[k]
        tile = jnp.zeros((8, 128), F32)
        for i in range(PER_TILE):
            strip = recv_ref[PER_TILE * row + i]
            value = w0 * strip + w1 * pltpu.roll(strip, 112, axis=1) + w2 * pltpu.roll(strip, 96, axis=1)
            if i:
                value = pltpu.roll(value, 16 * i, axis=1)
            tile = jnp.where((lane >= 16 * i) & (lane < 16 * i + 16), value, tile)
        owned_ref[k] = tile


VMEM = pl.BlockSpec(memory_space=pltpu.VMEM)
SMEM = pl.BlockSpec(memory_space=pltpu.SMEM)


def shape(*dims):
    return jax.ShapeDtypeStruct(dims, F32)


def call(kernel, ins, outs, scratch=(), interpret=False):
    single = len(outs) == 1
    return pl.pallas_call(
        kernel,
        out_shape=outs[0] if single else tuple(outs),
        in_specs=ins,
        out_specs=VMEM if single else tuple(VMEM for _ in outs),
        scratch_shapes=list(scratch),
        compiler_params=pltpu.CompilerParams(vmem_limit_bytes=VMEM_LIMIT),
        interpret=interpret,
    )


def pack(cond, src, interpret=False):
    return call(pack_kernel, [VMEM] * 2, [shape(LAYERS, 9, 8, 128)], interpret=interpret)(cond, src)


def halo(recv, interpret=False):
    side = shape(LAYERS, 3, 8, 128)
    return call(halo_kernel, [VMEM], [side, side], interpret=interpret)(recv)


def krylov(recv, low, high, interpret=False):
    field = pltpu.VMEM((LAYERS + 1, EXT_ROWS, EXT_COLS), F32)
    face = pltpu.VMEM((LAYERS, EXT_ROWS, EXT_COLS), F32)
    return call(
        krylov_kernel,
        [VMEM] * 3,
        [shape(LAYERS, 8, 128), shape(LAYERS, 12, 8, 128)],
        [field] * 4 + [face] * 4 + [pltpu.VMEM((128, 128), F32)],
        interpret=interpret,
    )(recv, low, high)


def route(owner, index, recv, interpret=False):
    return call(route_kernel, [SMEM, SMEM, VMEM], [shape(SLABS, 8, 128)], interpret=interpret)(owner, index, recv)


def finish(rows, recv, ret, interpret=False):
    return call(
        finish_kernel, [SMEM, VMEM, VMEM], [shape(1, ROWS, COLS), shape(OWNED, 8, 128)], interpret=interpret
    )(rows, recv, ret)


def owned_rows(tile_owner, index):
    held = jnp.any(tile_owner == index, axis=1)
    rank = jnp.cumsum(held.astype(jnp.int32)) - 1
    slot = jnp.arange(OWNED, dtype=jnp.int32)[:, None]
    row = jnp.arange(tile_owner.shape[0], dtype=jnp.int32)[None, :]
    return jnp.sum(jnp.where(held[None, :] & (rank[None, :] == slot), row, 0), axis=1)


def per_device(adjoint_source, conductivity, tile_owner):
    index = lax.axis_index("slab")
    count = lax.axis_size("slab")
    recv = lax.all_to_all(pack(conductivity, adjoint_source), "layer", 0, 0, tiled=True)
    up, down = halo(recv)
    low = lax.ppermute(up, "slab", [(i, i + 1) for i in range(count - 1)])
    high = lax.ppermute(down, "slab", [(i + 1, i) for i in range(count - 1)])
    msg, ret = krylov(recv, low, high)
    strips = lax.all_to_all(msg, "layer", 0, 0, tiled=True)
    back = lax.all_to_all(ret, "layer", 0, 0, tiled=True)
    outgoing = route(tile_owner, index.reshape(1), strips)
    received = lax.all_to_all(outgoing, "slab", 0, 0, tiled=True)
    return finish(owned_rows(tile_owner, index), received, back)


def solution(mesh):
    placed = (P("layer", "slab", None), P("layer", "slab", None), P())
    return jax.shard_map(
        per_device,
        mesh=mesh,
        in_specs=placed,
        out_specs=(P("layer", "slab", None), P("slab", "layer", None)),
        check_vma=False,
    )
```

time: 1060 us -> 135 us (0.13)
  blocking collectives: 825 us -> 66 us
  waiting for transfers between devices: 124 us -> 37.2 us
  starting transfers between devices: 63.4 us -> 12.6 us
  between operations: 21.2 us -> 0.69 us
  other arithmetic: 18.1 us -> 0.43 us
  Pallas kernels: 0 us -> 15.5 us
    psum x10 -> x0, blocking collectives: 825 us -> none  [the longest x5 564 us: combined(): slab_total = lax.psum(value, 'slab')]
    reduce_scatter x1 -> x0, waiting for transfers between devices: 81 us -> none  [per_device(): strips = lax.psum_scatter(blocks, 'layer', scatter_dimension=2, tiled=True)]
    all_to_all x0 -> x2, blocking collectives: none -> 66 us  [the longest x1 35.6 us: per_device(): lax.all_to_all(pack(conductivity, adjoint_source), 'layer', 0, 0, tiled=T...]
    ppermute x16 -> x2, starting transfers between devices: 52 us -> 2.59 us  [the longest x1 1.3 us: per_device(): low = lax.ppermute(up, 'slab', [(i, i + 1) for i in range(count - 1)])]
    ppermute x16 -> x2, waiting for transfers between devices: 32.3 us -> 7.06 us  [the longest x1 3.96 us: per_device(): high = lax.ppermute(down, 'slab', [(i + 1, i) for i in range(count - 1)])]
    all_to_all x1 -> x2, waiting for transfers between devices: 10.8 us -> 30.1 us  [the longest x1 22.3 us: per_device(): back = lax.all_to_all(ret, 'layer', 0, 0, tiled=True)]
    pallas_call x0 -> x5, Pallas kernels: none -> 15.5 us  [the longest x1 13.2 us: krylov(): call(krylov_kernel, [VMEM] * 3, [shape(LAYERS, 8, 128), shape(LAYERS, 12,...]
  transfers between devices with their start and end apart: 18 -> 4, of which waited for: 13 -> 4; matrix products, arithmetic and copies ran while one was open for 0% -> 0% of each run, Pallas kernels for 0% -> 0%
where the time goes in v1:
time: 135 us; the launch traced here: 134 us
  blocking collectives  66 us (49%)
  waiting for transfers between devices  37.2 us (28%)
  Pallas kernels  15.5 us (11%)
  starting transfers between devices  12.6 us (9%)
  local copies, waits for them, and re-layouts  1.9 us (1%)
    all_to_all x1, blocking collectives, per_device(): lax.all_to_all(pack(conductivity, adjoint_source), 'layer', 0, 0, tiled=T...  35.6 us
    all_to_all x1, blocking collectives, per_device(): received = lax.all_to_all(outgoing, 'slab', 0, 0, tiled=True)  30.4 us
    all_to_all x1, waiting for transfers between devices, per_device(): back = lax.all_to_all(ret, 'layer', 0, 0, tiled=True)  22.3 us
    pallas_call x1, Pallas kernels, krylov(): call(krylov_kernel, [VMEM] * 3, [shape(LAYERS, 8, 128), shape(LAYERS, 12,...  13.2 us
    all_to_all x1, waiting for transfers between devices, per_device(): strips = lax.all_to_all(msg, 'layer', 0, 0, tiled=True)  7.83 us
    all_to_all x1, starting transfers between devices, per_device(): back = lax.all_to_all(ret, 'layer', 0, 0, tiled=True)  5.83 us
    all_to_all x1, starting transfers between devices, per_device(): strips = lax.all_to_all(msg, 'layer', 0, 0, tiled=True)  4.16 us
    ppermute x1, waiting for transfers between devices, per_device(): high = lax.ppermute(down, 'slab', [(i + 1, i) for i in range(count - 1)])  3.96 us
  transfers between devices with their start and end apart: 4, of which 4 were waited for; matrix products, arithmetic and copies ran while one was open for 0% of the time, Pallas kernels for 0%

profile of v1, /device:TPU:1, one launch (start us, length us, event | category | flops | bytes accessed | tf_op | source)
XLA Modules:
  0.0 134.3 jit_solution(17416749273344952128)
XLA Ops:
  0.6 0.0 copy-start
  0.6 0.9 copy-done
  1.6 0.0 copy-start.1
  1.6 0.9 copy-done.1
  2.5 0.1 shard_map.50
  2.7 35.6 %all_to_all.20.recv_ref = f32[16,9,8,128]{3,2,1,0:T(8,128)S(1)} all-to-all(f32[16,9,8,128]{3,2,1,0:T(8,128)S(1)} %shard_map.50), channel_id=1, replica_groups=mesh['slab'=64,'layer'=16] {'layer'}, dimensions={0} | all-to-all | bytes 1179648 | tf_op jit(solution)/shard_map/all_to_all | solution.py:298
  38.4 1.3 collective-permute-start
  39.7 1.3 collective-permute-start.1
  41.0 3.1 %collective-permute-done.low_ref = f32[16,3,8,128]{3,2,1,0:T(8,128)S(1)} collective-permute-done((f32[16,3,8,128]{3,2,1,0:T(8,128)S(1)}, f32[16,3,8,128]{3,2,1,0:T(8,128)S(1)}, u32[]{:S(2)}, u32[]{:S(2)}) %collective-permute-start) | collective-permute-done | bytes 196640 | tf_op jit(solution)/shard_map/ppermute | solution.py:300
  44.1 4.0 %collective-permute-done.1.high_ref = f32[16,3,8,128]{3,2,1,0:T(8,128)S(1)} collective-permute-done((f32[16,3,8,128]{3,2,1,0:T(8,128)S(1)}, f32[16,3,8,128]{3,2,1,0:T(8,128)S(1)}, u32[]{:S(2)}, u32[]{:S(2)}) %collective-permute-start.1) | collective-permute-done | bytes 196640 | tf_op jit(solution)/shard_map/ppermute | solution.py:301
  48.0 13.2 %shard_map.52 = (f32[16,8,128]{2,1,0:T(8,128)}, f32[16,12,8,128]{3,2,1,0:T(8,128)}) custom-call(f32[16,9,8,128]{3,2,1,0:T(8,128)S(1)} %all_to_all.20.recv_ref, f32[16,3,8,128]{3,2,1,0:T(8,128)S(1)} %collective-permute-done.low_ref, f32[16,3,8,128]{3,2,1,0:T(8,128)S(1)} %collective-permute-done.1.high_ref), custom_call_target="tpu_custom_call" | custom-call | tf_op jit(solution)/shard_map/pallas_call | solution.py:268
  61.2 4.2 %all-to-all-start.1 = ((f32[16,8,128]{2,1,0:T(8,128)}), f32[16,8,128]{2,1,0:T(8,128)S(1)}, u32[]{:S(2)}, u32[]{:S(2)}) async-start(f32[16,8,128]{2,1,0:T(8,128)} %get-tuple-element.8), calls=%async_computation.1 | async-start | bytes 131072 | tf_op jit(solution)/shard_map/all_to_all | solution.py:303
  65.4 0.0 copy-start.2
  65.4 7.8 %all-to-all-done.1.recv_ref = f32[16,8,128]{2,1,0:T(8,128)S(1)} async-done(((f32[16,8,128]{2,1,0:T(8,128)}), f32[16,8,128]{2,1,0:T(8,128)S(1)}, u32[]{:S(2)}, u32[]{:S(2)}) %all-to-all-start.1) | async-done | bytes 65568 | tf_op jit(solution)/shard_map/all_to_all | solution.py:303
  73.2 0.0 copy-done.2
  73.2 0.7 shard_map.53
  73.9 30.4 %all_to_all.21.recv_ref = f32[64,8,128]{2,1,0:T(8,128)S(1)} all-to-all(f32[64,8,128]{2,1,0:T(8,128)S(1)} %shard_map.53), channel_id=1, replica_groups=mesh['slab'=64,'layer'=16] {'slab'}, dimensions={0} | all-to-all | bytes 524288 | tf_op jit(solution)/shard_map/all_to_all | solution.py:306
  104.3 5.8 %all-to-all-start.3 = ((f32[16,12,8,128]{3,2,1,0:T(8,128)}), f32[16,12,8,128]{3,2,1,0:T(8,128)S(1)}, u32[]{:S(2)}, u32[]{:S(2)}) async-start(f32[16,12,8,128]{3,2,1,0:T(8,128)} %get-tuple-element.9), calls=%async_computation.3 | async-start | bytes 1572864 | tf_op jit(solution)/shard_map/all_to_all | solution.py:304
  110.1 0.1 compare_reduce_fusion
  110.3 0.2 reduce-window.8
  110.5 0.1 select_reduce_fusion.rows_ref
  110.6 22.3 %all-to-all-done.3.ret_ref = f32[16,12,8,128]{3,2,1,0:T(8,128)S(1)} async-done(((f32[16,12,8,128]{3,2,1,0:T(8,128)}), f32[16,12,8,128]{3,2,1,0:T(8,128)S(1)}, u32[]{:S(2)}, u32[]{:S(2)}) %all-to-all-start.3) | async-done | bytes 786464 | tf_op jit(solution)/shard_map/all_to_all | solution.py:304
  132.9 1.4 %shard_map.54 = (f32[1,16,4096]{2,1,0:T(8,128)}, f32[4,8,128]{2,1,0:T(8,128)}) custom-call(s32[4]{0:T(128)S(1)} %select_reduce_fusion.rows_ref, f32[64,8,128]{2,1,0:T(8,128)S(1)} %all_to_all.21.recv_ref, f32[16,12,8,128]{3,2,1,0:T(8,128)S(1)} %all-to-all-done.3.ret_ref), custom_call_target="tpu_custom_call" | custom-call | tf_op jit(solution)/shard_map/pallas_call | solution.py:282
  (3 shorter events, 0.0 us)
Async XLA Ops:
  0.6 1.0 copy-start
  1.6 0.9 copy-start.1
  38.4 5.7 %collective-permute-start = (f32[16,3,8,128]{3,2,1,0:T(8,128)S(1)}, f32[16,3,8,128]{3,2,1,0:T(8,128)S(1)}, u32[]{:S(2)}, u32[]{:S(2)}) collective-permute-start(f32[16,3,8,128]{3,2,1,0:T(8,128)S(1)} %get-tuple-element.6), channel_id=1, source_target_pairs={{0,16},{16,32},{32,48},{48,64},{64,80},{80,96},{96,112},{112,128},... | collective-permute-start | bytes 589832 | tf_op jit(solution)/shard_map/ppermute | solution.py:300
  39.7 8.4 %collective-permute-start.1 = (f32[16,3,8,128]{3,2,1,0:T(8,128)S(1)}, f32[16,3,8,128]{3,2,1,0:T(8,128)S(1)}, u32[]{:S(2)}, u32[]{:S(2)}) collective-permute-start(f32[16,3,8,128]{3,2,1,0:T(8,128)S(1)} %get-tuple-element.7), channel_id=1, source_target_pairs={{16,0},{32,16},{48,32},{64,48},{80,64},{96,80},{112,96},{128,112},... | collective-permute-start | bytes 589832 | tf_op jit(solution)/shard_map/ppermute | solution.py:301
  61.2 12.0 %all-to-all-start.1 = ((f32[16,8,128]{2,1,0:T(8,128)}), f32[16,8,128]{2,1,0:T(8,128)S(1)}, u32[]{:S(2)}, u32[]{:S(2)}) async-start(f32[16,8,128]{2,1,0:T(8,128)} %get-tuple-element.8), calls=%async_computation.1 | async-start | bytes 131072 | tf_op jit(solution)/shard_map/all_to_all | solution.py:303
  65.4 7.8 %copy-start.2 = (s32[8,32]{1,0:T(8,128)S(1)}, s32[8,32]{1,0:T(8,128)}, u32[]{:S(2)}) copy-start(s32[8,32]{1,0:T(8,128)} %owner_ref.1) | copy-start | bytes 3076
  104.3 28.5 %all-to-all-start.3 = ((f32[16,12,8,128]{3,2,1,0:T(8,128)}), f32[16,12,8,128]{3,2,1,0:T(8,128)S(1)}, u32[]{:S(2)}, u32[]{:S(2)}) async-start(f32[16,12,8,128]{3,2,1,0:T(8,128)} %get-tuple-element.9), calls=%async_computation.3 | async-start | bytes 1572864 | tf_op jit(solution)/shard_map/all_to_all | solution.py:304

commit v2 on v1

--- a/solution.py
+++ b/solution.py
@@ -41,19 +41,26 @@
                 before = ref[0, rows, base - 128 : base] if j > 0 else zero
                 after = ref[0, rows, base + 256 : base + 384] if j < LAYERS - 1 else zero
                 both = jnp.where(lane < 4, after, jnp.where(lane >= 124, before, 0.0))
-                edge = edge + pltpu.roll(both, 4 + 8 * (2 * q + g), axis=1)
+                edge = edge + pltpu.roll(both, 4 + 8 * (2 * g + q), axis=1)
         out_ref[j, 8] = edge
 
 
 def halo_kernel(recv_ref, up_ref, down_ref):
+    lane = lanes()
     sub = sublanes()
+    up_edges = [jnp.zeros((8, 128), F32)] * 2
+    down_edges = [jnp.zeros((8, 128), F32)] * 2
     for l in range(LAYERS):
         for t in range(2):
-            up_ref[l, t] = jnp.where(sub >= 4, recv_ref[l, 2 + t], pltpu.roll(recv_ref[l, 6 + t], 4, axis=0))
-            down_ref[l, t] = jnp.where(sub < 4, recv_ref[l, t], pltpu.roll(recv_ref[l, 4 + t], 4, axis=0))
+            up_ref[2 * l + t] = jnp.where(sub >= 4, recv_ref[l, 2 + t], pltpu.roll(recv_ref[l, 6 + t], 4, axis=0))
+            down_ref[2 * l + t] = jnp.where(sub < 4, recv_ref[l, t], pltpu.roll(recv_ref[l, 4 + t], 4, axis=0))
         edge = recv_ref[l, 8]
-        up_ref[l, 2] = edge
-        down_ref[l, 2] = edge
+        half, place = l // 8, 16 * (l % 8)
+        here = (lane >= place) & (lane < place + 16)
+        up_edges[half] = jnp.where(here, pltpu.roll(edge, (place + 112) % 128, axis=1), up_edges[half])
+        down_edges[half] = jnp.where(here, pltpu.roll(edge, place, axis=1), down_edges[half])
+    up_ref[32] = jnp.where(sub >= 4, up_edges[0], pltpu.roll(up_edges[1], 4, axis=0))
+    down_ref[32] = jnp.where(sub < 4, down_edges[0], pltpu.roll(down_edges[1], 4, axis=0))
 
 
 def own(value):
@@ -65,7 +72,7 @@
 
 
 def krylov_kernel(
-    recv_ref, low_ref, high_ref, msg_ref, ret_ref, k_ref, v0_ref, v1_ref, v2_ref, inv_ref, cc_ref, cr_ref, cz_ref, square_ref
+    recv_ref, low_ref, high_ref, ret_ref, k_ref, v0_ref, v1_ref, v2_ref, inv_ref, cc_ref, cr_ref, cz_ref, square_ref
 ):
     lane = lanes()
     sub = sublanes()
@@ -74,29 +81,29 @@
     for ref in (k_ref, v0_ref, v1_ref, v2_ref):
         ref[LAYERS] = blank
 
-    def spread(tile, index):
-        return jnp.where(rim, pltpu.roll(tile, 128 - (4 + 8 * index), axis=1), 0.0)
-
-    def unpack(l, _):
+    def spread(tile, place):
+        return jnp.where(rim, pltpu.roll(tile, (252 - place) % 128, axis=1), 0.0)
+
+    low_edges = low_ref[32]
+    high_edges = high_ref[32]
+    halo_edges = (
+        jnp.where(sub < 4, high_edges, low_edges),
+        pltpu.roll(jnp.where(sub < 4, low_edges, high_edges), 4, axis=0),
+    )
+    for l in range(LAYERS):
         edge = recv_ref[l, 8]
-        high_edge = high_ref[l, 2]
-        low_edge = pltpu.roll(low_ref[l, 2], 120, axis=1)
-        halo_edge = jnp.where(sub < 4, high_edge, low_edge)
         for q, ref in enumerate((k_ref, v0_ref)):
             for g in range(2):
                 for t in range(2):
                     ref[l, 8 * g : 8 * g + 8, 128 * t : 128 * t + 128] = recv_ref[l, 4 * q + 2 * g + t]
-                ref[l, 8 * g : 8 * g + 8, 256:384] = spread(edge, 2 * q + g)
-            ref[l, 16:24, 256:384] = spread(halo_edge, 2 * q)
+                ref[l, 8 * g : 8 * g + 8, 256:384] = spread(edge, 8 * (2 * g + q))
+            ref[l, 16:24, 256:384] = spread(halo_edges[l // 8], 16 * (l % 8) + 8 * q)
         for t in range(2):
             cols = slice(128 * t, 128 * t + 128)
-            high = high_ref[l, t]
-            low = low_ref[l, t]
+            high = high_ref[2 * l + t]
+            low = low_ref[2 * l + t]
             k_ref[l, 16:24, cols] = jnp.where(sub < 4, high, low)
             v0_ref[l, 16:24, cols] = pltpu.roll(jnp.where(sub < 4, low, high), 4, axis=0)
-        return 0
-
-    lax.fori_loop(0, LAYERS, unpack, 0)
 
     def setup(l, carry):
         cz_before, s0, m0 = carry
@@ -121,7 +128,7 @@
 
     none = jnp.zeros((8, 128), F32)
     no_map = jnp.zeros((ROWS, WIDTH), F32)
-    _, s0, m0 = lax.fori_loop(0, LAYERS, setup, (k_ref[0], none, no_map))
+    _, s0, m0 = lax.fori_loop(0, LAYERS, setup, (k_ref[0], none, no_map), unroll=4)
 
     def image(l, v_ref, fz_before):
         v = v_ref[l]
@@ -145,7 +152,7 @@
             return fz, odd + folded(own(v) * got), even + folded(mine * got), total + mine
 
         start = (-(k_ref[0] * v_ref[0]), none, none, no_map)
-        return lax.fori_loop(0, LAYERS, body, start)[1:]
+        return lax.fori_loop(0, LAYERS, body, start, unroll=4)[1:]
 
     s1, s2, m1 = step(v0_ref, v1_ref, 1)
     s3, s4, m2 = step(v1_ref, v2_ref, 2)
@@ -155,7 +162,7 @@
         v, result, fz = image(l, v2_ref, fz_before)
         return fz, odd + folded(own(v) * own(result))
 
-    _, s5 = lax.fori_loop(0, LAYERS, last, (-(k_ref[0] * v2_ref[0]), none))
+    _, s5 = lax.fori_loop(0, LAYERS, last, (-(k_ref[0] * v2_ref[0]), none), unroll=4)
 
     sums = none
     for n, part in enumerate((s0, s1, s2, s3, s4, s5)):
@@ -167,7 +174,7 @@
     square_ref[104:128, :] = jnp.zeros((24, 128), F32)
     turned = square_ref[...].T
     for j in range(LAYERS):
-        msg_ref[j] = turned[8 * j : 8 * j + 8, :]
+        ret_ref[j, 12] = turned[8 * j : 8 * j + 8, :]
 
 
 def tree(values):
@@ -178,16 +185,17 @@
 
 def route_kernel(owner_ref, index_ref, recv_ref, msg_ref):
     lane = lanes()
-    total = tree([recv_ref[j] for j in range(LAYERS)])
+    total = tree([recv_ref[j, 12] for j in range(LAYERS)])
     common = pltpu.roll(total, 80, axis=1)
     for o in range(SLABS):
-        msg_ref[o] = common
+        msg_ref[o] = common[:4]
     row = index_ref[0] // PER_TILE
     for c in range(TILE_COLS):
-        strip = recv_ref[c // 2]
-        if c % 2:
-            strip = pltpu.roll(strip, 80, axis=1)
-        msg_ref[owner_ref[row, c]] = jnp.where(lane < 48, strip, common)
+        strip = recv_ref[c // 2, 12]
+        first = pltpu.roll(strip, 80, axis=1) if c % 2 else strip
+        second = pltpu.roll(pltpu.roll(strip, 16 if c % 2 else 64, axis=1), 4, axis=0)
+        both = jnp.where(lane < 48, first, jnp.where(lane < 64, common, second))
+        msg_ref[owner_ref[row, c]] = both[:4]
 
 
 def weights(s):
@@ -210,8 +218,9 @@
 
 def finish_kernel(rows_ref, recv_ref, ret_ref, adjoint_ref, owned_ref):
     lane = lanes()
+    sub = sublanes()
     total = tree([recv_ref[s] for s in range(SLABS)])
-    moments = [jnp.broadcast_to(total[:, 48 + n : 49 + n], (8, 128)) for n in range(6)]
+    moments = [jnp.broadcast_to(total[:1, 48 + n : 49 + n], (8, 128)) for n in range(6)]
     w0, w1, w2 = weights(moments)
     for j in range(LAYERS):
         for g in range(2):
@@ -224,7 +233,9 @@
         row = rows_ref[k]
         tile = jnp.zeros((8, 128), F32)
         for i in range(PER_TILE):
-            strip = recv_ref[PER_TILE * row + i]
+            half = recv_ref[PER_TILE * row + i]
+            whole = jnp.concatenate([half, half], axis=0)
+            strip = jnp.where(sub < 4, whole, pltpu.roll(whole, 64, axis=1))
             value = w0 * strip + w1 * pltpu.roll(strip, 112, axis=1) + w2 * pltpu.roll(strip, 96, axis=1)
             if i:
                 value = pltpu.roll(value, 16 * i, axis=1)
@@ -258,7 +269,7 @@
 
 
 def halo(recv, interpret=False):
-    side = shape(LAYERS, 3, 8, 128)
+    side = shape(2 * LAYERS + 1, 8, 128)
     return call(halo_kernel, [VMEM], [side, side], interpret=interpret)(recv)
 
 
@@ -268,14 +279,14 @@
     return call(
         krylov_kernel,
         [VMEM] * 3,
-        [shape(LAYERS, 8, 128), shape(LAYERS, 12, 8, 128)],
+        [shape(LAYERS, 13, 8, 128)],
         [field] * 4 + [face] * 4 + [pltpu.VMEM((128, 128), F32)],
         interpret=interpret,
     )(recv, low, high)
 
 
 def route(owner, index, recv, interpret=False):
-    return call(route_kernel, [SMEM, SMEM, VMEM], [shape(SLABS, 8, 128)], interpret=interpret)(owner, index, recv)
+    return call(route_kernel, [SMEM, SMEM, VMEM], [shape(SLABS, 4, 128)], interpret=interpret)(owner, index, recv)
 
 
 def finish(rows, recv, ret, interpret=False):
@@ -299,10 +310,8 @@
     up, down = halo(recv)
     low = lax.ppermute(up, "slab", [(i, i + 1) for i in range(count - 1)])
     high = lax.ppermute(down, "slab", [(i + 1, i) for i in range(count - 1)])
-    msg, ret = krylov(recv, low, high)
-    strips = lax.all_to_all(msg, "layer", 0, 0, tiled=True)
-    back = lax.all_to_all(ret, "layer", 0, 0, tiled=True)
-    outgoing = route(tile_owner, index.reshape(1), strips)
+    back = lax.all_to_all(krylov(recv, low, high), "layer", 0, 0, tiled=True)
+    outgoing = route(tile_owner, index.reshape(1), back)
     received = lax.all_to_all(outgoing, "slab", 0, 0, tiled=True)
     return finish(owned_rows(tile_owner, index), received, back)
 

time: 135 us -> 112 us (0.83)
  blocking collectives: 66 us -> 35.6 us
  starting transfers between devices: 12.6 us -> 24.1 us
  Pallas kernels: 15.5 us -> 7.52 us
  waiting for transfers between devices: 37.2 us -> 40.3 us
    all_to_all x1 -> x0, blocking collectives: 30.4 us -> none  [per_device(): received = lax.all_to_all(outgoing, 'slab', 0, 0, tiled=True)]
    all_to_all x2, starting transfers between devices: 10 us -> 21.5 us  [the longest x1 17.2 us: per_device(): received = lax.all_to_all(outgoing, 'slab', 0, 0, tiled=True)]
    pallas_call x2, Pallas kernels: 13.9 us -> 5.8 us  [the longest x1 4.42 us: krylov(): call(krylov_kernel, [VMEM] * 3, [shape(LAYERS, 13, 8, 128)], [field] * 4...]
    all_to_all x2, waiting for transfers between devices: 30.1 us -> 34.5 us  [the longest x1 23 us: per_device(): back = lax.all_to_all(krylov(recv, low, high), 'layer', 0, 0, tiled=True)]
where the time goes in v2:
time: 112 us; the launch traced here: 111 us
  waiting for transfers between devices  40.3 us (36%)
  blocking collectives  35.6 us (32%)
  starting transfers between devices  24.1 us (22%)
  Pallas kernels  7.52 us (7%)
  local copies, waits for them, and re-layouts  2.57 us (2%)
    all_to_all x1, blocking collectives, per_device(): lax.all_to_all(pack(conductivity, adjoint_source), 'layer', 0, 0, tiled=T...  35.6 us
    all_to_all x1, waiting for transfers between devices, per_device(): back = lax.all_to_all(krylov(recv, low, high), 'layer', 0, 0, tiled=True)  23 us
    all_to_all x1, starting transfers between devices, per_device(): received = lax.all_to_all(outgoing, 'slab', 0, 0, tiled=True)  17.2 us
    all_to_all x1, waiting for transfers between devices, per_device(): received = lax.all_to_all(outgoing, 'slab', 0, 0, tiled=True)  11.5 us
    pallas_call x1, Pallas kernels, krylov(): call(krylov_kernel, [VMEM] * 3, [shape(LAYERS, 13, 8, 128)], [field] * 4...  4.42 us
    all_to_all x1, starting transfers between devices, per_device(): back = lax.all_to_all(krylov(recv, low, high), 'layer', 0, 0, tiled=True)  4.28 us
    ppermute x1, waiting for transfers between devices, per_device(): high = lax.ppermute(down, 'slab', [(i + 1, i) for i in range(count - 1)])  3.96 us
    unnamed x6, local copies, waits for them, and re-layouts  2.57 us
  transfers between devices with their start and end apart: 4, of which 4 were waited for; matrix products, arithmetic and copies ran while one was open for 0% of the time, Pallas kernels for 0%

profile of v2, /device:TPU:1, one launch (start us, length us, event | category | flops | bytes accessed | tf_op | source)
XLA Modules:
  0.0 111.3 jit_solution(9545598390709414354)
XLA Ops:
  0.6 0.0 copy-start
  0.6 0.9 copy-done
  1.6 0.0 copy-start.1
  1.6 0.9 copy-done.1
  2.5 0.1 shard_map.50
  2.7 35.6 %all_to_all.15.recv_ref = f32[16,9,8,128]{3,2,1,0:T(8,128)S(1)} all-to-all(f32[16,9,8,128]{3,2,1,0:T(8,128)S(1)} %shard_map.50), channel_id=1, replica_groups=mesh['slab'=64,'layer'=16] {'layer'}, dimensions={0} | all-to-all | bytes 1179648 | tf_op jit(solution)/shard_map/all_to_all | solution.py:309
  38.3 0.1 shard_map.51
  38.4 1.3 %collective-permute-start = (f32[33,8,128]{2,1,0:T(8,128)S(1)}, f32[33,8,128]{2,1,0:T(8,128)S(1)}, u32[]{:S(2)}, u32[]{:S(2)}) collective-permute-start(f32[33,8,128]{2,1,0:T(8,128)S(1)} %get-tuple-element.4), channel_id=1, source_target_pairs={{0,16},{16,32},{32,48},{48,64},{64,80},{80,96},{96,112},{112,128},... | collective-permute-start | bytes 405512 | tf_op jit(solution)/shard_map/ppermute | solution.py:311
  39.7 1.3 %collective-permute-start.1 = (f32[33,8,128]{2,1,0:T(8,128)S(1)}, f32[33,8,128]{2,1,0:T(8,128)S(1)}, u32[]{:S(2)}, u32[]{:S(2)}) collective-permute-start(f32[33,8,128]{2,1,0:T(8,128)S(1)} %get-tuple-element.5), channel_id=1, source_target_pairs={{16,0},{32,16},{48,32},{64,48},{80,64},{96,80},{112,96},{128,112},... | collective-permute-start | bytes 405512 | tf_op jit(solution)/shard_map/ppermute | solution.py:312
  41.0 1.8 %collective-permute-done.low_ref = f32[33,8,128]{2,1,0:T(8,128)S(1)} collective-permute-done((f32[33,8,128]{2,1,0:T(8,128)S(1)}, f32[33,8,128]{2,1,0:T(8,128)S(1)}, u32[]{:S(2)}, u32[]{:S(2)}) %collective-permute-start) | collective-permute-done | bytes 135200 | tf_op jit(solution)/shard_map/ppermute | solution.py:311
  42.8 4.0 %collective-permute-done.1.high_ref = f32[33,8,128]{2,1,0:T(8,128)S(1)} collective-permute-done((f32[33,8,128]{2,1,0:T(8,128)S(1)}, f32[33,8,128]{2,1,0:T(8,128)S(1)}, u32[]{:S(2)}, u32[]{:S(2)}) %collective-permute-start.1) | collective-permute-done | bytes 135200 | tf_op jit(solution)/shard_map/ppermute | solution.py:312
  46.8 4.4 %shard_map.52 = f32[16,13,8,128]{3,2,1,0:T(8,128)} custom-call(f32[16,9,8,128]{3,2,1,0:T(8,128)S(1)} %all_to_all.15.recv_ref, f32[33,8,128]{2,1,0:T(8,128)S(1)} %collective-permute-done.low_ref, f32[33,8,128]{2,1,0:T(8,128)S(1)} %collective-permute-done.1.high_ref), custom_call_target="tpu_custom_call" | custom-call | tf_op jit(solution)/shard_map/pallas_call | solution.py:279
  51.2 4.3 %all-to-all-start.1 = ((f32[16,13,8,128]{3,2,1,0:T(8,128)}), f32[16,13,8,128]{3,2,1,0:T(8,128)S(1)}, u32[]{:S(2)}, u32[]{:S(2)}) async-start(f32[16,13,8,128]{3,2,1,0:T(8,128)} %shard_map.52), calls=%async_computation.1 | async-start | bytes 1703936 | tf_op jit(solution)/shard_map/all_to_all | solution.py:313
  55.5 0.0 copy-start.2
  55.5 0.7 copy-done.2
  56.2 0.1 compare_reduce_fusion
  56.3 0.2 reduce-window.8
  56.5 23.0 %all-to-all-done.1.recv_ref.ret_ref = f32[16,13,8,128]{3,2,1,0:T(8,128)S(1)} async-done(((f32[16,13,8,128]{3,2,1,0:T(8,128)}), f32[16,13,8,128]{3,2,1,0:T(8,128)S(1)}, u32[]{:S(2)}, u32[]{:S(2)}) %all-to-all-start.1) | async-done | bytes 852000 | tf_op jit(solution)/shard_map/all_to_all | solution.py:313
  79.5 1.4 %shard_map.53 = f32[64,4,128]{2,1,0:T(4,128)} custom-call(s32[8,32]{1,0:T(8,128)S(1)} %copy-done.2, s32[1]{0:T(128)} %bitcast.2.index_ref, f32[16,13,8,128]{3,2,1,0:T(8,128)S(1)} %all-to-all-done.1.recv_ref.ret_ref), custom_call_target="tpu_custom_call" | custom-call | tf_op jit(solution)/shard_map/pallas_call | solution.py:289
  80.9 17.2 %all-to-all-start.2 = ((f32[64,4,128]{2,1,0:T(4,128)}), f32[64,4,128]{2,1,0:T(4,128)S(1)}, u32[]{:S(2)}, u32[]{:S(2)}) async-start(f32[64,4,128]{2,1,0:T(4,128)} %shard_map.53), calls=%async_computation.2 | async-start | bytes 262144 | tf_op jit(solution)/shard_map/all_to_all | solution.py:315
  98.1 0.1 select_reduce_fusion.rows_ref
  98.3 11.5 %all-to-all-done.2.recv_ref = f32[64,4,128]{2,1,0:T(4,128)S(1)} async-done(((f32[64,4,128]{2,1,0:T(4,128)}), f32[64,4,128]{2,1,0:T(4,128)S(1)}, u32[]{:S(2)}, u32[]{:S(2)}) %all-to-all-start.2) | async-done | bytes 131104 | tf_op jit(solution)/shard_map/all_to_all | solution.py:315
  109.8 1.5 %shard_map.54 = (f32[1,16,4096]{2,1,0:T(8,128)}, f32[4,8,128]{2,1,0:T(8,128)}) custom-call(s32[4]{0:T(128)S(1)} %select_reduce_fusion.rows_ref, f32[64,4,128]{2,1,0:T(4,128)S(1)} %all-to-all-done.2.recv_ref, f32[16,13,8,128]{3,2,1,0:T(8,128)S(1)} %all-to-all-done.1.recv_ref.ret_ref), custom_call_target="tpu_custom_call" | custom-call | tf_op jit(solution)/shard_map/pallas_call | solution.py:293
  (2 shorter events, 0.0 us)
Async XLA Ops:
  0.6 1.0 copy-start
  1.6 0.9 copy-start.1
  38.4 4.4 %collective-permute-start = (f32[33,8,128]{2,1,0:T(8,128)S(1)}, f32[33,8,128]{2,1,0:T(8,128)S(1)}, u32[]{:S(2)}, u32[]{:S(2)}) collective-permute-start(f32[33,8,128]{2,1,0:T(8,128)S(1)} %get-tuple-element.4), channel_id=1, source_target_pairs={{0,16},{16,32},{32,48},{48,64},{64,80},{80,96},{96,112},{112,128},... | collective-permute-start | bytes 405512 | tf_op jit(solution)/shard_map/ppermute | solution.py:311
  39.7 7.0 %collective-permute-start.1 = (f32[33,8,128]{2,1,0:T(8,128)S(1)}, f32[33,8,128]{2,1,0:T(8,128)S(1)}, u32[]{:S(2)}, u32[]{:S(2)}) collective-permute-start(f32[33,8,128]{2,1,0:T(8,128)S(1)} %get-tuple-element.5), channel_id=1, source_target_pairs={{16,0},{32,16},{48,32},{64,48},{80,64},{96,80},{112,96},{128,112},... | collective-permute-start | bytes 405512 | tf_op jit(solution)/shard_map/ppermute | solution.py:312
  51.2 28.3 %all-to-all-start.1 = ((f32[16,13,8,128]{3,2,1,0:T(8,128)}), f32[16,13,8,128]{3,2,1,0:T(8,128)S(1)}, u32[]{:S(2)}, u32[]{:S(2)}) async-start(f32[16,13,8,128]{3,2,1,0:T(8,128)} %shard_map.52), calls=%async_computation.1 | async-start | bytes 1703936 | tf_op jit(solution)/shard_map/all_to_all | solution.py:313
  55.5 0.7 copy-start.2
  80.9 28.9 %all-to-all-start.2 = ((f32[64,4,128]{2,1,0:T(4,128)}), f32[64,4,128]{2,1,0:T(4,128)S(1)}, u32[]{:S(2)}, u32[]{:S(2)}) async-start(f32[64,4,128]{2,1,0:T(4,128)} %shard_map.53), calls=%async_computation.2 | async-start | bytes 262144 | tf_op jit(solution)/shard_map/all_to_all | solution.py:315

commit v3 on v2

--- a/solution.py
+++ b/solution.py
@@ -72,7 +72,7 @@
 
 
 def krylov_kernel(
-    recv_ref, low_ref, high_ref, ret_ref, k_ref, v0_ref, v1_ref, v2_ref, inv_ref, cc_ref, cr_ref, cz_ref, square_ref
+    index_ref, recv_ref, low_ref, high_ref, ret_ref, k_ref, v0_ref, v1_ref, v2_ref, inv_ref, cc_ref, cr_ref, cz_ref, square_ref
 ):
     lane = lanes()
     sub = sublanes()
@@ -84,6 +84,7 @@
     def spread(tile, place):
         return jnp.where(rim, pltpu.roll(tile, (252 - place) % 128, axis=1), 0.0)
 
+    inside = ((sub < 4) & (index_ref[0] < SLABS - 1)) | ((sub >= 4) & (index_ref[0] > 0))
     low_edges = low_ref[32]
     high_edges = high_ref[32]
     halo_edges = (
@@ -97,13 +98,13 @@
                 for t in range(2):
                     ref[l, 8 * g : 8 * g + 8, 128 * t : 128 * t + 128] = recv_ref[l, 4 * q + 2 * g + t]
                 ref[l, 8 * g : 8 * g + 8, 256:384] = spread(edge, 8 * (2 * g + q))
-            ref[l, 16:24, 256:384] = spread(halo_edges[l // 8], 16 * (l % 8) + 8 * q)
+            ref[l, 16:24, 256:384] = jnp.where(inside, spread(halo_edges[l // 8], 16 * (l % 8) + 8 * q), 0.0)
         for t in range(2):
             cols = slice(128 * t, 128 * t + 128)
             high = high_ref[2 * l + t]
             low = low_ref[2 * l + t]
-            k_ref[l, 16:24, cols] = jnp.where(sub < 4, high, low)
-            v0_ref[l, 16:24, cols] = pltpu.roll(jnp.where(sub < 4, low, high), 4, axis=0)
+            k_ref[l, 16:24, cols] = jnp.where(inside, jnp.where(sub < 4, high, low), 0.0)
+            v0_ref[l, 16:24, cols] = jnp.where(inside, pltpu.roll(jnp.where(sub < 4, low, high), 4, axis=0), 0.0)
 
     def setup(l, carry):
         cz_before, s0, m0 = carry
@@ -128,7 +129,7 @@
 
     none = jnp.zeros((8, 128), F32)
     no_map = jnp.zeros((ROWS, WIDTH), F32)
-    _, s0, m0 = lax.fori_loop(0, LAYERS, setup, (k_ref[0], none, no_map), unroll=4)
+    _, s0, m0 = lax.fori_loop(0, LAYERS, setup, (k_ref[0], none, no_map), unroll=8)
 
     def image(l, v_ref, fz_before):
         v = v_ref[l]
@@ -152,7 +153,7 @@
             return fz, odd + folded(own(v) * got), even + folded(mine * got), total + mine
 
         start = (-(k_ref[0] * v_ref[0]), none, none, no_map)
-        return lax.fori_loop(0, LAYERS, body, start, unroll=4)[1:]
+        return lax.fori_loop(0, LAYERS, body, start, unroll=8)[1:]
 
     s1, s2, m1 = step(v0_ref, v1_ref, 1)
     s3, s4, m2 = step(v1_ref, v2_ref, 2)
@@ -162,16 +163,20 @@
         v, result, fz = image(l, v2_ref, fz_before)
         return fz, odd + folded(own(v) * own(result))
 
-    _, s5 = lax.fori_loop(0, LAYERS, last, (-(k_ref[0] * v2_ref[0]), none), unroll=4)
+    _, s5 = lax.fori_loop(0, LAYERS, last, (-(k_ref[0] * v2_ref[0]), none), unroll=8)
 
     sums = none
     for n, part in enumerate((s0, s1, s2, s3, s4, s5)):
         sums = jnp.where(sub == n, jnp.sum(part), sums)
-    for t in range(2):
-        for f, total in enumerate((m0, m1, m2)):
-            square_ref[48 * t + 16 * f : 48 * t + 16 * f + 16, :] = total[:, 128 * t : 128 * t + 128]
-    square_ref[96:104, :] = sums
-    square_ref[104:128, :] = jnp.zeros((24, 128), F32)
+    first = lax.broadcasted_iota(jnp.int32, (ROWS, 128), 1) % 8 < 4
+    for f, total in enumerate((m0, m1, m2)):
+        left, right = total[:, :128], total[:, 128:]
+        square_ref[16 * f : 16 * f + 16, :] = jnp.where(first, left, pltpu.roll(right, 4, axis=1))
+        square_ref[64 + 16 * f : 80 + 16 * f, :] = jnp.where(first, pltpu.roll(left, 124, axis=1), right)
+    square_ref[48:56, :] = sums
+    square_ref[56:64, :] = none
+    square_ref[112:120, :] = none
+    square_ref[120:128, :] = none
     turned = square_ref[...].T
     for j in range(LAYERS):
         ret_ref[j, 12] = turned[8 * j : 8 * j + 8, :]
@@ -184,18 +189,17 @@
 
 
 def route_kernel(owner_ref, index_ref, recv_ref, msg_ref):
-    lane = lanes()
+    lane = lax.broadcasted_iota(jnp.int32, (4, 128), 1)
+    shared = (lane >= 48) & (lane < 64)
     total = tree([recv_ref[j, 12] for j in range(LAYERS)])
-    common = pltpu.roll(total, 80, axis=1)
+    common = total[:4]
     for o in range(SLABS):
-        msg_ref[o] = common[:4]
+        msg_ref[o] = common
     row = index_ref[0] // PER_TILE
     for c in range(TILE_COLS):
-        strip = recv_ref[c // 2, 12]
-        first = pltpu.roll(strip, 80, axis=1) if c % 2 else strip
-        second = pltpu.roll(pltpu.roll(strip, 16 if c % 2 else 64, axis=1), 4, axis=0)
-        both = jnp.where(lane < 48, first, jnp.where(lane < 64, common, second))
-        msg_ref[owner_ref[row, c]] = both[:4]
+        half = 4 * (c % 2)
+        strip = recv_ref[c // 2, 12, half : half + 4]
+        msg_ref[owner_ref[row, c]] = jnp.where(shared, common, strip)
 
 
 def weights(s):
@@ -273,16 +277,16 @@
     return call(halo_kernel, [VMEM], [side, side], interpret=interpret)(recv)
 
 
-def krylov(recv, low, high, interpret=False):
+def krylov(index, recv, low, high, interpret=False):
     field = pltpu.VMEM((LAYERS + 1, EXT_ROWS, EXT_COLS), F32)
     face = pltpu.VMEM((LAYERS, EXT_ROWS, EXT_COLS), F32)
     return call(
         krylov_kernel,
-        [VMEM] * 3,
+        [SMEM] + [VMEM] * 3,
         [shape(LAYERS, 13, 8, 128)],
         [field] * 4 + [face] * 4 + [pltpu.VMEM((128, 128), F32)],
         interpret=interpret,
-    )(recv, low, high)
+    )(index, recv, low, high)
 
 
 def route(owner, index, recv, interpret=False):
@@ -308,10 +312,11 @@
     count = lax.axis_size("slab")
     recv = lax.all_to_all(pack(conductivity, adjoint_source), "layer", 0, 0, tiled=True)
     up, down = halo(recv)
-    low = lax.ppermute(up, "slab", [(i, i + 1) for i in range(count - 1)])
-    high = lax.ppermute(down, "slab", [(i + 1, i) for i in range(count - 1)])
-    back = lax.all_to_all(krylov(recv, low, high), "layer", 0, 0, tiled=True)
-    outgoing = route(tile_owner, index.reshape(1), back)
+    place = index.reshape(1)
+    low = lax.ppermute(up, "slab", [(i, (i + 1) % count) for i in range(count)])
+    high = lax.ppermute(down, "slab", [((i + 1) % count, i) for i in range(count)])
+    back = lax.all_to_all(krylov(place, recv, low, high), "layer", 0, 0, tiled=True)
+    outgoing = route(tile_owner, place, back)
     received = lax.all_to_all(outgoing, "slab", 0, 0, tiled=True)
     return finish(owned_rows(tile_owner, index), received, back)
 

time: 112 us -> 111 us (level)
  starting transfers between devices: 24.1 us -> 27.2 us
  waiting for transfers between devices: 40.3 us -> 38 us
    ppermute x2, starting transfers between devices: 2.59 us -> 13.5 us  [the longest x1 11.5 us: per_device(): lax.ppermute(down, 'slab', [((i + 1) % count, i) for i in range(count)])]
    all_to_all x1, starting transfers between devices: 17.2 us -> 9.21 us  [per_device(): received = lax.all_to_all(outgoing, 'slab', 0, 0, tiled=True)]
    ppermute x2, waiting for transfers between devices: 5.75 us -> 2.77 us  [the longest x1 1.91 us: per_device(): low = lax.ppermute(up, 'slab', [(i, (i + 1) % count) for i in range(count)])]
where the time goes in v3:
time: 111 us
  waiting for transfers between devices  38 us (34%)
  blocking collectives  35.6 us (32%)
  starting transfers between devices  27.2 us (25%)
  Pallas kernels  6.83 us (6%)
  local copies, waits for them, and re-layouts  1.9 us (2%)
    all_to_all x1, blocking collectives, per_device(): lax.all_to_all(pack(conductivity, adjoint_source), 'layer', 0, 0, tiled=T...  35.6 us
    all_to_all x1, waiting for transfers between devices, per_device(): lax.all_to_all(krylov(place, recv, low, high), 'layer', 0, 0, tiled=True)  23.7 us
    ppermute x1, starting transfers between devices, per_device(): lax.ppermute(down, 'slab', [((i + 1) % count, i) for i in range(count)])  11.5 us
    all_to_all x1, waiting for transfers between devices, per_device(): received = lax.all_to_all(outgoing, 'slab', 0, 0, tiled=True)  11.5 us
    all_to_all x1, starting transfers between devices, per_device(): received = lax.all_to_all(outgoing, 'slab', 0, 0, tiled=True)  9.21 us
    all_to_all x1, starting transfers between devices, per_device(): lax.all_to_all(krylov(place, recv, low, high), 'layer', 0, 0, tiled=True)  4.55 us
    pallas_call x1, Pallas kernels, krylov(): call(krylov_kernel, [SMEM] + [VMEM] * 3, [shape(LAYERS, 13, 8, 128)], [fi...  3.81 us
  transfers between devices with their start and end apart: 4, of which 4 were waited for; matrix products, arithmetic and copies ran while one was open for 0% of the time, Pallas kernels for 0%

profile of v3, /device:TPU:1, one launch (start us, length us, event | category | flops | bytes accessed | tf_op | source)
XLA Modules:
  0.0 110.7 jit_solution(9784256963504562812)
XLA Ops:
  0.6 0.0 copy-start
  0.6 0.9 copy-done
  1.6 0.0 copy-start.1
  1.6 0.9 copy-done.1
  2.5 0.1 shard_map.50
  2.7 35.6 %all_to_all.15.recv_ref = f32[16,9,8,128]{3,2,1,0:T(8,128)S(1)} all-to-all(f32[16,9,8,128]{3,2,1,0:T(8,128)S(1)} %shard_map.50), channel_id=1, replica_groups=mesh['slab'=64,'layer'=16] {'layer'}, dimensions={0} | all-to-all | bytes 1179648 | tf_op jit(solution)/shard_map/all_to_all | solution.py:313
  38.3 0.1 shard_map.51
  38.4 1.9 %collective-permute-start = (f32[33,8,128]{2,1,0:T(8,128)S(1)}, f32[33,8,128]{2,1,0:T(8,128)S(1)}, u32[]{:S(2)}, u32[]{:S(2)}) collective-permute-start(f32[33,8,128]{2,1,0:T(8,128)S(1)} %get-tuple-element.4), channel_id=1, source_target_pairs={{0,16},{16,32},{32,48},{48,64},{64,80},{80,96},{96,112},{112,128},... | collective-permute-start | bytes 405512 | tf_op jit(solution)/shard_map/ppermute | solution.py:316
  40.4 11.5 %collective-permute-start.1 = (f32[33,8,128]{2,1,0:T(8,128)S(1)}, f32[33,8,128]{2,1,0:T(8,128)S(1)}, u32[]{:S(2)}, u32[]{:S(2)}) collective-permute-start(f32[33,8,128]{2,1,0:T(8,128)S(1)} %get-tuple-element.5), channel_id=1, source_target_pairs={{16,0},{32,16},{48,32},{64,48},{80,64},{96,80},{112,96},{128,112},... | collective-permute-start | bytes 405512 | tf_op jit(solution)/shard_map/ppermute | solution.py:317
  51.9 1.9 %collective-permute-done.low_ref = f32[33,8,128]{2,1,0:T(8,128)S(1)} collective-permute-done((f32[33,8,128]{2,1,0:T(8,128)S(1)}, f32[33,8,128]{2,1,0:T(8,128)S(1)}, u32[]{:S(2)}, u32[]{:S(2)}) %collective-permute-start) | collective-permute-done | bytes 135200 | tf_op jit(solution)/shard_map/ppermute | solution.py:316
  53.8 0.9 collective-permute-done.1.high_ref
  54.7 3.8 %shard_map.52 = f32[16,13,8,128]{3,2,1,0:T(8,128)} custom-call(s32[1]{0:T(128)} %bitcast.2.index_ref, f32[16,9,8,128]{3,2,1,0:T(8,128)S(1)} %all_to_all.15.recv_ref, f32[33,8,128]{2,1,0:T(8,128)S(1)} %collective-permute-done.low_ref, f32[33,8,128]{2,1,0:T(8,128)S(1)} %collective-permute-done.1.high_ref), custom_call_target="tpu_custom_call" | custom-call | tf_op jit(solution)/shard_map/pallas_call | solution.py:283
  58.5 0.0 copy-start.2
  58.5 4.5 %all-to-all-start.1 = ((f32[16,13,8,128]{3,2,1,0:T(8,128)}), f32[16,13,8,128]{3,2,1,0:T(8,128)S(1)}, u32[]{:S(2)}, u32[]{:S(2)}) async-start(f32[16,13,8,128]{3,2,1,0:T(8,128)} %shard_map.52), calls=%async_computation.1 | async-start | bytes 1703936 | tf_op jit(solution)/shard_map/all_to_all | solution.py:318
  63.0 0.0 copy-done.2
  63.0 0.1 compare_reduce_fusion
  63.2 0.2 reduce-window.8
  63.3 23.7 %all-to-all-done.1.recv_ref.ret_ref = f32[16,13,8,128]{3,2,1,0:T(8,128)S(1)} async-done(((f32[16,13,8,128]{3,2,1,0:T(8,128)}), f32[16,13,8,128]{3,2,1,0:T(8,128)S(1)}, u32[]{:S(2)}, u32[]{:S(2)}) %all-to-all-start.1) | async-done | bytes 852000 | tf_op jit(solution)/shard_map/all_to_all | solution.py:318
  87.1 1.3 %shard_map.53 = f32[64,4,128]{2,1,0:T(4,128)} custom-call(s32[8,32]{1,0:T(8,128)S(1)} %copy-done.2, s32[1]{0:T(128)} %bitcast.2.index_ref, f32[16,13,8,128]{3,2,1,0:T(8,128)S(1)} %all-to-all-done.1.recv_ref.ret_ref), custom_call_target="tpu_custom_call" | custom-call | tf_op jit(solution)/shard_map/pallas_call | solution.py:293
  88.4 9.2 %all-to-all-start.2 = ((f32[64,4,128]{2,1,0:T(4,128)}), f32[64,4,128]{2,1,0:T(4,128)S(1)}, u32[]{:S(2)}, u32[]{:S(2)}) async-start(f32[64,4,128]{2,1,0:T(4,128)} %shard_map.53), calls=%async_computation.2 | async-start | bytes 262144 | tf_op jit(solution)/shard_map/all_to_all | solution.py:320
  97.6 0.1 select_reduce_fusion.rows_ref
  97.7 11.5 %all-to-all-done.2.recv_ref = f32[64,4,128]{2,1,0:T(4,128)S(1)} async-done(((f32[64,4,128]{2,1,0:T(4,128)}), f32[64,4,128]{2,1,0:T(4,128)S(1)}, u32[]{:S(2)}, u32[]{:S(2)}) %all-to-all-start.2) | async-done | bytes 131104 | tf_op jit(solution)/shard_map/all_to_all | solution.py:320
  109.2 1.5 %shard_map.54 = (f32[1,16,4096]{2,1,0:T(8,128)}, f32[4,8,128]{2,1,0:T(8,128)}) custom-call(s32[4]{0:T(128)S(1)} %select_reduce_fusion.rows_ref, f32[64,4,128]{2,1,0:T(4,128)S(1)} %all-to-all-done.2.recv_ref, f32[16,13,8,128]{3,2,1,0:T(8,128)S(1)} %all-to-all-done.1.recv_ref.ret_ref), custom_call_target="tpu_custom_call" | custom-call | tf_op jit(solution)/shard_map/pallas_call | solution.py:297
  (2 shorter events, 0.0 us)
Async XLA Ops:
  0.6 1.0 copy-start
  1.6 0.9 copy-start.1
  38.4 15.4 %collective-permute-start = (f32[33,8,128]{2,1,0:T(8,128)S(1)}, f32[33,8,128]{2,1,0:T(8,128)S(1)}, u32[]{:S(2)}, u32[]{:S(2)}) collective-permute-start(f32[33,8,128]{2,1,0:T(8,128)S(1)} %get-tuple-element.4), channel_id=1, source_target_pairs={{0,16},{16,32},{32,48},{48,64},{64,80},{80,96},{96,112},{112,128},... | collective-permute-start | bytes 405512 | tf_op jit(solution)/shard_map/ppermute | solution.py:316
  40.4 14.3 %collective-permute-start.1 = (f32[33,8,128]{2,1,0:T(8,128)S(1)}, f32[33,8,128]{2,1,0:T(8,128)S(1)}, u32[]{:S(2)}, u32[]{:S(2)}) collective-permute-start(f32[33,8,128]{2,1,0:T(8,128)S(1)} %get-tuple-element.5), channel_id=1, source_target_pairs={{16,0},{32,16},{48,32},{64,48},{80,64},{96,80},{112,96},{128,112},... | collective-permute-start | bytes 405512 | tf_op jit(solution)/shard_map/ppermute | solution.py:317
  58.5 4.5 %copy-start.2 = (s32[8,32]{1,0:T(8,128)S(1)}, s32[8,32]{1,0:T(8,128)}, u32[]{:S(2)}) copy-start(s32[8,32]{1,0:T(8,128)} %owner_ref.1) | copy-start | bytes 3076
  58.5 28.6 %all-to-all-start.1 = ((f32[16,13,8,128]{3,2,1,0:T(8,128)}), f32[16,13,8,128]{3,2,1,0:T(8,128)S(1)}, u32[]{:S(2)}, u32[]{:S(2)}) async-start(f32[16,13,8,128]{3,2,1,0:T(8,128)} %shard_map.52), calls=%async_computation.1 | async-start | bytes 1703936 | tf_op jit(solution)/shard_map/all_to_all | solution.py:318
  88.4 20.9 %all-to-all-start.2 = ((f32[64,4,128]{2,1,0:T(4,128)}), f32[64,4,128]{2,1,0:T(4,128)S(1)}, u32[]{:S(2)}, u32[]{:S(2)}) async-start(f32[64,4,128]{2,1,0:T(4,128)} %shard_map.53), calls=%async_computation.2 | async-start | bytes 262144 | tf_op jit(solution)/shard_map/all_to_all | solution.py:320

commit v4 on v3

--- a/solution.py
+++ b/solution.py
@@ -27,19 +27,19 @@
     return lax.broadcasted_iota(jnp.int32, (8, 128), 0)
 
 
-def pack_kernel(cond_ref, src_ref, out_ref):
+def pack_kernel(both_ref, out_ref):
     lane = lanes()
     zero = jnp.zeros((8, 128), F32)
     for j in range(LAYERS):
         edge = zero
-        for q, ref in enumerate((cond_ref, src_ref)):
+        for q in range(2):
             for g in range(2):
                 rows = slice(8 * g, 8 * g + 8)
                 base = WIDTH * j
                 for t in range(2):
-                    out_ref[j, 4 * q + 2 * g + t] = ref[0, rows, base + 128 * t : base + 128 * t + 128]
-                before = ref[0, rows, base - 128 : base] if j > 0 else zero
-                after = ref[0, rows, base + 256 : base + 384] if j < LAYERS - 1 else zero
+                    out_ref[j, 4 * q + 2 * g + t] = both_ref[q, rows, base + 128 * t : base + 128 * t + 128]
+                before = both_ref[q, rows, base - 128 : base] if j > 0 else zero
+                after = both_ref[q, rows, base + 256 : base + 384] if j < LAYERS - 1 else zero
                 both = jnp.where(lane < 4, after, jnp.where(lane >= 124, before, 0.0))
                 edge = edge + pltpu.roll(both, 4 + 8 * (2 * g + q), axis=1)
         out_ref[j, 8] = edge
@@ -72,7 +72,7 @@
 
 
 def krylov_kernel(
-    index_ref, recv_ref, low_ref, high_ref, ret_ref, k_ref, v0_ref, v1_ref, v2_ref, inv_ref, cc_ref, cr_ref, cz_ref, square_ref
+    index_ref, rows_ref, recv_ref, low_ref, high_ref, msg_ref, ret_ref, k_ref, v0_ref, v1_ref, v2_ref, inv_ref, cc_ref, cr_ref, cz_ref, square_ref
 ):
     lane = lanes()
     sub = sublanes()
@@ -179,7 +179,7 @@
     square_ref[120:128, :] = none
     turned = square_ref[...].T
     for j in range(LAYERS):
-        ret_ref[j, 12] = turned[8 * j : 8 * j + 8, :]
+        msg_ref[j] = turned[8 * j : 8 * j + 8, :]
 
 
 def tree(values):
@@ -191,14 +191,14 @@
 def route_kernel(owner_ref, index_ref, recv_ref, msg_ref):
     lane = lax.broadcasted_iota(jnp.int32, (4, 128), 1)
     shared = (lane >= 48) & (lane < 64)
-    total = tree([recv_ref[j, 12] for j in range(LAYERS)])
+    total = tree([recv_ref[j] for j in range(LAYERS)])
     common = total[:4]
     for o in range(SLABS):
         msg_ref[o] = common
     row = index_ref[0] // PER_TILE
     for c in range(TILE_COLS):
         half = 4 * (c % 2)
-        strip = recv_ref[c // 2, 12, half : half + 4]
+        strip = recv_ref[c // 2, half : half + 4]
         msg_ref[owner_ref[row, c]] = jnp.where(shared, common, strip)
 
 
@@ -220,19 +220,32 @@
     return x0 + a2 * p0, x1 + a2 * p1, a2 * p2
 
 
-def finish_kernel(rows_ref, recv_ref, ret_ref, adjoint_ref, owned_ref):
+def solved(recv_ref):
+    total = tree([recv_ref[s] for s in range(SLABS)])
+    return weights([jnp.broadcast_to(total[:1, 48 + n : 49 + n], (8, 128)) for n in range(6)])
+
+
+def combine_kernel(recv_ref, ret_ref, out_ref):
+    w0, w1, w2 = solved(recv_ref)
+    for l in range(LAYERS):
+        for n in range(4):
+            out_ref[l, n] = w0 * ret_ref[l, n] + w1 * ret_ref[l, 4 + n] + w2 * ret_ref[l, 8 + n]
+
+
+def finish_kernel(rows_ref, recv_ref, back_ref, adjoint_ref, owned_ref, full_ref, sems):
     lane = lanes()
     sub = sublanes()
-    total = tree([recv_ref[s] for s in range(SLABS)])
-    moments = [jnp.broadcast_to(total[:1, 48 + n : 49 + n], (8, 128)) for n in range(6)]
-    w0, w1, w2 = weights(moments)
-    for j in range(LAYERS):
-        for g in range(2):
-            for t in range(2):
-                n = 2 * g + t
-                value = w0 * ret_ref[j, n] + w1 * ret_ref[j, 4 + n] + w2 * ret_ref[j, 8 + n]
-                col = WIDTH * j + 128 * t
-                adjoint_ref[0, 8 * g : 8 * g + 8, col : col + 128] = value
+    copies = []
+    for part in range(4):
+        for j in range(4 * part, 4 * part + 4):
+            for n in range(4):
+                col = WIDTH * j + 128 * (n % 2)
+                full_ref[0, 8 * (n // 2) : 8 * (n // 2) + 8, col : col + 128] = back_ref[j, n]
+        cols = slice(COLS // 4 * part, COLS // 4 * (part + 1))
+        copy = pltpu.make_async_copy(full_ref.at[:, :, cols], adjoint_ref.at[:, :, cols], sems.at[part])
+        copy.start()
+        copies.append(copy)
+    w0, w1, w2 = solved(recv_ref)
     for k in range(OWNED):
         row = rows_ref[k]
         tile = jnp.zeros((8, 128), F32)
@@ -245,6 +258,8 @@
                 value = pltpu.roll(value, 16 * i, axis=1)
             tile = jnp.where((lane >= 16 * i) & (lane < 16 * i + 16), value, tile)
         owned_ref[k] = tile
+    for copy in copies:
+        copy.wait()
 
 
 VMEM = pl.BlockSpec(memory_space=pltpu.VMEM)
@@ -255,21 +270,23 @@
     return jax.ShapeDtypeStruct(dims, F32)
 
 
-def call(kernel, ins, outs, scratch=(), interpret=False):
+def call(kernel, ins, outs, scratch=(), interpret=False, out_specs=None):
     single = len(outs) == 1
+    if out_specs is None:
+        out_specs = VMEM if single else tuple(VMEM for _ in outs)
     return pl.pallas_call(
         kernel,
         out_shape=outs[0] if single else tuple(outs),
         in_specs=ins,
-        out_specs=VMEM if single else tuple(VMEM for _ in outs),
+        out_specs=out_specs,
         scratch_shapes=list(scratch),
         compiler_params=pltpu.CompilerParams(vmem_limit_bytes=VMEM_LIMIT),
         interpret=interpret,
     )
 
 
-def pack(cond, src, interpret=False):
-    return call(pack_kernel, [VMEM] * 2, [shape(LAYERS, 9, 8, 128)], interpret=interpret)(cond, src)
+def pack(both, interpret=False):
+    return call(pack_kernel, [VMEM], [shape(LAYERS, 9, 8, 128)], interpret=interpret)(both)
 
 
 def halo(recv, interpret=False):
@@ -277,26 +294,35 @@
     return call(halo_kernel, [VMEM], [side, side], interpret=interpret)(recv)
 
 
-def krylov(index, recv, low, high, interpret=False):
+def krylov(index, rows, recv, low, high, interpret=False):
     field = pltpu.VMEM((LAYERS + 1, EXT_ROWS, EXT_COLS), F32)
     face = pltpu.VMEM((LAYERS, EXT_ROWS, EXT_COLS), F32)
     return call(
         krylov_kernel,
-        [SMEM] + [VMEM] * 3,
-        [shape(LAYERS, 13, 8, 128)],
+        [SMEM] * 2 + [VMEM] * 3,
+        [shape(LAYERS, 8, 128), shape(LAYERS, 12, 8, 128)],
         [field] * 4 + [face] * 4 + [pltpu.VMEM((128, 128), F32)],
         interpret=interpret,
-    )(index, recv, low, high)
+    )(index, rows, recv, low, high)
 
 
 def route(owner, index, recv, interpret=False):
     return call(route_kernel, [SMEM, SMEM, VMEM], [shape(SLABS, 4, 128)], interpret=interpret)(owner, index, recv)
 
 
-def finish(rows, recv, ret, interpret=False):
+def combine(recv, ret, interpret=False):
+    return call(combine_kernel, [VMEM] * 2, [shape(LAYERS, 4, 8, 128)], interpret=interpret)(recv, ret)
+
+
+def finish(rows, recv, back, interpret=False):
     return call(
-        finish_kernel, [SMEM, VMEM, VMEM], [shape(1, ROWS, COLS), shape(OWNED, 8, 128)], interpret=interpret
-    )(rows, recv, ret)
+        finish_kernel,
+        [SMEM, VMEM, VMEM],
+        [shape(1, ROWS, COLS), shape(OWNED, 8, 128)],
+        [pltpu.VMEM((1, ROWS, COLS), F32), pltpu.SemaphoreType.DMA((4,))],
+        interpret=interpret,
+        out_specs=(pl.BlockSpec(memory_space=pl.ANY), VMEM),
+    )(rows, recv, back)
 
 
 def owned_rows(tile_owner, index):
@@ -310,15 +336,19 @@
 def per_device(adjoint_source, conductivity, tile_owner):
     index = lax.axis_index("slab")
     count = lax.axis_size("slab")
-    recv = lax.all_to_all(pack(conductivity, adjoint_source), "layer", 0, 0, tiled=True)
+    recv = lax.all_to_all(pack(jnp.concatenate([conductivity, adjoint_source], axis=0)), "layer", 0, 0, tiled=True)
     up, down = halo(recv)
+    tile_owner, up = lax.optimization_barrier((tile_owner, up))
+    rows = owned_rows(tile_owner, index)
     place = index.reshape(1)
     low = lax.ppermute(up, "slab", [(i, (i + 1) % count) for i in range(count)])
     high = lax.ppermute(down, "slab", [((i + 1) % count, i) for i in range(count)])
-    back = lax.all_to_all(krylov(place, recv, low, high), "layer", 0, 0, tiled=True)
-    outgoing = route(tile_owner, place, back)
+    msg, ret = krylov(place, rows, recv, low, high)
+    strips = lax.all_to_all(msg, "layer", 0, 0, tiled=True)
+    outgoing = route(tile_owner, place, strips)
     received = lax.all_to_all(outgoing, "slab", 0, 0, tiled=True)
-    return finish(owned_rows(tile_owner, index), received, back)
+    back = lax.all_to_all(combine(received, ret), "layer", 0, 0, tiled=True)
+    return finish(rows, received, back)
 
 
 def solution(mesh):

time: 111 us -> 110 us (level)
  waiting for transfers between devices: 38 us -> 20.8 us
  blocking collectives: 35.6 us -> 48.3 us
  starting transfers between devices: 27.2 us -> 30.4 us
  local copies, waits for them, and re-layouts: 1.9 us -> 0.59 us
    all_to_all x2 -> x1, waiting for transfers between devices: 35.2 us -> 18.6 us  [per_device(): lax.all_to_all(pack(jnp.concatenate([conductivity, adjoint_source], axis=...]
    all_to_all x1 -> x3, blocking collectives: 35.6 us -> 48.3 us  [the longest x1 20.5 us: per_device(): received = lax.all_to_all(outgoing, 'slab', 0, 0, tiled=True)]
    all_to_all x2 -> x1, starting transfers between devices: 13.8 us -> 17.5 us  [per_device(): lax.all_to_all(pack(jnp.concatenate([conductivity, adjoint_source], axis=...]
    ppermute x1, waiting for transfers between devices: 1.91 us -> 0.42 us  [per_device(): low = lax.ppermute(up, 'slab', [(i, (i + 1) % count) for i in range(count)])]
    unnamed x6 -> x2, local copies, waits for them, and re-layouts: 1.9 us -> 0.59 us
    pallas_call x2 -> x3, Pallas kernels: 3.95 us -> 4.59 us  [the longest x1 3.42 us: krylov(): call(krylov_kernel, [SMEM] * 2 + [VMEM] * 3, [shape(LAYERS, 8, 128), shap...]
  transfers between devices with their start and end apart: 4 -> 3, of which waited for: 4 -> 3; matrix products, arithmetic and copies ran while one was open for 0% -> 0% of each run, Pallas kernels for 0% -> 0%
where the time goes in v4:
time: 110 us
  blocking collectives  48.3 us (44%)
  starting transfers between devices  30.4 us (28%)
  waiting for transfers between devices  20.8 us (19%)
  Pallas kernels  7.44 us (7%)
  other arithmetic  1.5 us (1%)
    all_to_all x1, blocking collectives, per_device(): received = lax.all_to_all(outgoing, 'slab', 0, 0, tiled=True)  20.5 us
    all_to_all x1, waiting for transfers between devices, per_device(): lax.all_to_all(pack(jnp.concatenate([conductivity, adjoint_source], axis=...  18.6 us
    all_to_all x1, starting transfers between devices, per_device(): lax.all_to_all(pack(jnp.concatenate([conductivity, adjoint_source], axis=...  17.5 us
    all_to_all x1, blocking collectives, per_device(): back = lax.all_to_all(combine(received, ret), 'layer', 0, 0, tiled=True)  16.4 us
    all_to_all x1, blocking collectives, per_device(): strips = lax.all_to_all(msg, 'layer', 0, 0, tiled=True)  11.5 us
    ppermute x1, starting transfers between devices, per_device(): lax.ppermute(down, 'slab', [((i + 1) % count, i) for i in range(count)])  10.9 us
    pallas_call x1, Pallas kernels, krylov(): call(krylov_kernel, [SMEM] * 2 + [VMEM] * 3, [shape(LAYERS, 8, 128), shap...  3.42 us
  transfers between devices with their start and end apart: 3, of which 3 were waited for; matrix products, arithmetic and copies ran while one was open for 0% of the time, Pallas kernels for 0%

profile of v4, /device:TPU:1, one launch (start us, length us, event | category | flops | bytes accessed | tf_op | source)
XLA Modules:
  0.0 109.7 jit_solution(1049898284068429422)
XLA Ops:
  0.6 1.1 pad_maximum_fusion.both_ref
  1.7 1.0 shard_map.50
  2.7 17.5 %all-to-all-start = ((f32[16,9,8,128]{3,2,1,0:T(8,128)}), f32[16,9,8,128]{3,2,1,0:T(8,128)S(1)}, u32[]{:S(2)}, u32[]{:S(2)}) async-start(f32[16,9,8,128]{3,2,1,0:T(8,128)} %shard_map.50), calls=%async_computation | async-start | bytes 1179648 | tf_op jit(solution)/shard_map/all_to_all | solution.py:339
  20.2 18.6 %all-to-all-done.recv_ref = f32[16,9,8,128]{3,2,1,0:T(8,128)S(1)} async-done(((f32[16,9,8,128]{3,2,1,0:T(8,128)}), f32[16,9,8,128]{3,2,1,0:T(8,128)S(1)}, u32[]{:S(2)}, u32[]{:S(2)}) %all-to-all-start) | async-done | bytes 589856 | tf_op jit(solution)/shard_map/all_to_all | solution.py:339
  38.8 0.0 copy-start
  38.8 0.1 shard_map.51
  38.9 0.6 copy-done
  39.5 0.1 compare_reduce_fusion
  39.6 1.9 %collective-permute-start = (f32[33,8,128]{2,1,0:T(8,128)S(1)}, f32[33,8,128]{2,1,0:T(8,128)S(1)}, u32[]{:S(2)}, u32[]{:S(2)}) collective-permute-start(f32[33,8,128]{2,1,0:T(8,128)S(1)} %get-tuple-element.10), channel_id=1, source_target_pairs={{0,16},{16,32},{32,48},{48,64},{64,80},{80,96},{96,112},{112,128},... | collective-permute-start | bytes 405512 | tf_op jit(solution)/shard_map/ppermute | solution.py:344
  41.6 10.9 %collective-permute-start.1 = (f32[33,8,128]{2,1,0:T(8,128)S(1)}, f32[33,8,128]{2,1,0:T(8,128)S(1)}, u32[]{:S(2)}, u32[]{:S(2)}) collective-permute-start(f32[33,8,128]{2,1,0:T(8,128)S(1)} %get-tuple-element.11), channel_id=1, source_target_pairs={{16,0},{32,16},{48,32},{64,48},{80,64},{96,80},{112,96},{128,112},... | collective-permute-start | bytes 405512 | tf_op jit(solution)/shard_map/ppermute | solution.py:345
  52.5 0.2 reduce-window.8
  52.7 0.1 select_reduce_fusion.rows_ref
  52.8 0.4 collective-permute-done.low_ref
  53.2 1.8 %collective-permute-done.1.high_ref = f32[33,8,128]{2,1,0:T(8,128)S(1)} collective-permute-done((f32[33,8,128]{2,1,0:T(8,128)S(1)}, f32[33,8,128]{2,1,0:T(8,128)S(1)}, u32[]{:S(2)}, u32[]{:S(2)}) %collective-permute-start.1) | collective-permute-done | bytes 135200 | tf_op jit(solution)/shard_map/ppermute | solution.py:345
  55.0 3.4 %shard_map.52 = (f32[16,8,128]{2,1,0:T(8,128)S(1)}, f32[16,12,8,128]{3,2,1,0:T(8,128)S(1)}) custom-call(s32[1]{0:T(128)} %bitcast.2.index_ref, s32[4]{0:T(128)S(1)} %select_reduce_fusion.rows_ref, f32[16,9,8,128]{3,2,1,0:T(8,128)S(1)} %all-to-all-done.recv_ref, f32[33,8,128]{2,1,0:T(8,128)S(1)} %collective-permute-done.low_ref, ...), custom_call_target="tpu_custom_call" | custom-call | tf_op jit(solution)/shard_map/pallas_call | solution.py:300
  58.4 11.5 %all_to_all.20.recv_ref = f32[16,8,128]{2,1,0:T(8,128)S(1)} all-to-all(f32[16,8,128]{2,1,0:T(8,128)S(1)} %get-tuple-element.12), channel_id=1, replica_groups=mesh['slab'=64,'layer'=16] {'layer'}, dimensions={0} | all-to-all | bytes 131072 | tf_op jit(solution)/shard_map/all_to_all | solution.py:347
  69.9 0.6 shard_map.53
  70.5 20.5 %all_to_all.21.recv_ref = f32[64,4,128]{2,1,0:T(4,128)S(1)} all-to-all(f32[64,4,128]{2,1,0:T(4,128)S(1)} %shard_map.53), channel_id=1, replica_groups=mesh['slab'=64,'layer'=16] {'slab'}, dimensions={0} | all-to-all | bytes 262144 | tf_op jit(solution)/shard_map/all_to_all | solution.py:349
  91.0 0.2 shard_map.54
  91.2 16.4 %all_to_all.22.back_ref = f32[16,4,8,128]{3,2,1,0:T(8,128)S(1)} all-to-all(f32[16,4,8,128]{3,2,1,0:T(8,128)S(1)} %shard_map.54), channel_id=1, replica_groups=mesh['slab'=64,'layer'=16] {'layer'}, dimensions={0} | all-to-all | bytes 524288 | tf_op jit(solution)/shard_map/all_to_all | solution.py:350
  107.6 2.1 %shard_map.55 = (f32[1,16,4096]{2,1,0:T(8,128)}, f32[4,8,128]{2,1,0:T(8,128)}) custom-call(s32[4]{0:T(128)S(1)} %select_reduce_fusion.rows_ref, f32[64,4,128]{2,1,0:T(4,128)S(1)} %all_to_all.21.recv_ref, f32[16,4,8,128]{3,2,1,0:T(8,128)S(1)} %all_to_all.22.back_ref), custom_call_target="tpu_custom_call" | custom-call | tf_op jit(solution)/shard_map/pallas_call | solution.py:318
  (2 shorter events, 0.0 us)
Async XLA Ops:
  2.7 36.2 %all-to-all-start = ((f32[16,9,8,128]{3,2,1,0:T(8,128)}), f32[16,9,8,128]{3,2,1,0:T(8,128)S(1)}, u32[]{:S(2)}, u32[]{:S(2)}) async-start(f32[16,9,8,128]{3,2,1,0:T(8,128)} %shard_map.50), calls=%async_computation | async-start | bytes 1179648 | tf_op jit(solution)/shard_map/all_to_all | solution.py:339
  38.8 0.7 copy-start
  39.6 13.6 %collective-permute-start = (f32[33,8,128]{2,1,0:T(8,128)S(1)}, f32[33,8,128]{2,1,0:T(8,128)S(1)}, u32[]{:S(2)}, u32[]{:S(2)}) collective-permute-start(f32[33,8,128]{2,1,0:T(8,128)S(1)} %get-tuple-element.10), channel_id=1, source_target_pairs={{0,16},{16,32},{32,48},{48,64},{64,80},{80,96},{96,112},{112,128},... | collective-permute-start | bytes 405512 | tf_op jit(solution)/shard_map/ppermute | solution.py:344
  41.6 13.4 %collective-permute-start.1 = (f32[33,8,128]{2,1,0:T(8,128)S(1)}, f32[33,8,128]{2,1,0:T(8,128)S(1)}, u32[]{:S(2)}, u32[]{:S(2)}) collective-permute-start(f32[33,8,128]{2,1,0:T(8,128)S(1)} %get-tuple-element.11), channel_id=1, source_target_pairs={{16,0},{32,16},{48,32},{64,48},{80,64},{96,80},{112,96},{128,112},... | collective-permute-start | bytes 405512 | tf_op jit(solution)/shard_map/ppermute | solution.py:345

commit v5 on v4

--- a/solution.py
+++ b/solution.py
@@ -45,22 +45,30 @@
         out_ref[j, 8] = edge
 
 
-def halo_kernel(recv_ref, up_ref, down_ref):
+def halo_kernel(index_ref, recv_ref, first_ref, second_ref):
+    even = index_ref[0] % 2 == 0
+
+    def put(n, up, down):
+        first_ref[n] = jnp.where(even, up, down)
+        second_ref[n] = jnp.where(even, down, up)
+
     lane = lanes()
     sub = sublanes()
     up_edges = [jnp.zeros((8, 128), F32)] * 2
     down_edges = [jnp.zeros((8, 128), F32)] * 2
     for l in range(LAYERS):
         for t in range(2):
-            up_ref[2 * l + t] = jnp.where(sub >= 4, recv_ref[l, 2 + t], pltpu.roll(recv_ref[l, 6 + t], 4, axis=0))
-            down_ref[2 * l + t] = jnp.where(sub < 4, recv_ref[l, t], pltpu.roll(recv_ref[l, 4 + t], 4, axis=0))
+            up = jnp.where(sub >= 4, recv_ref[l, 2 + t], pltpu.roll(recv_ref[l, 6 + t], 4, axis=0))
+            down = jnp.where(sub < 4, recv_ref[l, t], pltpu.roll(recv_ref[l, 4 + t], 4, axis=0))
+            put(2 * l + t, up, down)
         edge = recv_ref[l, 8]
         half, place = l // 8, 16 * (l % 8)
         here = (lane >= place) & (lane < place + 16)
         up_edges[half] = jnp.where(here, pltpu.roll(edge, (place + 112) % 128, axis=1), up_edges[half])
         down_edges[half] = jnp.where(here, pltpu.roll(edge, place, axis=1), down_edges[half])
-    up_ref[32] = jnp.where(sub >= 4, up_edges[0], pltpu.roll(up_edges[1], 4, axis=0))
-    down_ref[32] = jnp.where(sub < 4, down_edges[0], pltpu.roll(down_edges[1], 4, axis=0))
+    up = jnp.where(sub >= 4, up_edges[0], pltpu.roll(up_edges[1], 4, axis=0))
+    down = jnp.where(sub < 4, down_edges[0], pltpu.roll(down_edges[1], 4, axis=0))
+    put(32, up, down)
 
 
 def own(value):
@@ -72,7 +80,7 @@
 
 
 def krylov_kernel(
-    index_ref, rows_ref, recv_ref, low_ref, high_ref, msg_ref, ret_ref, k_ref, v0_ref, v1_ref, v2_ref, inv_ref, cc_ref, cr_ref, cz_ref, square_ref
+    index_ref, recv_ref, first_ref, second_ref, msg_ref, ret_ref, k_ref, v0_ref, v1_ref, v2_ref, inv_ref, cc_ref, cr_ref, cz_ref, square_ref
 ):
     lane = lanes()
     sub = sublanes()
@@ -84,13 +92,14 @@
     def spread(tile, place):
         return jnp.where(rim, pltpu.roll(tile, (252 - place) % 128, axis=1), 0.0)
 
-    inside = ((sub < 4) & (index_ref[0] < SLABS - 1)) | ((sub >= 4) & (index_ref[0] > 0))
-    low_edges = low_ref[32]
-    high_edges = high_ref[32]
-    halo_edges = (
-        jnp.where(sub < 4, high_edges, low_edges),
-        pltpu.roll(jnp.where(sub < 4, low_edges, high_edges), 4, axis=0),
-    )
+    even = index_ref[0] % 2 == 0
+    upper = (sub < 4) == even
+
+    def halves(n):
+        one, two = first_ref[n], second_ref[n]
+        return jnp.where(upper, one, two), pltpu.roll(jnp.where(upper, two, one), 4, axis=0)
+
+    halo_edges = halves(32)
     for l in range(LAYERS):
         edge = recv_ref[l, 8]
         for q, ref in enumerate((k_ref, v0_ref)):
@@ -98,13 +107,10 @@
                 for t in range(2):
                     ref[l, 8 * g : 8 * g + 8, 128 * t : 128 * t + 128] = recv_ref[l, 4 * q + 2 * g + t]
                 ref[l, 8 * g : 8 * g + 8, 256:384] = spread(edge, 8 * (2 * g + q))
-            ref[l, 16:24, 256:384] = jnp.where(inside, spread(halo_edges[l // 8], 16 * (l % 8) + 8 * q), 0.0)
+            ref[l, 16:24, 256:384] = spread(halo_edges[l // 8], 16 * (l % 8) + 8 * q)
         for t in range(2):
             cols = slice(128 * t, 128 * t + 128)
-            high = high_ref[2 * l + t]
-            low = low_ref[2 * l + t]
-            k_ref[l, 16:24, cols] = jnp.where(inside, jnp.where(sub < 4, high, low), 0.0)
-            v0_ref[l, 16:24, cols] = jnp.where(inside, pltpu.roll(jnp.where(sub < 4, low, high), 4, axis=0), 0.0)
+            k_ref[l, 16:24, cols], v0_ref[l, 16:24, cols] = halves(2 * l + t)
 
     def setup(l, carry):
         cz_before, s0, m0 = carry
@@ -232,19 +238,13 @@
             out_ref[l, n] = w0 * ret_ref[l, n] + w1 * ret_ref[l, 4 + n] + w2 * ret_ref[l, 8 + n]
 
 
-def finish_kernel(rows_ref, recv_ref, back_ref, adjoint_ref, owned_ref, full_ref, sems):
+def finish_kernel(rows_ref, recv_ref, back_ref, adjoint_ref, owned_ref):
     lane = lanes()
     sub = sublanes()
-    copies = []
-    for part in range(4):
-        for j in range(4 * part, 4 * part + 4):
-            for n in range(4):
-                col = WIDTH * j + 128 * (n % 2)
-                full_ref[0, 8 * (n // 2) : 8 * (n // 2) + 8, col : col + 128] = back_ref[j, n]
-        cols = slice(COLS // 4 * part, COLS // 4 * (part + 1))
-        copy = pltpu.make_async_copy(full_ref.at[:, :, cols], adjoint_ref.at[:, :, cols], sems.at[part])
-        copy.start()
-        copies.append(copy)
+    for j in range(LAYERS):
+        for n in range(4):
+            col = WIDTH * j + 128 * (n % 2)
+            adjoint_ref[0, 8 * (n // 2) : 8 * (n // 2) + 8, col : col + 128] = back_ref[j, n]
     w0, w1, w2 = solved(recv_ref)
     for k in range(OWNED):
         row = rows_ref[k]
@@ -258,8 +258,6 @@
                 value = pltpu.roll(value, 16 * i, axis=1)
             tile = jnp.where((lane >= 16 * i) & (lane < 16 * i + 16), value, tile)
         owned_ref[k] = tile
-    for copy in copies:
-        copy.wait()
 
 
 VMEM = pl.BlockSpec(memory_space=pltpu.VMEM)
@@ -270,15 +268,13 @@
     return jax.ShapeDtypeStruct(dims, F32)
 
 
-def call(kernel, ins, outs, scratch=(), interpret=False, out_specs=None):
+def call(kernel, ins, outs, scratch=(), interpret=False):
     single = len(outs) == 1
-    if out_specs is None:
-        out_specs = VMEM if single else tuple(VMEM for _ in outs)
     return pl.pallas_call(
         kernel,
         out_shape=outs[0] if single else tuple(outs),
         in_specs=ins,
-        out_specs=out_specs,
+        out_specs=VMEM if single else tuple(VMEM for _ in outs),
         scratch_shapes=list(scratch),
         compiler_params=pltpu.CompilerParams(vmem_limit_bytes=VMEM_LIMIT),
         interpret=interpret,
@@ -289,21 +285,21 @@
     return call(pack_kernel, [VMEM], [shape(LAYERS, 9, 8, 128)], interpret=interpret)(both)
 
 
-def halo(recv, interpret=False):
+def halo(index, recv, interpret=False):
     side = shape(2 * LAYERS + 1, 8, 128)
-    return call(halo_kernel, [VMEM], [side, side], interpret=interpret)(recv)
-
-
-def krylov(index, rows, recv, low, high, interpret=False):
+    return call(halo_kernel, [SMEM, VMEM], [side, side], interpret=interpret)(index, recv)
+
+
+def krylov(index, recv, first, second, interpret=False):
     field = pltpu.VMEM((LAYERS + 1, EXT_ROWS, EXT_COLS), F32)
     face = pltpu.VMEM((LAYERS, EXT_ROWS, EXT_COLS), F32)
     return call(
         krylov_kernel,
-        [SMEM] * 2 + [VMEM] * 3,
+        [SMEM] + [VMEM] * 3,
         [shape(LAYERS, 8, 128), shape(LAYERS, 12, 8, 128)],
         [field] * 4 + [face] * 4 + [pltpu.VMEM((128, 128), F32)],
         interpret=interpret,
-    )(index, rows, recv, low, high)
+    )(index, recv, first, second)
 
 
 def route(owner, index, recv, interpret=False):
@@ -315,14 +311,8 @@
 
 
 def finish(rows, recv, back, interpret=False):
-    return call(
-        finish_kernel,
-        [SMEM, VMEM, VMEM],
-        [shape(1, ROWS, COLS), shape(OWNED, 8, 128)],
-        [pltpu.VMEM((1, ROWS, COLS), F32), pltpu.SemaphoreType.DMA((4,))],
-        interpret=interpret,
-        out_specs=(pl.BlockSpec(memory_space=pl.ANY), VMEM),
-    )(rows, recv, back)
+    outs = [shape(1, ROWS, COLS), shape(OWNED, 8, 128)]
+    return call(finish_kernel, [SMEM, VMEM, VMEM], outs, interpret=interpret)(rows, recv, back)
 
 
 def owned_rows(tile_owner, index):
@@ -335,15 +325,17 @@
 
 def per_device(adjoint_source, conductivity, tile_owner):
     index = lax.axis_index("slab")
+    place = index.reshape(1)
     count = lax.axis_size("slab")
-    recv = lax.all_to_all(pack(jnp.concatenate([conductivity, adjoint_source], axis=0)), "layer", 0, 0, tiled=True)
-    up, down = halo(recv)
-    tile_owner, up = lax.optimization_barrier((tile_owner, up))
-    rows = owned_rows(tile_owner, index)
-    place = index.reshape(1)
-    low = lax.ppermute(up, "slab", [(i, (i + 1) % count) for i in range(count)])
-    high = lax.ppermute(down, "slab", [((i + 1) % count, i) for i in range(count)])
-    msg, ret = krylov(place, rows, recv, low, high)
+    both = jnp.concatenate([conductivity, adjoint_source], axis=0)
+    both, rows, tile_owner = lax.optimization_barrier((both, owned_rows(tile_owner, index), tile_owner))
+    recv = lax.all_to_all(pack(both), "layer", 0, 0, tiled=True)
+    first, second = halo(place, recv)
+    meet = [(i, i + 1) for i in range(0, count - 1, 2)]
+    part = [(i, i + 1) for i in range(1, count - 1, 2)]
+    first = lax.ppermute(first, "slab", meet + [(j, i) for i, j in meet])
+    second = lax.ppermute(second, "slab", part + [(j, i) for i, j in part])
+    msg, ret = krylov(place, recv, first, second)
     strips = lax.all_to_all(msg, "layer", 0, 0, tiled=True)
     outgoing = route(tile_owner, place, strips)
     received = lax.all_to_all(outgoing, "slab", 0, 0, tiled=True)

time: 110 us -> 109 us (level)
  blocking collectives: 48.3 us -> 92.9 us
  starting transfers between devices: 30.4 us -> 2.59 us
  waiting for transfers between devices: 20.8 us -> 4.45 us
  Pallas kernels: 7.44 us -> 5.5 us
    all_to_all x0 -> x1, blocking collectives: none -> 35.6 us  [per_device(): recv = lax.all_to_all(pack(both), 'layer', 0, 0, tiled=True)]
    all_to_all x1 -> x0, waiting for transfers between devices: 18.6 us -> none  [per_device(): lax.all_to_all(pack(jnp.concatenate([conductivity, adjoint_source], axis=...]
    all_to_all x1 -> x0, starting transfers between devices: 17.5 us -> none  [per_device(): lax.all_to_all(pack(jnp.concatenate([conductivity, adjoint_source], axis=...]
    ppermute x2, starting transfers between devices: 12.8 us -> 2.59 us  [the longest x1 1.92 us: per_device(): first = lax.ppermute(first, 'slab', meet + [(j, i) for i, j in meet])]
    all_to_all x1, blocking collectives: 20.5 us -> 29.8 us  [per_device(): received = lax.all_to_all(outgoing, 'slab', 0, 0, tiled=True)]
    ppermute x2, waiting for transfers between devices: 2.18 us -> 4.45 us  [the longest x1 4.44 us: per_device(): first = lax.ppermute(first, 'slab', meet + [(j, i) for i, j in meet])]
    pallas_call x3, Pallas kernels: 5.62 us -> 4.5 us  [the longest x1 2.91 us: krylov(): call(krylov_kernel, [SMEM] + [VMEM] * 3, [shape(LAYERS, 8, 128), shape(LA...]
  transfers between devices with their start and end apart: 3 -> 2, of which waited for: 3 -> 1; matrix products, arithmetic and copies ran while one was open for 0% -> 0% of each run, Pallas kernels for 0% -> 0%
where the time goes in v5:
time: 109 us; the launch traced here: 108 us
  blocking collectives  92.9 us (85%)
  Pallas kernels  5.5 us (5%)
  waiting for transfers between devices  4.45 us (4%)
  starting transfers between devices  2.59 us (2%)
  other arithmetic  1.5 us (1%)
    all_to_all x1, blocking collectives, per_device(): recv = lax.all_to_all(pack(both), 'layer', 0, 0, tiled=True)  35.6 us
    all_to_all x1, blocking collectives, per_device(): received = lax.all_to_all(outgoing, 'slab', 0, 0, tiled=True)  29.8 us
    all_to_all x1, blocking collectives, per_device(): back = lax.all_to_all(combine(received, ret), 'layer', 0, 0, tiled=True)  16.4 us
    all_to_all x1, blocking collectives, per_device(): strips = lax.all_to_all(msg, 'layer', 0, 0, tiled=True)  11.1 us
    ppermute x1, waiting for transfers between devices, per_device(): first = lax.ppermute(first, 'slab', meet + [(j, i) for i, j in meet])  4.44 us
    pallas_call x1, Pallas kernels, krylov(): call(krylov_kernel, [SMEM] + [VMEM] * 3, [shape(LAYERS, 8, 128), shape(LA...  2.91 us
  transfers between devices with their start and end apart: 2, of which 1 were waited for; matrix products, arithmetic and copies ran while one was open for 0% of the time, Pallas kernels for 0%

profile of v5, /device:TPU:1, one launch (start us, length us, event | category | flops | bytes accessed | tf_op | source)
XLA Modules:
  0.0 108.3 jit_solution(4643999412187381870)
XLA Ops:
  0.6 0.0 copy-start
  0.6 0.7 copy-done
  1.3 0.1 compare_reduce_fusion
  1.4 0.2 reduce-window.8
  1.6 0.1 select_reduce_fusion.rows_ref
  1.8 1.1 pad_maximum_fusion.both_ref
  2.8 0.1 shard_map.50
  3.0 35.6 %all_to_all.20.recv_ref = f32[16,9,8,128]{3,2,1,0:T(8,128)S(1)} all-to-all(f32[16,9,8,128]{3,2,1,0:T(8,128)S(1)} %shard_map.50), channel_id=1, replica_groups=mesh['slab'=64,'layer'=16] {'layer'}, dimensions={0} | all-to-all | bytes 1179648 | tf_op jit(solution)/shard_map/all_to_all | solution.py:332
  38.6 0.1 shard_map.51
  38.7 1.9 %collective-permute-start = (f32[33,8,128]{2,1,0:T(8,128)S(1)}, f32[33,8,128]{2,1,0:T(8,128)S(1)}, u32[]{:S(2)}, u32[]{:S(2)}) collective-permute-start(f32[33,8,128]{2,1,0:T(8,128)S(1)} %get-tuple-element.12), channel_id=1, source_target_pairs={{0,16},{32,48},{64,80},{96,112},{128,144},{160,176},{192,208},{224... | collective-permute-start | bytes 405512 | tf_op jit(solution)/shard_map/ppermute | solution.py:336
  40.7 0.7 collective-permute-start.1
  41.3 4.4 %collective-permute-done.first_ref = f32[33,8,128]{2,1,0:T(8,128)S(1)} collective-permute-done((f32[33,8,128]{2,1,0:T(8,128)S(1)}, f32[33,8,128]{2,1,0:T(8,128)S(1)}, u32[]{:S(2)}, u32[]{:S(2)}) %collective-permute-start) | collective-permute-done | bytes 135200 | tf_op jit(solution)/shard_map/ppermute | solution.py:336
  45.8 0.0 collective-permute-done.1.second_ref
  45.8 2.9 %shard_map.52 = (f32[16,8,128]{2,1,0:T(8,128)S(1)}, f32[16,12,8,128]{3,2,1,0:T(8,128)S(1)}) custom-call(s32[1]{0:T(128)} %bitcast.2.index_ref, f32[16,9,8,128]{3,2,1,0:T(8,128)S(1)} %all_to_all.20.recv_ref, f32[33,8,128]{2,1,0:T(8,128)S(1)} %collective-permute-done.first_ref, f32[33,8,128]{2,1,0:T(8,128)S(1)} %collective-permute-done.1.second_ref), custom_call_target="tpu_custom_call" | custom-call | tf_op jit(solution)/shard_map/pallas_call | solution.py:296
  48.7 11.1 %all_to_all.21.recv_ref = f32[16,8,128]{2,1,0:T(8,128)S(1)} all-to-all(f32[16,8,128]{2,1,0:T(8,128)S(1)} %get-tuple-element.14), channel_id=1, replica_groups=mesh['slab'=64,'layer'=16] {'layer'}, dimensions={0} | all-to-all | bytes 131072 | tf_op jit(solution)/shard_map/all_to_all | solution.py:339
  59.8 0.6 shard_map.53
  60.5 29.8 %all_to_all.22.recv_ref = f32[64,4,128]{2,1,0:T(4,128)S(1)} all-to-all(f32[64,4,128]{2,1,0:T(4,128)S(1)} %shard_map.53), channel_id=1, replica_groups=mesh['slab'=64,'layer'=16] {'slab'}, dimensions={0} | all-to-all | bytes 262144 | tf_op jit(solution)/shard_map/all_to_all | solution.py:341
  90.3 0.2 shard_map.54
  90.5 16.4 %all_to_all.23.back_ref = f32[16,4,8,128]{3,2,1,0:T(8,128)S(1)} all-to-all(f32[16,4,8,128]{3,2,1,0:T(8,128)S(1)} %shard_map.54), channel_id=1, replica_groups=mesh['slab'=64,'layer'=16] {'layer'}, dimensions={0} | all-to-all | bytes 524288 | tf_op jit(solution)/shard_map/all_to_all | solution.py:342
  106.9 1.5 %shard_map.55 = (f32[1,16,4096]{2,1,0:T(8,128)}, f32[4,8,128]{2,1,0:T(8,128)}) custom-call(s32[4]{0:T(128)S(1)} %select_reduce_fusion.rows_ref, f32[64,4,128]{2,1,0:T(4,128)S(1)} %all_to_all.22.recv_ref, f32[16,4,8,128]{3,2,1,0:T(8,128)S(1)} %all_to_all.23.back_ref), custom_call_target="tpu_custom_call" | custom-call | tf_op jit(solution)/shard_map/pallas_call | solution.py:315
  (2 shorter events, 0.0 us)
Async XLA Ops:
  0.6 0.7 copy-start
  38.7 7.0 %collective-permute-start = (f32[33,8,128]{2,1,0:T(8,128)S(1)}, f32[33,8,128]{2,1,0:T(8,128)S(1)}, u32[]{:S(2)}, u32[]{:S(2)}) collective-permute-start(f32[33,8,128]{2,1,0:T(8,128)S(1)} %get-tuple-element.12), channel_id=1, source_target_pairs={{0,16},{32,48},{64,80},{96,112},{128,144},{160,176},{192,208},{224... | collective-permute-start | bytes 405512 | tf_op jit(solution)/shard_map/ppermute | solution.py:336
  40.7 5.1 %collective-permute-start.1 = (f32[33,8,128]{2,1,0:T(8,128)S(1)}, f32[33,8,128]{2,1,0:T(8,128)S(1)}, u32[]{:S(2)}, u32[]{:S(2)}) collective-permute-start(f32[33,8,128]{2,1,0:T(8,128)S(1)} %get-tuple-element.13), channel_id=1, source_target_pairs={{16,32},{48,64},{80,96},{112,128},{144,160},{176,192},{208,224},{2... | collective-permute-start | bytes 405512 | tf_op jit(solution)/shard_map/ppermute | solution.py:337

commit v6 on v5

--- a/solution.py
+++ b/solution.py
@@ -27,9 +27,10 @@
     return lax.broadcasted_iota(jnp.int32, (8, 128), 0)
 
 
-def pack_kernel(both_ref, out_ref):
+def pack_kernel(both_ref, owner_ref, out_ref, table_ref):
     lane = lanes()
     zero = jnp.zeros((8, 128), F32)
+    table_ref[...] = owner_ref[...]
     for j in range(LAYERS):
         edge = zero
         for q in range(2):
@@ -45,8 +46,8 @@
         out_ref[j, 8] = edge
 
 
-def halo_kernel(index_ref, recv_ref, first_ref, second_ref):
-    even = index_ref[0] % 2 == 0
+def halo_kernel(turn_ref, recv_ref, first_ref, second_ref):
+    even = turn_ref[0] % 2 == 0
 
     def put(n, up, down):
         first_ref[n] = jnp.where(even, up, down)
@@ -80,7 +81,7 @@
 
 
 def krylov_kernel(
-    index_ref, recv_ref, first_ref, second_ref, msg_ref, ret_ref, k_ref, v0_ref, v1_ref, v2_ref, inv_ref, cc_ref, cr_ref, cz_ref, square_ref
+    turn_ref, recv_ref, first_ref, second_ref, msg_ref, ret_ref, k_ref, v0_ref, v1_ref, v2_ref, inv_ref, cc_ref, cr_ref, cz_ref, square_ref
 ):
     lane = lanes()
     sub = sublanes()
@@ -92,7 +93,7 @@
     def spread(tile, place):
         return jnp.where(rim, pltpu.roll(tile, (252 - place) % 128, axis=1), 0.0)
 
-    even = index_ref[0] % 2 == 0
+    even = turn_ref[0] % 2 == 0
     upper = (sub < 4) == even
 
     def halves(n):
@@ -281,16 +282,17 @@
     )
 
 
-def pack(both, interpret=False):
-    return call(pack_kernel, [VMEM], [shape(LAYERS, 9, 8, 128)], interpret=interpret)(both)
-
-
-def halo(index, recv, interpret=False):
+def pack(both, owner, interpret=False):
+    outs = [shape(LAYERS, 9, 8, 128), jax.ShapeDtypeStruct(owner.shape, owner.dtype)]
+    return call(pack_kernel, [VMEM] * 2, outs, interpret=interpret)(both, owner)
+
+
+def halo(turn, recv, interpret=False):
     side = shape(2 * LAYERS + 1, 8, 128)
-    return call(halo_kernel, [SMEM, VMEM], [side, side], interpret=interpret)(index, recv)
-
-
-def krylov(index, recv, first, second, interpret=False):
+    return call(halo_kernel, [SMEM, VMEM], [side, side], interpret=interpret)(turn, recv)
+
+
+def krylov(turn, recv, first, second, interpret=False):
     field = pltpu.VMEM((LAYERS + 1, EXT_ROWS, EXT_COLS), F32)
     face = pltpu.VMEM((LAYERS, EXT_ROWS, EXT_COLS), F32)
     return call(
@@ -299,7 +301,7 @@
         [shape(LAYERS, 8, 128), shape(LAYERS, 12, 8, 128)],
         [field] * 4 + [face] * 4 + [pltpu.VMEM((128, 128), F32)],
         interpret=interpret,
-    )(index, recv, first, second)
+    )(turn, recv, first, second)
 
 
 def route(owner, index, recv, interpret=False):
@@ -323,21 +325,31 @@
     return jnp.sum(jnp.where(held[None, :] & (rank[None, :] == slot), row, 0), axis=1)
 
 
+def pairing(turn):
+    pairs = []
+    for layer in range(LAYERS):
+        for low in range((turn + layer) % 2, SLABS - 1, 2):
+            here, there = low * LAYERS + layer, (low + 1) * LAYERS + layer
+            pairs += [(here, there), (there, here)]
+    return pairs
+
+
 def per_device(adjoint_source, conductivity, tile_owner):
     index = lax.axis_index("slab")
     place = index.reshape(1)
-    count = lax.axis_size("slab")
+    turn = (index + lax.axis_index("layer")).reshape(1)
     both = jnp.concatenate([conductivity, adjoint_source], axis=0)
-    both, rows, tile_owner = lax.optimization_barrier((both, owned_rows(tile_owner, index), tile_owner))
-    recv = lax.all_to_all(pack(both), "layer", 0, 0, tiled=True)
-    first, second = halo(place, recv)
-    meet = [(i, i + 1) for i in range(0, count - 1, 2)]
-    part = [(i, i + 1) for i in range(1, count - 1, 2)]
-    first = lax.ppermute(first, "slab", meet + [(j, i) for i, j in meet])
-    second = lax.ppermute(second, "slab", part + [(j, i) for i, j in part])
-    msg, ret = krylov(place, recv, first, second)
+    packed, table = pack(both, tile_owner)
+    recv = lax.all_to_all(packed, "layer", 0, 0, tiled=True)
+    first, second = halo(turn, recv)
+    first, table = lax.optimization_barrier((first, table))
+    rows = owned_rows(table, index)
+    first = lax.ppermute(first, ("slab", "layer"), pairing(0))
+    second = lax.ppermute(second, ("slab", "layer"), pairing(1))
+    first, second, rows = lax.optimization_barrier((first, second, rows))
+    msg, ret = krylov(turn, recv, first, second)
     strips = lax.all_to_all(msg, "layer", 0, 0, tiled=True)
-    outgoing = route(tile_owner, place, strips)
+    outgoing = route(table, place, strips)
     received = lax.all_to_all(outgoing, "slab", 0, 0, tiled=True)
     back = lax.all_to_all(combine(received, ret), "layer", 0, 0, tiled=True)
     return finish(rows, received, back)

time: 109 us -> 108 us (level)
  blocking collectives: 92.9 us -> 56.6 us
  waiting for transfers between devices: 4.45 us -> 22.2 us
  starting transfers between devices: 2.59 us -> 20.1 us
    all_to_all x1 -> x0, blocking collectives: 35.6 us -> none  [per_device(): recv = lax.all_to_all(pack(both), 'layer', 0, 0, tiled=True)]
    all_to_all x0 -> x1, waiting for transfers between devices: none -> 18.6 us  [per_device(): recv = lax.all_to_all(packed, 'layer', 0, 0, tiled=True)]
    all_to_all x0 -> x1, starting transfers between devices: none -> 17.5 us  [per_device(): recv = lax.all_to_all(packed, 'layer', 0, 0, tiled=True)]
    all_to_all x1, blocking collectives: 29.8 us -> 27.9 us  [per_device(): received = lax.all_to_all(outgoing, 'slab', 0, 0, tiled=True)]
    all_to_all x1, blocking collectives: 11.1 us -> 12.4 us  [per_device(): strips = lax.all_to_all(msg, 'layer', 0, 0, tiled=True)]
  transfers between devices with their start and end apart: 2 -> 3, of which waited for: 1 -> 2; matrix products, arithmetic and copies ran while one was open for 0% -> 0% of each run, Pallas kernels for 0% -> 0%
where the time goes in v6:
time: 108 us; the launch traced here: 107 us
  blocking collectives  56.6 us (52%)
  waiting for transfers between devices  22.2 us (21%)
  starting transfers between devices  20.1 us (19%)
  Pallas kernels  6.32 us (6%)
  other arithmetic  1.5 us (1%)
    all_to_all x1, blocking collectives, per_device(): received = lax.all_to_all(outgoing, 'slab', 0, 0, tiled=True)  27.9 us
    all_to_all x1, waiting for transfers between devices, per_device(): recv = lax.all_to_all(packed, 'layer', 0, 0, tiled=True)  18.6 us
    all_to_all x1, starting transfers between devices, per_device(): recv = lax.all_to_all(packed, 'layer', 0, 0, tiled=True)  17.5 us
    all_to_all x1, blocking collectives, per_device(): back = lax.all_to_all(combine(received, ret), 'layer', 0, 0, tiled=True)  16.4 us
    all_to_all x1, blocking collectives, per_device(): strips = lax.all_to_all(msg, 'layer', 0, 0, tiled=True)  12.4 us
    ppermute x1, waiting for transfers between devices, per_device(): second = lax.ppermute(second, ('slab', 'layer'), pairing(1))  3.51 us
    pallas_call x1, Pallas kernels, krylov(): call(krylov_kernel, [SMEM] + [VMEM] * 3, [shape(LAYERS, 8, 128), shape(LA...  2.91 us
  transfers between devices with their start and end apart: 3, of which 2 were waited for; matrix products, arithmetic and copies ran while one was open for 0% of the time, Pallas kernels for 0%

profile of v6, /device:TPU:1, one launch (start us, length us, event | category | flops | bytes accessed | tf_op | source)
XLA Modules:
  0.0 107.4 jit_solution(3417071641709698337)
XLA Ops:
  0.6 0.0 copy-start
  0.6 1.1 pad_maximum_fusion.both_ref
  1.7 0.0 copy-done
  1.7 1.0 shard_map.50
  2.7 17.5 %all-to-all-start = ((f32[16,9,8,128]{3,2,1,0:T(8,128)}), f32[16,9,8,128]{3,2,1,0:T(8,128)S(1)}, u32[]{:S(2)}, u32[]{:S(2)}) async-start(f32[16,9,8,128]{3,2,1,0:T(8,128)} %get-tuple-element.13), calls=%async_computation | async-start | bytes 1179648 | tf_op jit(solution)/shard_map/all_to_all | solution.py:343
  20.2 18.6 %all-to-all-done.recv_ref = f32[16,9,8,128]{3,2,1,0:T(8,128)S(1)} async-done(((f32[16,9,8,128]{3,2,1,0:T(8,128)}), f32[16,9,8,128]{3,2,1,0:T(8,128)S(1)}, u32[]{:S(2)}, u32[]{:S(2)}) %all-to-all-start) | async-done | bytes 589856 | tf_op jit(solution)/shard_map/all_to_all | solution.py:343
  38.8 0.1 shard_map.51
  38.9 0.1 compare_reduce_fusion
  39.1 0.7 collective-permute-start
  39.7 1.9 %collective-permute-start.1 = (f32[33,8,128]{2,1,0:T(8,128)S(1)}, f32[33,8,128]{2,1,0:T(8,128)S(1)}, u32[]{:S(2)}, u32[]{:S(2)}) collective-permute-start(f32[33,8,128]{2,1,0:T(8,128)S(1)} %get-tuple-element.17), channel_id=1, source_target_pairs={{16,32},{32,16},{48,64},{64,48},{80,96},{96,80},{112,128},{128,112... | collective-permute-start | bytes 405512 | tf_op jit(solution)/shard_map/ppermute | solution.py:348
  41.7 0.2 reduce-window.8
  41.9 0.1 select_reduce_fusion.rows_ref
  42.0 0.0 collective-permute-done.first_ref
  42.0 3.5 %collective-permute-done.1.second_ref = f32[33,8,128]{2,1,0:T(8,128)S(1)} collective-permute-done((f32[33,8,128]{2,1,0:T(8,128)S(1)}, f32[33,8,128]{2,1,0:T(8,128)S(1)}, u32[]{:S(2)}, u32[]{:S(2)}) %collective-permute-start.1) | collective-permute-done | bytes 135200 | tf_op jit(solution)/shard_map/ppermute | solution.py:348
  45.5 2.9 %shard_map.52 = (f32[16,8,128]{2,1,0:T(8,128)S(1)}, f32[16,12,8,128]{3,2,1,0:T(8,128)S(1)}) custom-call(s32[1]{0:T(128)} %bitcast.turn_ref, f32[16,9,8,128]{3,2,1,0:T(8,128)S(1)} %all-to-all-done.recv_ref, f32[33,8,128]{2,1,0:T(8,128)S(1)} %collective-permute-done.first_ref, f32[33,8,128]{2,1,0:T(8,128)S(1)} %collective-permute-done.1.second_ref), custom_call_target="tpu_custom_call" | custom-call | tf_op jit(solution)/shard_map/pallas_call | solution.py:298
  48.4 12.4 %all_to_all.20.recv_ref = f32[16,8,128]{2,1,0:T(8,128)S(1)} all-to-all(f32[16,8,128]{2,1,0:T(8,128)S(1)} %get-tuple-element.22), channel_id=1, replica_groups=mesh['slab'=64,'layer'=16] {'layer'}, dimensions={0} | all-to-all | bytes 131072 | tf_op jit(solution)/shard_map/all_to_all | solution.py:351
  60.8 0.6 shard_map.53
  61.4 27.9 %all_to_all.21.recv_ref = f32[64,4,128]{2,1,0:T(4,128)S(1)} all-to-all(f32[64,4,128]{2,1,0:T(4,128)S(1)} %shard_map.53), channel_id=1, replica_groups=mesh['slab'=64,'layer'=16] {'slab'}, dimensions={0} | all-to-all | bytes 262144 | tf_op jit(solution)/shard_map/all_to_all | solution.py:353
  89.3 0.2 shard_map.54
  89.6 16.4 %all_to_all.22.back_ref = f32[16,4,8,128]{3,2,1,0:T(8,128)S(1)} all-to-all(f32[16,4,8,128]{3,2,1,0:T(8,128)S(1)} %shard_map.54), channel_id=1, replica_groups=mesh['slab'=64,'layer'=16] {'layer'}, dimensions={0} | all-to-all | bytes 524288 | tf_op jit(solution)/shard_map/all_to_all | solution.py:354
  105.9 1.5 %shard_map.55 = (f32[1,16,4096]{2,1,0:T(8,128)}, f32[4,8,128]{2,1,0:T(8,128)}) custom-call(s32[4]{0:T(128)S(1)} %select_reduce_fusion.rows_ref, f32[64,4,128]{2,1,0:T(4,128)S(1)} %all_to_all.21.recv_ref, f32[16,4,8,128]{3,2,1,0:T(8,128)S(1)} %all_to_all.22.back_ref), custom_call_target="tpu_custom_call" | custom-call | tf_op jit(solution)/shard_map/pallas_call | solution.py:317
  (2 shorter events, 0.0 us)
Async XLA Ops:
  0.6 1.1 %copy-start = (s32[8,32]{1,0:T(8,128)S(1)}, s32[8,32]{1,0:T(8,128)}, u32[]{:S(2)}) copy-start(s32[8,32]{1,0:T(8,128)} %owner_ref.1) | copy-start | bytes 3076
  2.7 36.2 %all-to-all-start = ((f32[16,9,8,128]{3,2,1,0:T(8,128)}), f32[16,9,8,128]{3,2,1,0:T(8,128)S(1)}, u32[]{:S(2)}, u32[]{:S(2)}) async-start(f32[16,9,8,128]{3,2,1,0:T(8,128)} %get-tuple-element.13), calls=%async_computation | async-start | bytes 1179648 | tf_op jit(solution)/shard_map/all_to_all | solution.py:343
  39.1 2.9 %collective-permute-start = (f32[33,8,128]{2,1,0:T(8,128)S(1)}, f32[33,8,128]{2,1,0:T(8,128)S(1)}, u32[]{:S(2)}, u32[]{:S(2)}) collective-permute-start(f32[33,8,128]{2,1,0:T(8,128)S(1)} %get-tuple-element.16), channel_id=1, source_target_pairs={{0,16},{16,0},{32,48},{48,32},{64,80},{80,64},{96,112},{112,96},{1... | collective-permute-start | bytes 405512 | tf_op jit(solution)/shard_map/ppermute | solution.py:347
  39.7 5.8 %collective-permute-start.1 = (f32[33,8,128]{2,1,0:T(8,128)S(1)}, f32[33,8,128]{2,1,0:T(8,128)S(1)}, u32[]{:S(2)}, u32[]{:S(2)}) collective-permute-start(f32[33,8,128]{2,1,0:T(8,128)S(1)} %get-tuple-element.17), channel_id=1, source_target_pairs={{16,32},{32,16},{48,64},{64,48},{80,96},{96,80},{112,128},{128,112... | collective-permute-start | bytes 405512 | tf_op jit(solution)/shard_map/ppermute | solution.py:348

commit v7 on v6

--- a/solution.py
+++ b/solution.py
@@ -325,27 +325,23 @@
     return jnp.sum(jnp.where(held[None, :] & (rank[None, :] == slot), row, 0), axis=1)
 
 
-def pairing(turn):
-    pairs = []
-    for layer in range(LAYERS):
-        for low in range((turn + layer) % 2, SLABS - 1, 2):
-            here, there = low * LAYERS + layer, (low + 1) * LAYERS + layer
-            pairs += [(here, there), (there, here)]
-    return pairs
+def pairing(first):
+    pairs = [(low, low + 1) for low in range(first, SLABS - 1, 2)]
+    return pairs + [(high, low) for low, high in pairs]
 
 
 def per_device(adjoint_source, conductivity, tile_owner):
     index = lax.axis_index("slab")
     place = index.reshape(1)
-    turn = (index + lax.axis_index("layer")).reshape(1)
+    turn = (index + 1).reshape(1)
     both = jnp.concatenate([conductivity, adjoint_source], axis=0)
     packed, table = pack(both, tile_owner)
     recv = lax.all_to_all(packed, "layer", 0, 0, tiled=True)
     first, second = halo(turn, recv)
     first, table = lax.optimization_barrier((first, table))
     rows = owned_rows(table, index)
-    first = lax.ppermute(first, ("slab", "layer"), pairing(0))
-    second = lax.ppermute(second, ("slab", "layer"), pairing(1))
+    first = lax.ppermute(first, "slab", pairing(1))
+    second = lax.ppermute(second, "slab", pairing(0))
     first, second, rows = lax.optimization_barrier((first, second, rows))
     msg, ret = krylov(turn, recv, first, second)
     strips = lax.all_to_all(msg, "layer", 0, 0, tiled=True)

time: 108 us -> 107 us (level)
  blocking collectives: 56.6 us -> 54.8 us
    all_to_all x1, blocking collectives: 27.9 us -> 26.7 us  [per_device(): received = lax.all_to_all(outgoing, 'slab', 0, 0, tiled=True)]
where the time goes in v7:
time: 107 us; the launch traced here: 106 us
  blocking collectives  54.8 us (51%)
  waiting for transfers between devices  22.8 us (21%)
  starting transfers between devices  20.1 us (19%)
  Pallas kernels  6.32 us (6%)
  other arithmetic  1.5 us (1%)
    all_to_all x1, blocking collectives, per_device(): received = lax.all_to_all(outgoing, 'slab', 0, 0, tiled=True)  26.7 us
    all_to_all x1, waiting for transfers between devices, per_device(): recv = lax.all_to_all(packed, 'layer', 0, 0, tiled=True)  18.6 us
    all_to_all x1, starting transfers between devices, per_device(): recv = lax.all_to_all(packed, 'layer', 0, 0, tiled=True)  17.5 us
    all_to_all x1, blocking collectives, per_device(): back = lax.all_to_all(combine(received, ret), 'layer', 0, 0, tiled=True)  16.4 us
    all_to_all x1, blocking collectives, per_device(): strips = lax.all_to_all(msg, 'layer', 0, 0, tiled=True)  11.7 us
    ppermute x1, waiting for transfers between devices, per_device(): second = lax.ppermute(second, 'slab', pairing(0))  4.14 us
    pallas_call x1, Pallas kernels, krylov(): call(krylov_kernel, [SMEM] + [VMEM] * 3, [shape(LAYERS, 8, 128), shape(LA...  2.91 us
  transfers between devices with their start and end apart: 3, of which 2 were waited for; matrix products, arithmetic and copies ran while one was open for 0% of the time, Pallas kernels for 0%

profile of v7, /device:TPU:1, one launch (start us, length us, event | category | flops | bytes accessed | tf_op | source)
XLA Modules:
  0.0 106.2 jit_solution(2415781752866832645)
XLA Ops:
  0.6 0.0 copy-start
  0.6 1.1 %pad_maximum_fusion.both_ref = f32[2,16,4096]{2,1,0:T(8,128)S(1)} fusion(f32[1,16,4096]{2,1,0:T(8,128)} %param.3, f32[1,16,4096]{2,1,0:T(8,128)} %param.4), kind=kLoop, calls=%fused_computation | loop fusion | flops 131072 | bytes 1048576 | tf_op jit(solution)/shard_map/concatenate | solution.py:337
  1.7 0.0 copy-done
  1.7 1.0 shard_map.50
  2.7 17.5 %all-to-all-start = ((f32[16,9,8,128]{3,2,1,0:T(8,128)}), f32[16,9,8,128]{3,2,1,0:T(8,128)S(1)}, u32[]{:S(2)}, u32[]{:S(2)}) async-start(f32[16,9,8,128]{3,2,1,0:T(8,128)} %get-tuple-element.13), calls=%async_computation | async-start | bytes 1179648 | tf_op jit(solution)/shard_map/all_to_all | solution.py:339
  20.2 18.6 %all-to-all-done.recv_ref = f32[16,9,8,128]{3,2,1,0:T(8,128)S(1)} async-done(((f32[16,9,8,128]{3,2,1,0:T(8,128)}), f32[16,9,8,128]{3,2,1,0:T(8,128)S(1)}, u32[]{:S(2)}, u32[]{:S(2)}) %all-to-all-start) | async-done | bytes 589856 | tf_op jit(solution)/shard_map/all_to_all | solution.py:339
  38.8 0.1 shard_map.51
  38.9 0.1 compare_reduce_fusion
  39.1 0.7 collective-permute-start
  39.7 1.9 %collective-permute-start.1 = (f32[33,8,128]{2,1,0:T(8,128)S(1)}, f32[33,8,128]{2,1,0:T(8,128)S(1)}, u32[]{:S(2)}, u32[]{:S(2)}) collective-permute-start(f32[33,8,128]{2,1,0:T(8,128)S(1)} %get-tuple-element.17), channel_id=1, source_target_pairs={{0,16},{32,48},{64,80},{96,112},{128,144},{160,176},{192,208},{224... | collective-permute-start | bytes 405512 | tf_op jit(solution)/shard_map/ppermute | solution.py:344
  41.7 0.2 reduce-window.8
  41.9 0.1 select_reduce_fusion.rows_ref
  42.0 0.0 collective-permute-done.first_ref
  42.0 4.1 %collective-permute-done.1.second_ref = f32[33,8,128]{2,1,0:T(8,128)S(1)} collective-permute-done((f32[33,8,128]{2,1,0:T(8,128)S(1)}, f32[33,8,128]{2,1,0:T(8,128)S(1)}, u32[]{:S(2)}, u32[]{:S(2)}) %collective-permute-start.1) | collective-permute-done | bytes 135200 | tf_op jit(solution)/shard_map/ppermute | solution.py:344
  46.1 2.9 %shard_map.52 = (f32[16,8,128]{2,1,0:T(8,128)S(1)}, f32[16,12,8,128]{3,2,1,0:T(8,128)S(1)}) custom-call(s32[1]{0:T(128)} %bitcast.turn_ref, f32[16,9,8,128]{3,2,1,0:T(8,128)S(1)} %all-to-all-done.recv_ref, f32[33,8,128]{2,1,0:T(8,128)S(1)} %collective-permute-done.first_ref, f32[33,8,128]{2,1,0:T(8,128)S(1)} %collective-permute-done.1.second_ref), custom_call_target="tpu_custom_call" | custom-call | tf_op jit(solution)/shard_map/pallas_call | solution.py:298
  49.0 11.7 %all_to_all.20.recv_ref = f32[16,8,128]{2,1,0:T(8,128)S(1)} all-to-all(f32[16,8,128]{2,1,0:T(8,128)S(1)} %get-tuple-element.22), channel_id=1, replica_groups=mesh['slab'=64,'layer'=16] {'layer'}, dimensions={0} | all-to-all | bytes 131072 | tf_op jit(solution)/shard_map/all_to_all | solution.py:347
  60.8 0.6 shard_map.53
  61.4 26.7 %all_to_all.21.recv_ref = f32[64,4,128]{2,1,0:T(4,128)S(1)} all-to-all(f32[64,4,128]{2,1,0:T(4,128)S(1)} %shard_map.53), channel_id=1, replica_groups=mesh['slab'=64,'layer'=16] {'slab'}, dimensions={0} | all-to-all | bytes 262144 | tf_op jit(solution)/shard_map/all_to_all | solution.py:349
  88.1 0.2 shard_map.54
  88.3 16.4 %all_to_all.22.back_ref = f32[16,4,8,128]{3,2,1,0:T(8,128)S(1)} all-to-all(f32[16,4,8,128]{3,2,1,0:T(8,128)S(1)} %shard_map.54), channel_id=1, replica_groups=mesh['slab'=64,'layer'=16] {'layer'}, dimensions={0} | all-to-all | bytes 524288 | tf_op jit(solution)/shard_map/all_to_all | solution.py:350
  104.7 1.5 %shard_map.55 = (f32[1,16,4096]{2,1,0:T(8,128)}, f32[4,8,128]{2,1,0:T(8,128)}) custom-call(s32[4]{0:T(128)S(1)} %select_reduce_fusion.rows_ref, f32[64,4,128]{2,1,0:T(4,128)S(1)} %all_to_all.21.recv_ref, f32[16,4,8,128]{3,2,1,0:T(8,128)S(1)} %all_to_all.22.back_ref), custom_call_target="tpu_custom_call" | custom-call | tf_op jit(solution)/shard_map/pallas_call | solution.py:317
  (2 shorter events, 0.0 us)
Async XLA Ops:
  0.6 1.1 %copy-start = (s32[8,32]{1,0:T(8,128)S(1)}, s32[8,32]{1,0:T(8,128)}, u32[]{:S(2)}) copy-start(s32[8,32]{1,0:T(8,128)} %owner_ref.1) | copy-start | bytes 3076
  2.7 36.2 %all-to-all-start = ((f32[16,9,8,128]{3,2,1,0:T(8,128)}), f32[16,9,8,128]{3,2,1,0:T(8,128)S(1)}, u32[]{:S(2)}, u32[]{:S(2)}) async-start(f32[16,9,8,128]{3,2,1,0:T(8,128)} %get-tuple-element.13), calls=%async_computation | async-start | bytes 1179648 | tf_op jit(solution)/shard_map/all_to_all | solution.py:339
  39.1 2.9 %collective-permute-start = (f32[33,8,128]{2,1,0:T(8,128)S(1)}, f32[33,8,128]{2,1,0:T(8,128)S(1)}, u32[]{:S(2)}, u32[]{:S(2)}) collective-permute-start(f32[33,8,128]{2,1,0:T(8,128)S(1)} %get-tuple-element.16), channel_id=1, source_target_pairs={{16,32},{48,64},{80,96},{112,128},{144,160},{176,192},{208,224},{2... | collective-permute-start | bytes 405512 | tf_op jit(solution)/shard_map/ppermute | solution.py:343
  39.7 6.4 %collective-permute-start.1 = (f32[33,8,128]{2,1,0:T(8,128)S(1)}, f32[33,8,128]{2,1,0:T(8,128)S(1)}, u32[]{:S(2)}, u32[]{:S(2)}) collective-permute-start(f32[33,8,128]{2,1,0:T(8,128)S(1)} %get-tuple-element.17), channel_id=1, source_target_pairs={{0,16},{32,48},{64,80},{96,112},{128,144},{160,176},{192,208},{224... | collective-permute-start | bytes 405512 | tf_op jit(solution)/shard_map/ppermute | solution.py:344

commit v8 on v7

--- a/solution.py
+++ b/solution.py
@@ -16,6 +16,7 @@
 OWNED = 4
 EXT_ROWS = 24
 EXT_COLS = 384
+SCALE = 2.0**-6
 VMEM_LIMIT = 48 * 1024 * 1024
 
 
@@ -132,7 +133,7 @@
         for g in range(2):
             for t in range(2):
                 ret_ref[l, 2 * g + t] = mine[8 * g : 8 * g + 8, 128 * t : 128 * t + 128]
-        return cz, s0 + folded(mine * own(twice)), m0 + mine
+        return cz, s0 + folded(mine * (own(twice) * SCALE)), m0 + mine
 
     none = jnp.zeros((8, 128), F32)
     no_map = jnp.zeros((ROWS, WIDTH), F32)
@@ -156,7 +157,7 @@
             for g in range(2):
                 for t in range(2):
                     ret_ref[l, 4 * slot + 2 * g + t] = mine[8 * g : 8 * g + 8, 128 * t : 128 * t + 128]
-            got = own(result)
+            got = own(result) * SCALE
             return fz, odd + folded(own(v) * got), even + folded(mine * got), total + mine
 
         start = (-(k_ref[0] * v_ref[0]), none, none, no_map)
@@ -168,9 +169,9 @@
     def last(l, carry):
         fz_before, odd = carry
         v, result, fz = image(l, v2_ref, fz_before)
-        return fz, odd + folded(own(v) * own(result))
-
-    _, s5 = lax.fori_loop(0, LAYERS, last, (-(k_ref[0] * v2_ref[0]), none), unroll=8)
+        return fz, odd + folded(own(v) * (own(result) * SCALE))
+
+    _, s5 = lax.fori_loop(0, LAYERS, last, (-(k_ref[0] * v2_ref[0]), none), unroll=16)
 
     sums = none
     for n, part in enumerate((s0, s1, s2, s3, s4, s5)):
@@ -210,7 +211,8 @@
 
 
 def weights(s):
-    s0, s1, s2, s3, s4, s5 = s
+    level = jnp.where(s[0] > 2.0**60, 2.0**-60, jnp.where(s[0] < 2.0**-60, 2.0**60, 1.0))
+    s0, s1, s2, s3, s4, s5 = [value * level for value in s]
     a0 = s0 / s1
     z1 = -a0
     n1 = s0 + z1 * (2.0 * s1 + z1 * s2)

time: 107 us -> 106 us (level)
  no operation moved by 1% of the time
where the time goes in v8:
time: 106 us
  blocking collectives  54.8 us (52%)
  waiting for transfers between devices  22.8 us (22%)
  starting transfers between devices  20.1 us (19%)
  Pallas kernels  6.2 us (6%)
  other arithmetic  1.5 us (1%)
    all_to_all x1, blocking collectives, per_device(): received = lax.all_to_all(outgoing, 'slab', 0, 0, tiled=True)  26.7 us
    all_to_all x1, waiting for transfers between devices, per_device(): recv = lax.all_to_all(packed, 'layer', 0, 0, tiled=True)  18.6 us
    all_to_all x1, starting transfers between devices, per_device(): recv = lax.all_to_all(packed, 'layer', 0, 0, tiled=True)  17.5 us
    all_to_all x1, blocking collectives, per_device(): back = lax.all_to_all(combine(received, ret), 'layer', 0, 0, tiled=True)  16.4 us
    all_to_all x1, blocking collectives, per_device(): strips = lax.all_to_all(msg, 'layer', 0, 0, tiled=True)  11.7 us
    ppermute x1, waiting for transfers between devices, per_device(): second = lax.ppermute(second, 'slab', pairing(0))  4.14 us
    pallas_call x1, Pallas kernels, krylov(): call(krylov_kernel, [SMEM] + [VMEM] * 3, [shape(LAYERS, 8, 128), shape(LA...  2.79 us
  transfers between devices with their start and end apart: 3, of which 2 were waited for; matrix products, arithmetic and copies ran while one was open for 0% of the time, Pallas kernels for 0%

profile of v8, /device:TPU:1, one launch (start us, length us, event | category | flops | bytes accessed | tf_op | source)
XLA Modules:
  0.0 106.1 jit_solution(14836204926971016580)
XLA Ops:
  0.6 0.0 copy-start
  0.6 1.1 %pad_maximum_fusion.both_ref = f32[2,16,4096]{2,1,0:T(8,128)S(1)} fusion(f32[1,16,4096]{2,1,0:T(8,128)} %param.3, f32[1,16,4096]{2,1,0:T(8,128)} %param.4), kind=kLoop, calls=%fused_computation | loop fusion | flops 131072 | bytes 1048576 | tf_op jit(solution)/shard_map/concatenate | solution.py:339
  1.7 0.0 copy-done
  1.7 1.0 shard_map.50
  2.7 17.5 %all-to-all-start = ((f32[16,9,8,128]{3,2,1,0:T(8,128)}), f32[16,9,8,128]{3,2,1,0:T(8,128)S(1)}, u32[]{:S(2)}, u32[]{:S(2)}) async-start(f32[16,9,8,128]{3,2,1,0:T(8,128)} %get-tuple-element.13), calls=%async_computation | async-start | bytes 1179648 | tf_op jit(solution)/shard_map/all_to_all | solution.py:341
  20.2 18.6 %all-to-all-done.recv_ref = f32[16,9,8,128]{3,2,1,0:T(8,128)S(1)} async-done(((f32[16,9,8,128]{3,2,1,0:T(8,128)}), f32[16,9,8,128]{3,2,1,0:T(8,128)S(1)}, u32[]{:S(2)}, u32[]{:S(2)}) %all-to-all-start) | async-done | bytes 589856 | tf_op jit(solution)/shard_map/all_to_all | solution.py:341
  38.8 0.1 shard_map.51
  38.9 0.1 compare_reduce_fusion
  39.1 0.7 collective-permute-start
  39.7 1.9 %collective-permute-start.1 = (f32[33,8,128]{2,1,0:T(8,128)S(1)}, f32[33,8,128]{2,1,0:T(8,128)S(1)}, u32[]{:S(2)}, u32[]{:S(2)}) collective-permute-start(f32[33,8,128]{2,1,0:T(8,128)S(1)} %get-tuple-element.17), channel_id=1, source_target_pairs={{0,16},{32,48},{64,80},{96,112},{128,144},{160,176},{192,208},{224... | collective-permute-start | bytes 405512 | tf_op jit(solution)/shard_map/ppermute | solution.py:346
  41.7 0.2 reduce-window.8
  41.9 0.1 select_reduce_fusion.rows_ref
  42.0 0.0 collective-permute-done.first_ref
  42.0 4.1 %collective-permute-done.1.second_ref = f32[33,8,128]{2,1,0:T(8,128)S(1)} collective-permute-done((f32[33,8,128]{2,1,0:T(8,128)S(1)}, f32[33,8,128]{2,1,0:T(8,128)S(1)}, u32[]{:S(2)}, u32[]{:S(2)}) %collective-permute-start.1) | collective-permute-done | bytes 135200 | tf_op jit(solution)/shard_map/ppermute | solution.py:346
  46.1 2.8 %shard_map.52 = (f32[16,8,128]{2,1,0:T(8,128)S(1)}, f32[16,12,8,128]{3,2,1,0:T(8,128)S(1)}) custom-call(s32[1]{0:T(128)} %bitcast.turn_ref, f32[16,9,8,128]{3,2,1,0:T(8,128)S(1)} %all-to-all-done.recv_ref, f32[33,8,128]{2,1,0:T(8,128)S(1)} %collective-permute-done.first_ref, f32[33,8,128]{2,1,0:T(8,128)S(1)} %collective-permute-done.1.second_ref), custom_call_target="tpu_custom_call" | custom-call | tf_op jit(solution)/shard_map/pallas_call | solution.py:300
  48.9 11.7 %all_to_all.20.recv_ref = f32[16,8,128]{2,1,0:T(8,128)S(1)} all-to-all(f32[16,8,128]{2,1,0:T(8,128)S(1)} %get-tuple-element.22), channel_id=1, replica_groups=mesh['slab'=64,'layer'=16] {'layer'}, dimensions={0} | all-to-all | bytes 131072 | tf_op jit(solution)/shard_map/all_to_all | solution.py:349
  60.7 0.6 shard_map.53
  61.3 26.7 %all_to_all.21.recv_ref = f32[64,4,128]{2,1,0:T(4,128)S(1)} all-to-all(f32[64,4,128]{2,1,0:T(4,128)S(1)} %shard_map.53), channel_id=1, replica_groups=mesh['slab'=64,'layer'=16] {'slab'}, dimensions={0} | all-to-all | bytes 262144 | tf_op jit(solution)/shard_map/all_to_all | solution.py:351
  88.0 0.2 shard_map.54
  88.2 16.4 %all_to_all.22.back_ref = f32[16,4,8,128]{3,2,1,0:T(8,128)S(1)} all-to-all(f32[16,4,8,128]{3,2,1,0:T(8,128)S(1)} %shard_map.54), channel_id=1, replica_groups=mesh['slab'=64,'layer'=16] {'layer'}, dimensions={0} | all-to-all | bytes 524288 | tf_op jit(solution)/shard_map/all_to_all | solution.py:352
  104.6 1.5 %shard_map.55 = (f32[1,16,4096]{2,1,0:T(8,128)}, f32[4,8,128]{2,1,0:T(8,128)}) custom-call(s32[4]{0:T(128)S(1)} %select_reduce_fusion.rows_ref, f32[64,4,128]{2,1,0:T(4,128)S(1)} %all_to_all.21.recv_ref, f32[16,4,8,128]{3,2,1,0:T(8,128)S(1)} %all_to_all.22.back_ref), custom_call_target="tpu_custom_call" | custom-call | tf_op jit(solution)/shard_map/pallas_call | solution.py:319
  (2 shorter events, 0.0 us)
Async XLA Ops:
  0.6 1.1 %copy-start = (s32[8,32]{1,0:T(8,128)S(1)}, s32[8,32]{1,0:T(8,128)}, u32[]{:S(2)}) copy-start(s32[8,32]{1,0:T(8,128)} %owner_ref.1) | copy-start | bytes 3076
  2.7 36.2 %all-to-all-start = ((f32[16,9,8,128]{3,2,1,0:T(8,128)}), f32[16,9,8,128]{3,2,1,0:T(8,128)S(1)}, u32[]{:S(2)}, u32[]{:S(2)}) async-start(f32[16,9,8,128]{3,2,1,0:T(8,128)} %get-tuple-element.13), calls=%async_computation | async-start | bytes 1179648 | tf_op jit(solution)/shard_map/all_to_all | solution.py:341
  39.1 2.9 %collective-permute-start = (f32[33,8,128]{2,1,0:T(8,128)S(1)}, f32[33,8,128]{2,1,0:T(8,128)S(1)}, u32[]{:S(2)}, u32[]{:S(2)}) collective-permute-start(f32[33,8,128]{2,1,0:T(8,128)S(1)} %get-tuple-element.16), channel_id=1, source_target_pairs={{16,32},{48,64},{80,96},{112,128},{144,160},{176,192},{208,224},{2... | collective-permute-start | bytes 405512 | tf_op jit(solution)/shard_map/ppermute | solution.py:345
  39.7 6.4 %collective-permute-start.1 = (f32[33,8,128]{2,1,0:T(8,128)S(1)}, f32[33,8,128]{2,1,0:T(8,128)S(1)}, u32[]{:S(2)}, u32[]{:S(2)}) collective-permute-start(f32[33,8,128]{2,1,0:T(8,128)S(1)} %get-tuple-element.17), channel_id=1, source_target_pairs={{0,16},{32,48},{64,80},{96,112},{128,144},{160,176},{192,208},{224... | collective-permute-start | bytes 405512 | tf_op jit(solution)/shard_map/ppermute | solution.py:346

commit v9 on v8

--- a/solution.py
+++ b/solution.py
@@ -81,18 +81,43 @@
     return (value[:8, :128] + value[8:, :128]) + (value[:8, 128:] + value[8:, 128:])
 
 
+def spread(tile, place):
+    lane = lanes()
+    return jnp.where((lane < 4) | (lane >= 124), pltpu.roll(tile, (252 - place) % 128, axis=1), 0.0)
+
+
+def stage_kernel(recv_ref, k_ref, s_ref, cc_ref, cz_ref, diag_ref):
+    k_ref[LAYERS] = jnp.zeros((ROWS, EXT_COLS), F32)
+    for l in range(LAYERS):
+        edge = recv_ref[l, 8]
+        for q, ref in enumerate((k_ref, s_ref)):
+            for g in range(2):
+                rows = slice(8 * g, 8 * g + 8)
+                for t in range(2):
+                    ref[l, rows, 128 * t : 128 * t + 128] = recv_ref[l, 4 * q + 2 * g + t]
+                ref[l, rows, 256:384] = spread(edge, 8 * (2 * g + q))
+
+    def body(l, cz_before):
+        k = k_ref[l]
+        cc = k + pltpu.roll(k, EXT_COLS - 1, axis=1)
+        cz = k + k_ref[l + 1]
+        cc_ref[l] = cc
+        cz_ref[l] = cz
+        diag_ref[l] = (cc + pltpu.roll(cc, 1, axis=1)) + (cz + cz_before)
+        return cz
+
+    lax.fori_loop(0, LAYERS, body, k_ref[0], unroll=8)
+
+
 def krylov_kernel(
-    turn_ref, recv_ref, first_ref, second_ref, msg_ref, ret_ref, k_ref, v0_ref, v1_ref, v2_ref, inv_ref, cc_ref, cr_ref, cz_ref, square_ref
+    turn_ref, first_ref, second_ref, own_k_ref, own_s_ref, own_cc_ref, own_cz_ref, own_diag_ref, msg_ref, ret_ref,
+    k_ref, v0_ref, v1_ref, v2_ref, inv_ref, cc_ref, cr_ref, cz_ref, square_ref
 ):
-    lane = lanes()
     sub = sublanes()
-    rim = (lane < 4) | (lane >= 124)
     blank = jnp.zeros((EXT_ROWS, EXT_COLS), F32)
-    for ref in (k_ref, v0_ref, v1_ref, v2_ref):
+    k_ref[LAYERS] = blank[ROWS:]
+    for ref in (v0_ref, v1_ref, v2_ref):
         ref[LAYERS] = blank
-
-    def spread(tile, place):
-        return jnp.where(rim, pltpu.roll(tile, (252 - place) % 128, axis=1), 0.0)
 
     even = turn_ref[0] % 2 == 0
     upper = (sub < 4) == even
@@ -103,30 +128,31 @@
 
     halo_edges = halves(32)
     for l in range(LAYERS):
-        edge = recv_ref[l, 8]
-        for q, ref in enumerate((k_ref, v0_ref)):
-            for g in range(2):
-                for t in range(2):
-                    ref[l, 8 * g : 8 * g + 8, 128 * t : 128 * t + 128] = recv_ref[l, 4 * q + 2 * g + t]
-                ref[l, 8 * g : 8 * g + 8, 256:384] = spread(edge, 8 * (2 * g + q))
-            ref[l, 16:24, 256:384] = spread(halo_edges[l // 8], 16 * (l % 8) + 8 * q)
+        place = 16 * (l % 8)
+        k_ref[l, :, 256:384] = spread(halo_edges[l // 8], place)
+        v0_ref[l, 16:24, 256:384] = spread(halo_edges[l // 8], place + 8)
         for t in range(2):
             cols = slice(128 * t, 128 * t + 128)
-            k_ref[l, 16:24, cols], v0_ref[l, 16:24, cols] = halves(2 * l + t)
+            k_ref[l, :, cols], v0_ref[l, 16:24, cols] = halves(2 * l + t)
+
+    def joined(own_ref, rim_ref, l):
+        return jnp.concatenate([own_ref[l], rim_ref[l]], axis=0)
 
     def setup(l, carry):
         cz_before, s0, m0 = carry
-        k = k_ref[l]
-        cc = k + pltpu.roll(k, EXT_COLS - 1, axis=1)
+        rim = k_ref[l]
+        cc = rim + pltpu.roll(rim, EXT_COLS - 1, axis=1)
+        cz = rim + k_ref[l + 1]
+        cc_ref[l] = cc
+        cz_ref[l] = cz
+        diag = (cc + pltpu.roll(cc, 1, axis=1)) + (cz + cz_before)
+        k = joined(own_k_ref, k_ref, l)
         cr = k + pltpu.roll(k, EXT_ROWS - 1, axis=0)
-        cz = k + k_ref[l + 1]
-        diag = (cc + pltpu.roll(cc, 1, axis=1)) + (cr + pltpu.roll(cr, 1, axis=0)) + (cz + cz_before)
+        cr_ref[l] = cr
+        diag = jnp.concatenate([own_diag_ref[l], diag], axis=0) + (cr + pltpu.roll(cr, 1, axis=0))
         inv = jnp.where(k > 0.0, 1.0 / diag, 0.0)
-        twice = v0_ref[l] * 2.0
+        twice = jnp.concatenate([own_s_ref[l], v0_ref[l, 16:24, :]], axis=0) * 2.0
         v0 = twice * inv
-        cc_ref[l] = cc
-        cr_ref[l] = cr
-        cz_ref[l] = cz
         inv_ref[l] = inv
         v0_ref[l] = v0
         mine = own(v0)
@@ -141,9 +167,9 @@
 
     def image(l, v_ref, fz_before):
         v = v_ref[l]
-        fc = cc_ref[l] * (v - pltpu.roll(v, EXT_COLS - 1, axis=1))
+        fc = joined(own_cc_ref, cc_ref, l) * (v - pltpu.roll(v, EXT_COLS - 1, axis=1))
         fr = cr_ref[l] * (v - pltpu.roll(v, EXT_ROWS - 1, axis=0))
-        fz = cz_ref[l] * (v - v_ref[l + 1])
+        fz = joined(own_cz_ref, cz_ref, l) * (v - v_ref[l + 1])
         result = (fc - pltpu.roll(fc, 1, axis=1)) + (fr - pltpu.roll(fr, 1, axis=0)) + (fz - fz_before)
         return v, result, fz
 
@@ -160,7 +186,7 @@
             got = own(result) * SCALE
             return fz, odd + folded(own(v) * got), even + folded(mine * got), total + mine
 
-        start = (-(k_ref[0] * v_ref[0]), none, none, no_map)
+        start = (-(joined(own_k_ref, k_ref, 0) * v_ref[0]), none, none, no_map)
         return lax.fori_loop(0, LAYERS, body, start, unroll=8)[1:]
 
     s1, s2, m1 = step(v0_ref, v1_ref, 1)
@@ -171,7 +197,7 @@
         v, result, fz = image(l, v2_ref, fz_before)
         return fz, odd + folded(own(v) * (own(result) * SCALE))
 
-    _, s5 = lax.fori_loop(0, LAYERS, last, (-(k_ref[0] * v2_ref[0]), none), unroll=16)
+    _, s5 = lax.fori_loop(0, LAYERS, last, (-(joined(own_k_ref, k_ref, 0) * v2_ref[0]), none), unroll=16)
 
     sums = none
     for n, part in enumerate((s0, s1, s2, s3, s4, s5)):
@@ -294,16 +320,23 @@
     return call(halo_kernel, [SMEM, VMEM], [side, side], interpret=interpret)(turn, recv)
 
 
-def krylov(turn, recv, first, second, interpret=False):
+def stage(recv, interpret=False):
+    block = shape(LAYERS, ROWS, EXT_COLS)
+    outs = [shape(LAYERS + 1, ROWS, EXT_COLS)] + [block] * 4
+    return call(stage_kernel, [VMEM], outs, interpret=interpret)(recv)
+
+
+def krylov(turn, first, second, staged, interpret=False):
     field = pltpu.VMEM((LAYERS + 1, EXT_ROWS, EXT_COLS), F32)
     face = pltpu.VMEM((LAYERS, EXT_ROWS, EXT_COLS), F32)
+    rim = pltpu.VMEM((LAYERS + 1, EXT_ROWS - ROWS, EXT_COLS), F32)
     return call(
         krylov_kernel,
-        [SMEM] + [VMEM] * 3,
+        [SMEM] + [VMEM] * 7,
         [shape(LAYERS, 8, 128), shape(LAYERS, 12, 8, 128)],
-        [field] * 4 + [face] * 4 + [pltpu.VMEM((128, 128), F32)],
+        [rim, field, field, field, face, rim, face, rim, pltpu.VMEM((128, 128), F32)],
         interpret=interpret,
-    )(turn, recv, first, second)
+    )(turn, first, second, *staged)
 
 
 def route(owner, index, recv, interpret=False):
@@ -340,12 +373,13 @@
     packed, table = pack(both, tile_owner)
     recv = lax.all_to_all(packed, "layer", 0, 0, tiled=True)
     first, second = halo(turn, recv)
-    first, table = lax.optimization_barrier((first, table))
+    first, second, recv, table = lax.optimization_barrier((first, second, recv, table))
+    staged = stage(recv)
     rows = owned_rows(table, index)
     first = lax.ppermute(first, "slab", pairing(1))
     second = lax.ppermute(second, "slab", pairing(0))
     first, second, rows = lax.optimization_barrier((first, second, rows))
-    msg, ret = krylov(turn, recv, first, second)
+    msg, ret = krylov(turn, first, second, staged)
     strips = lax.all_to_all(msg, "layer", 0, 0, tiled=True)
     outgoing = route(table, place, strips)
     received = lax.all_to_all(outgoing, "slab", 0, 0, tiled=True)

time: 106 us -> 106 us (level)
    pallas_call x1 -> x2, Pallas kernels: 2.79 us -> 3.18 us  [the longest x1 2.63 us: krylov(): call(krylov_kernel, [SMEM] + [VMEM] * 7, [shape(LAYERS, 8, 128), shape(LA...]
  transfers between devices with their start and end apart: 3 -> 3, of which waited for: 2 -> 2; matrix products, arithmetic and copies ran while one was open for 0% -> 0% of each run, Pallas kernels for 0% -> 1%
where the time goes in v9:
time: 106 us
  blocking collectives  54.8 us (52%)
  waiting for transfers between devices  22.2 us (21%)
  starting transfers between devices  20.1 us (19%)
  Pallas kernels  6.6 us (6%)
  other arithmetic  1.5 us (1%)
    all_to_all x1, blocking collectives, per_device(): received = lax.all_to_all(outgoing, 'slab', 0, 0, tiled=True)  26.7 us
    all_to_all x1, waiting for transfers between devices, per_device(): recv = lax.all_to_all(packed, 'layer', 0, 0, tiled=True)  18.6 us
    all_to_all x1, starting transfers between devices, per_device(): recv = lax.all_to_all(packed, 'layer', 0, 0, tiled=True)  17.5 us
    all_to_all x1, blocking collectives, per_device(): back = lax.all_to_all(combine(received, ret), 'layer', 0, 0, tiled=True)  16.4 us
    all_to_all x1, blocking collectives, per_device(): strips = lax.all_to_all(msg, 'layer', 0, 0, tiled=True)  11.7 us
    ppermute x1, waiting for transfers between devices, per_device(): second = lax.ppermute(second, 'slab', pairing(0))  3.58 us
    pallas_call x1, Pallas kernels, krylov(): call(krylov_kernel, [SMEM] + [VMEM] * 7, [shape(LAYERS, 8, 128), shape(LA...  2.63 us
  transfers between devices with their start and end apart: 3, of which 2 were waited for; matrix products, arithmetic and copies ran while one was open for 0% of the time, Pallas kernels for 1%

profile of v9, /device:TPU:1, one launch (start us, length us, event | category | flops | bytes accessed | tf_op | source)
XLA Modules:
  0.0 105.9 jit_solution(3589747027725402503)
XLA Ops:
  0.6 0.0 copy-start
  0.6 1.1 %pad_maximum_fusion.both_ref = f32[2,16,4096]{2,1,0:T(8,128)S(1)} fusion(f32[1,16,4096]{2,1,0:T(8,128)} %param.3, f32[1,16,4096]{2,1,0:T(8,128)} %param.4), kind=kLoop, calls=%fused_computation | loop fusion | flops 131072 | bytes 1048576 | tf_op jit(solution)/shard_map/concatenate | solution.py:372
  1.7 0.0 copy-done
  1.7 1.0 shard_map.50
  2.7 17.5 %all-to-all-start = ((f32[16,9,8,128]{3,2,1,0:T(8,128)}), f32[16,9,8,128]{3,2,1,0:T(8,128)S(1)}, u32[]{:S(2)}, u32[]{:S(2)}) async-start(f32[16,9,8,128]{3,2,1,0:T(8,128)} %get-tuple-element.20), calls=%async_computation | async-start | bytes 1179648 | tf_op jit(solution)/shard_map/all_to_all | solution.py:374
  20.2 18.6 %all-to-all-done.recv_ref = f32[16,9,8,128]{3,2,1,0:T(8,128)S(1)} async-done(((f32[16,9,8,128]{3,2,1,0:T(8,128)}), f32[16,9,8,128]{3,2,1,0:T(8,128)S(1)}, u32[]{:S(2)}, u32[]{:S(2)}) %all-to-all-start) | async-done | bytes 589856 | tf_op jit(solution)/shard_map/all_to_all | solution.py:374
  38.9 0.1 shard_map.51
  39.0 0.1 compare_reduce_fusion
  39.1 0.7 collective-permute-start
  39.8 1.9 %collective-permute-start.1 = (f32[33,8,128]{2,1,0:T(8,128)S(1)}, f32[33,8,128]{2,1,0:T(8,128)S(1)}, u32[]{:S(2)}, u32[]{:S(2)}) collective-permute-start(f32[33,8,128]{2,1,0:T(8,128)S(1)} %get-tuple-element.25), channel_id=1, source_target_pairs={{0,16},{32,48},{64,80},{96,112},{128,144},{160,176},{192,208},{224... | collective-permute-start | bytes 405512 | tf_op jit(solution)/shard_map/ppermute | solution.py:380
  41.7 0.2 reduce-window.8
  41.9 0.6 shard_map.52
  42.4 0.1 select_reduce_fusion.rows_ref
  42.6 0.0 collective-permute-done.first_ref
  42.6 3.6 %collective-permute-done.1.second_ref = f32[33,8,128]{2,1,0:T(8,128)S(1)} collective-permute-done((f32[33,8,128]{2,1,0:T(8,128)S(1)}, f32[33,8,128]{2,1,0:T(8,128)S(1)}, u32[]{:S(2)}, u32[]{:S(2)}) %collective-permute-start.1) | collective-permute-done | bytes 135200 | tf_op jit(solution)/shard_map/ppermute | solution.py:380
  46.1 2.6 %shard_map.53 = (f32[16,8,128]{2,1,0:T(8,128)S(1)}, f32[16,12,8,128]{3,2,1,0:T(8,128)S(1)}) custom-call(s32[1]{0:T(128)} %bitcast.turn_ref, f32[33,8,128]{2,1,0:T(8,128)S(1)} %collective-permute-done.first_ref, f32[33,8,128]{2,1,0:T(8,128)S(1)} %collective-permute-done.1.second_ref, f32[17,16,384]{2,1,0:T(8,128)S(1)} %get-tuple-element.31.own_k_ref, ...), custom_call_target="tpu_custom_call" | custom-call | tf_op jit(solution)/shard_map/pallas_call | solution.py:333
  48.8 11.7 %all_to_all.20.recv_ref = f32[16,8,128]{2,1,0:T(8,128)S(1)} all-to-all(f32[16,8,128]{2,1,0:T(8,128)S(1)} %get-tuple-element.36), channel_id=1, replica_groups=mesh['slab'=64,'layer'=16] {'layer'}, dimensions={0} | all-to-all | bytes 131072 | tf_op jit(solution)/shard_map/all_to_all | solution.py:383
  60.5 0.6 shard_map.54
  61.1 26.7 %all_to_all.21.recv_ref = f32[64,4,128]{2,1,0:T(4,128)S(1)} all-to-all(f32[64,4,128]{2,1,0:T(4,128)S(1)} %shard_map.54), channel_id=1, replica_groups=mesh['slab'=64,'layer'=16] {'slab'}, dimensions={0} | all-to-all | bytes 262144 | tf_op jit(solution)/shard_map/all_to_all | solution.py:385
  87.8 0.2 shard_map.55
  88.0 16.4 %all_to_all.22.back_ref = f32[16,4,8,128]{3,2,1,0:T(8,128)S(1)} all-to-all(f32[16,4,8,128]{3,2,1,0:T(8,128)S(1)} %shard_map.55), channel_id=1, replica_groups=mesh['slab'=64,'layer'=16] {'layer'}, dimensions={0} | all-to-all | bytes 524288 | tf_op jit(solution)/shard_map/all_to_all | solution.py:386
  104.4 1.5 %shard_map.56 = (f32[1,16,4096]{2,1,0:T(8,128)}, f32[4,8,128]{2,1,0:T(8,128)}) custom-call(s32[4]{0:T(128)S(1)} %select_reduce_fusion.rows_ref, f32[64,4,128]{2,1,0:T(4,128)S(1)} %all_to_all.21.recv_ref, f32[16,4,8,128]{3,2,1,0:T(8,128)S(1)} %all_to_all.22.back_ref), custom_call_target="tpu_custom_call" | custom-call | tf_op jit(solution)/shard_map/pallas_call | solution.py:352
  (2 shorter events, 0.0 us)
Async XLA Ops:
  0.6 1.1 %copy-start = (s32[8,32]{1,0:T(8,128)S(1)}, s32[8,32]{1,0:T(8,128)}, u32[]{:S(2)}) copy-start(s32[8,32]{1,0:T(8,128)} %owner_ref.1) | copy-start | bytes 3076
  2.7 36.2 %all-to-all-start = ((f32[16,9,8,128]{3,2,1,0:T(8,128)}), f32[16,9,8,128]{3,2,1,0:T(8,128)S(1)}, u32[]{:S(2)}, u32[]{:S(2)}) async-start(f32[16,9,8,128]{3,2,1,0:T(8,128)} %get-tuple-element.20), calls=%async_computation | async-start | bytes 1179648 | tf_op jit(solution)/shard_map/all_to_all | solution.py:374
  39.1 3.5 %collective-permute-start = (f32[33,8,128]{2,1,0:T(8,128)S(1)}, f32[33,8,128]{2,1,0:T(8,128)S(1)}, u32[]{:S(2)}, u32[]{:S(2)}) collective-permute-start(f32[33,8,128]{2,1,0:T(8,128)S(1)} %get-tuple-element.24), channel_id=1, source_target_pairs={{16,32},{48,64},{80,96},{112,128},{144,160},{176,192},{208,224},{2... | collective-permute-start | bytes 405512 | tf_op jit(solution)/shard_map/ppermute | solution.py:379
  39.8 6.4 %collective-permute-start.1 = (f32[33,8,128]{2,1,0:T(8,128)S(1)}, f32[33,8,128]{2,1,0:T(8,128)S(1)}, u32[]{:S(2)}, u32[]{:S(2)}) collective-permute-start(f32[33,8,128]{2,1,0:T(8,128)S(1)} %get-tuple-element.25), channel_id=1, source_target_pairs={{0,16},{32,48},{64,80},{96,112},{128,144},{160,176},{192,208},{224... | collective-permute-start | bytes 405512 | tf_op jit(solution)/shard_map/ppermute | solution.py:380

commit v10 on v8

--- a/solution.py
+++ b/solution.py
@@ -28,7 +28,7 @@
     return lax.broadcasted_iota(jnp.int32, (8, 128), 0)
 
 
-def pack_kernel(both_ref, owner_ref, out_ref, table_ref):
+def pack_kernel(turn_ref, both_ref, owner_ref, out_ref, table_ref):
     lane = lanes()
     zero = jnp.zeros((8, 128), F32)
     table_ref[...] = owner_ref[...]
@@ -284,9 +284,9 @@
     )
 
 
-def pack(both, owner, interpret=False):
+def pack(turn, both, owner, interpret=False):
     outs = [shape(LAYERS, 9, 8, 128), jax.ShapeDtypeStruct(owner.shape, owner.dtype)]
-    return call(pack_kernel, [VMEM] * 2, outs, interpret=interpret)(both, owner)
+    return call(pack_kernel, [SMEM] + [VMEM] * 2, outs, interpret=interpret)(turn, both, owner)
 
 
 def halo(turn, recv, interpret=False):
@@ -337,7 +337,7 @@
     place = index.reshape(1)
     turn = (index + 1).reshape(1)
     both = jnp.concatenate([conductivity, adjoint_source], axis=0)
-    packed, table = pack(both, tile_owner)
+    packed, table = pack(turn, both, tile_owner)
     recv = lax.all_to_all(packed, "layer", 0, 0, tiled=True)
     first, second = halo(turn, recv)
     first, table = lax.optimization_barrier((first, table))

time: 106 us -> 106 us (level)
  blocking collectives: 54.8 us -> 90.5 us
  waiting for transfers between devices: 22.8 us -> 4.81 us
  starting transfers between devices: 20.1 us -> 2.59 us
    all_to_all x0 -> x1, blocking collectives: none -> 35.6 us  [per_device(): recv = lax.all_to_all(packed, 'layer', 0, 0, tiled=True)]
    all_to_all x1 -> x0, waiting for transfers between devices: 18.6 us -> none  [per_device(): recv = lax.all_to_all(packed, 'layer', 0, 0, tiled=True)]
    all_to_all x1 -> x0, starting transfers between devices: 17.5 us -> none  [per_device(): recv = lax.all_to_all(packed, 'layer', 0, 0, tiled=True)]
  transfers between devices with their start and end apart: 3 -> 2, of which waited for: 2 -> 1; matrix products, arithmetic and copies ran while one was open for 0% -> 0% of each run, Pallas kernels for 0% -> 0%
where the time goes in v10:
time: 106 us
  blocking collectives  90.5 us (85%)
  Pallas kernels  5.39 us (5%)
  waiting for transfers between devices  4.81 us (5%)
  starting transfers between devices  2.59 us (2%)
  other arithmetic  1.5 us (1%)
    all_to_all x1, blocking collectives, per_device(): recv = lax.all_to_all(packed, 'layer', 0, 0, tiled=True)  35.6 us
    all_to_all x1, blocking collectives, per_device(): received = lax.all_to_all(outgoing, 'slab', 0, 0, tiled=True)  27.4 us
    all_to_all x1, blocking collectives, per_device(): back = lax.all_to_all(combine(received, ret), 'layer', 0, 0, tiled=True)  16.4 us
    all_to_all x1, blocking collectives, per_device(): strips = lax.all_to_all(msg, 'layer', 0, 0, tiled=True)  11.1 us
    ppermute x1, waiting for transfers between devices, per_device(): second = lax.ppermute(second, 'slab', pairing(0))  4.81 us
    pallas_call x1, Pallas kernels, krylov(): call(krylov_kernel, [SMEM] + [VMEM] * 3, [shape(LAYERS, 8, 128), shape(LA...  2.79 us
  transfers between devices with their start and end apart: 2, of which 1 were waited for; matrix products, arithmetic and copies ran while one was open for 0% of the time, Pallas kernels for 0%

profile of v10, /device:TPU:1, one launch (start us, length us, event | category | flops | bytes accessed | tf_op | source)
XLA Modules:
  0.0 105.5 jit_solution(8289292933707360214)
XLA Ops:
  0.6 0.0 copy-start
  0.6 1.1 %pad_maximum_fusion.both_ref = f32[2,16,4096]{2,1,0:T(8,128)S(1)} fusion(f32[1,16,4096]{2,1,0:T(8,128)} %param.3, f32[1,16,4096]{2,1,0:T(8,128)} %param.4), kind=kLoop, calls=%fused_computation | loop fusion | flops 131072 | bytes 1048576 | tf_op jit(solution)/shard_map/concatenate | solution.py:339
  1.7 0.0 copy-done
  1.7 0.1 shard_map.50
  1.9 35.6 %all_to_all.20.recv_ref = f32[16,9,8,128]{3,2,1,0:T(8,128)S(1)} all-to-all(f32[16,9,8,128]{3,2,1,0:T(8,128)S(1)} %get-tuple-element.13), channel_id=1, replica_groups=mesh['slab'=64,'layer'=16] {'layer'}, dimensions={0} | all-to-all | bytes 1179648 | tf_op jit(solution)/shard_map/all_to_all | solution.py:341
  37.5 0.1 shard_map.51
  37.6 0.1 compare_reduce_fusion
  37.8 0.7 collective-permute-start
  38.4 1.9 %collective-permute-start.1 = (f32[33,8,128]{2,1,0:T(8,128)S(1)}, f32[33,8,128]{2,1,0:T(8,128)S(1)}, u32[]{:S(2)}, u32[]{:S(2)}) collective-permute-start(f32[33,8,128]{2,1,0:T(8,128)S(1)} %get-tuple-element.17), channel_id=1, source_target_pairs={{0,16},{32,48},{64,80},{96,112},{128,144},{160,176},{192,208},{224... | collective-permute-start | bytes 405512 | tf_op jit(solution)/shard_map/ppermute | solution.py:346
  40.4 0.2 reduce-window.8
  40.5 0.1 select_reduce_fusion.rows_ref
  40.7 0.0 collective-permute-done.first_ref
  40.7 4.8 %collective-permute-done.1.second_ref = f32[33,8,128]{2,1,0:T(8,128)S(1)} collective-permute-done((f32[33,8,128]{2,1,0:T(8,128)S(1)}, f32[33,8,128]{2,1,0:T(8,128)S(1)}, u32[]{:S(2)}, u32[]{:S(2)}) %collective-permute-start.1) | collective-permute-done | bytes 135200 | tf_op jit(solution)/shard_map/ppermute | solution.py:346
  45.5 2.8 %shard_map.52 = (f32[16,8,128]{2,1,0:T(8,128)S(1)}, f32[16,12,8,128]{3,2,1,0:T(8,128)S(1)}) custom-call(s32[1]{0:T(128)} %bitcast.turn_ref, f32[16,9,8,128]{3,2,1,0:T(8,128)S(1)} %all_to_all.20.recv_ref, f32[33,8,128]{2,1,0:T(8,128)S(1)} %collective-permute-done.first_ref, f32[33,8,128]{2,1,0:T(8,128)S(1)} %collective-permute-done.1.second_ref), custom_call_target="tpu_custom_call" | custom-call | tf_op jit(solution)/shard_map/pallas_call | solution.py:300
  48.3 11.1 %all_to_all.21.recv_ref = f32[16,8,128]{2,1,0:T(8,128)S(1)} all-to-all(f32[16,8,128]{2,1,0:T(8,128)S(1)} %get-tuple-element.22), channel_id=1, replica_groups=mesh['slab'=64,'layer'=16] {'layer'}, dimensions={0} | all-to-all | bytes 131072 | tf_op jit(solution)/shard_map/all_to_all | solution.py:349
  59.4 0.6 shard_map.53
  60.0 27.4 %all_to_all.22.recv_ref = f32[64,4,128]{2,1,0:T(4,128)S(1)} all-to-all(f32[64,4,128]{2,1,0:T(4,128)S(1)} %shard_map.53), channel_id=1, replica_groups=mesh['slab'=64,'layer'=16] {'slab'}, dimensions={0} | all-to-all | bytes 262144 | tf_op jit(solution)/shard_map/all_to_all | solution.py:351
  87.4 0.2 shard_map.54
  87.6 16.4 %all_to_all.23.back_ref = f32[16,4,8,128]{3,2,1,0:T(8,128)S(1)} all-to-all(f32[16,4,8,128]{3,2,1,0:T(8,128)S(1)} %shard_map.54), channel_id=1, replica_groups=mesh['slab'=64,'layer'=16] {'layer'}, dimensions={0} | all-to-all | bytes 524288 | tf_op jit(solution)/shard_map/all_to_all | solution.py:352
  104.0 1.5 %shard_map.55 = (f32[1,16,4096]{2,1,0:T(8,128)}, f32[4,8,128]{2,1,0:T(8,128)}) custom-call(s32[4]{0:T(128)S(1)} %select_reduce_fusion.rows_ref, f32[64,4,128]{2,1,0:T(4,128)S(1)} %all_to_all.22.recv_ref, f32[16,4,8,128]{3,2,1,0:T(8,128)S(1)} %all_to_all.23.back_ref), custom_call_target="tpu_custom_call" | custom-call | tf_op jit(solution)/shard_map/pallas_call | solution.py:319
  (2 shorter events, 0.0 us)
Async XLA Ops:
  0.6 1.1 %copy-start = (s32[8,32]{1,0:T(8,128)S(1)}, s32[8,32]{1,0:T(8,128)}, u32[]{:S(2)}) copy-start(s32[8,32]{1,0:T(8,128)} %owner_ref.1) | copy-start | bytes 3076
  37.8 2.9 %collective-permute-start = (f32[33,8,128]{2,1,0:T(8,128)S(1)}, f32[33,8,128]{2,1,0:T(8,128)S(1)}, u32[]{:S(2)}, u32[]{:S(2)}) collective-permute-start(f32[33,8,128]{2,1,0:T(8,128)S(1)} %get-tuple-element.16), channel_id=1, source_target_pairs={{16,32},{48,64},{80,96},{112,128},{144,160},{176,192},{208,224},{2... | collective-permute-start | bytes 405512 | tf_op jit(solution)/shard_map/ppermute | solution.py:345
  38.4 7.0 %collective-permute-start.1 = (f32[33,8,128]{2,1,0:T(8,128)S(1)}, f32[33,8,128]{2,1,0:T(8,128)S(1)}, u32[]{:S(2)}, u32[]{:S(2)}) collective-permute-start(f32[33,8,128]{2,1,0:T(8,128)S(1)} %get-tuple-element.17), channel_id=1, source_target_pairs={{0,16},{32,48},{64,80},{96,112},{128,144},{160,176},{192,208},{224... | collective-permute-start | bytes 405512 | tf_op jit(solution)/shard_map/ppermute | solution.py:346

commit v11 on v9

--- a/solution.py
+++ b/solution.py
@@ -28,7 +28,7 @@
     return lax.broadcasted_iota(jnp.int32, (8, 128), 0)
 
 
-def pack_kernel(both_ref, owner_ref, out_ref, table_ref):
+def pack_kernel(turn_ref, both_ref, owner_ref, out_ref, table_ref):
     lane = lanes()
     zero = jnp.zeros((8, 128), F32)
     table_ref[...] = owner_ref[...]
@@ -201,7 +201,8 @@
 
     sums = none
     for n, part in enumerate((s0, s1, s2, s3, s4, s5)):
-        sums = jnp.where(sub == n, jnp.sum(part), sums)
+        sums = jnp.where(sub == n, jnp.sum(part, axis=0, keepdims=True), sums)
+    sums = jnp.broadcast_to(jnp.sum(sums, axis=1, keepdims=True), (8, 128))
     first = lax.broadcasted_iota(jnp.int32, (ROWS, 128), 1) % 8 < 4
     for f, total in enumerate((m0, m1, m2)):
         left, right = total[:, :128], total[:, 128:]
@@ -310,9 +311,9 @@
     )
 
 
-def pack(both, owner, interpret=False):
+def pack(turn, both, owner, interpret=False):
     outs = [shape(LAYERS, 9, 8, 128), jax.ShapeDtypeStruct(owner.shape, owner.dtype)]
-    return call(pack_kernel, [VMEM] * 2, outs, interpret=interpret)(both, owner)
+    return call(pack_kernel, [SMEM] + [VMEM] * 2, outs, interpret=interpret)(turn, both, owner)
 
 
 def halo(turn, recv, interpret=False):
@@ -370,7 +371,7 @@
     place = index.reshape(1)
     turn = (index + 1).reshape(1)
     both = jnp.concatenate([conductivity, adjoint_source], axis=0)
-    packed, table = pack(both, tile_owner)
+    packed, table = pack(turn, both, tile_owner)
     recv = lax.all_to_all(packed, "layer", 0, 0, tiled=True)
     first, second = halo(turn, recv)
     first, second, recv, table = lax.optimization_barrier((first, second, recv, table))

time: 106 us -> 106 us (level)
  blocking collectives: 54.8 us -> 90.5 us
  waiting for transfers between devices: 22.2 us -> 4.25 us
  starting transfers between devices: 20.1 us -> 2.59 us
    all_to_all x0 -> x1, blocking collectives: none -> 35.6 us  [per_device(): recv = lax.all_to_all(packed, 'layer', 0, 0, tiled=True)]
    all_to_all x1 -> x0, waiting for transfers between devices: 18.6 us -> none  [per_device(): recv = lax.all_to_all(packed, 'layer', 0, 0, tiled=True)]
    all_to_all x1 -> x0, starting transfers between devices: 17.5 us -> none  [per_device(): recv = lax.all_to_all(packed, 'layer', 0, 0, tiled=True)]
  transfers between devices with their start and end apart: 3 -> 2, of which waited for: 2 -> 1; matrix products, arithmetic and copies ran while one was open for 0% -> 0% of each run, Pallas kernels for 1% -> 1%
where the time goes in v11:
time: 106 us; the launch traced here: 105 us
  blocking collectives  90.5 us (85%)
  Pallas kernels  5.76 us (5%)
  waiting for transfers between devices  4.25 us (4%)
  starting transfers between devices  2.59 us (2%)
  other arithmetic  1.5 us (1%)
    all_to_all x1, blocking collectives, per_device(): recv = lax.all_to_all(packed, 'layer', 0, 0, tiled=True)  35.6 us
    all_to_all x1, blocking collectives, per_device(): received = lax.all_to_all(outgoing, 'slab', 0, 0, tiled=True)  27.4 us
    all_to_all x1, blocking collectives, per_device(): back = lax.all_to_all(combine(received, ret), 'layer', 0, 0, tiled=True)  16.4 us
    all_to_all x1, blocking collectives, per_device(): strips = lax.all_to_all(msg, 'layer', 0, 0, tiled=True)  11.1 us
    ppermute x1, waiting for transfers between devices, per_device(): second = lax.ppermute(second, 'slab', pairing(0))  4.24 us
    pallas_call x1, Pallas kernels, krylov(): call(krylov_kernel, [SMEM] + [VMEM] * 7, [shape(LAYERS, 8, 128), shape(LA...  2.61 us
  transfers between devices with their start and end apart: 2, of which 1 were waited for; matrix products, arithmetic and copies ran while one was open for 0% of the time, Pallas kernels for 1%

profile of v11, /device:TPU:1, one launch (start us, length us, event | category | flops | bytes accessed | tf_op | source)
XLA Modules:
  0.0 105.3 jit_solution(3981915216131538597)
XLA Ops:
  0.6 0.0 copy-start
  0.6 1.1 %pad_maximum_fusion.both_ref = f32[2,16,4096]{2,1,0:T(8,128)S(1)} fusion(f32[1,16,4096]{2,1,0:T(8,128)} %param.3, f32[1,16,4096]{2,1,0:T(8,128)} %param.4), kind=kLoop, calls=%fused_computation | loop fusion | flops 131072 | bytes 1048576 | tf_op jit(solution)/shard_map/concatenate | solution.py:373
  1.7 0.0 copy-done
  1.7 0.1 shard_map.50
  1.9 35.6 %all_to_all.20.recv_ref = f32[16,9,8,128]{3,2,1,0:T(8,128)S(1)} all-to-all(f32[16,9,8,128]{3,2,1,0:T(8,128)S(1)} %get-tuple-element.20), channel_id=1, replica_groups=mesh['slab'=64,'layer'=16] {'layer'}, dimensions={0} | all-to-all | bytes 1179648 | tf_op jit(solution)/shard_map/all_to_all | solution.py:375
  37.5 0.1 shard_map.51
  37.6 0.1 compare_reduce_fusion
  37.8 0.7 collective-permute-start
  38.4 1.9 %collective-permute-start.1 = (f32[33,8,128]{2,1,0:T(8,128)S(1)}, f32[33,8,128]{2,1,0:T(8,128)S(1)}, u32[]{:S(2)}, u32[]{:S(2)}) collective-permute-start(f32[33,8,128]{2,1,0:T(8,128)S(1)} %get-tuple-element.25), channel_id=1, source_target_pairs={{0,16},{32,48},{64,80},{96,112},{128,144},{160,176},{192,208},{224... | collective-permute-start | bytes 405512 | tf_op jit(solution)/shard_map/ppermute | solution.py:381
  40.4 0.2 reduce-window.8
  40.5 0.6 shard_map.52
  41.1 0.1 select_reduce_fusion.rows_ref
  41.2 0.0 collective-permute-done.first_ref
  41.2 4.2 %collective-permute-done.1.second_ref = f32[33,8,128]{2,1,0:T(8,128)S(1)} collective-permute-done((f32[33,8,128]{2,1,0:T(8,128)S(1)}, f32[33,8,128]{2,1,0:T(8,128)S(1)}, u32[]{:S(2)}, u32[]{:S(2)}) %collective-permute-start.1) | collective-permute-done | bytes 135200 | tf_op jit(solution)/shard_map/ppermute | solution.py:381
  45.5 2.6 %shard_map.53 = (f32[16,8,128]{2,1,0:T(8,128)S(1)}, f32[16,12,8,128]{3,2,1,0:T(8,128)S(1)}) custom-call(s32[1]{0:T(128)} %bitcast.turn_ref, f32[33,8,128]{2,1,0:T(8,128)S(1)} %collective-permute-done.first_ref, f32[33,8,128]{2,1,0:T(8,128)S(1)} %collective-permute-done.1.second_ref, f32[17,16,384]{2,1,0:T(8,128)S(1)} %get-tuple-element.31.own_k_ref, ...), custom_call_target="tpu_custom_call" | custom-call | tf_op jit(solution)/shard_map/pallas_call | solution.py:334
  48.1 11.1 %all_to_all.21.recv_ref = f32[16,8,128]{2,1,0:T(8,128)S(1)} all-to-all(f32[16,8,128]{2,1,0:T(8,128)S(1)} %get-tuple-element.36), channel_id=1, replica_groups=mesh['slab'=64,'layer'=16] {'layer'}, dimensions={0} | all-to-all | bytes 131072 | tf_op jit(solution)/shard_map/all_to_all | solution.py:384
  59.2 0.6 shard_map.54
  59.9 27.4 %all_to_all.22.recv_ref = f32[64,4,128]{2,1,0:T(4,128)S(1)} all-to-all(f32[64,4,128]{2,1,0:T(4,128)S(1)} %shard_map.54), channel_id=1, replica_groups=mesh['slab'=64,'layer'=16] {'slab'}, dimensions={0} | all-to-all | bytes 262144 | tf_op jit(solution)/shard_map/all_to_all | solution.py:386
  87.2 0.2 shard_map.55
  87.5 16.4 %all_to_all.23.back_ref = f32[16,4,8,128]{3,2,1,0:T(8,128)S(1)} all-to-all(f32[16,4,8,128]{3,2,1,0:T(8,128)S(1)} %shard_map.55), channel_id=1, replica_groups=mesh['slab'=64,'layer'=16] {'layer'}, dimensions={0} | all-to-all | bytes 524288 | tf_op jit(solution)/shard_map/all_to_all | solution.py:387
  103.8 1.5 %shard_map.56 = (f32[1,16,4096]{2,1,0:T(8,128)}, f32[4,8,128]{2,1,0:T(8,128)}) custom-call(s32[4]{0:T(128)S(1)} %select_reduce_fusion.rows_ref, f32[64,4,128]{2,1,0:T(4,128)S(1)} %all_to_all.22.recv_ref, f32[16,4,8,128]{3,2,1,0:T(8,128)S(1)} %all_to_all.23.back_ref), custom_call_target="tpu_custom_call" | custom-call | tf_op jit(solution)/shard_map/pallas_call | solution.py:353
  (2 shorter events, 0.0 us)
Async XLA Ops:
  0.6 1.1 %copy-start = (s32[8,32]{1,0:T(8,128)S(1)}, s32[8,32]{1,0:T(8,128)}, u32[]{:S(2)}) copy-start(s32[8,32]{1,0:T(8,128)} %owner_ref.1) | copy-start | bytes 3076
  37.8 3.5 %collective-permute-start = (f32[33,8,128]{2,1,0:T(8,128)S(1)}, f32[33,8,128]{2,1,0:T(8,128)S(1)}, u32[]{:S(2)}, u32[]{:S(2)}) collective-permute-start(f32[33,8,128]{2,1,0:T(8,128)S(1)} %get-tuple-element.24), channel_id=1, source_target_pairs={{16,32},{48,64},{80,96},{112,128},{144,160},{176,192},{208,224},{2... | collective-permute-start | bytes 405512 | tf_op jit(solution)/shard_map/ppermute | solution.py:380
  38.4 7.0 %collective-permute-start.1 = (f32[33,8,128]{2,1,0:T(8,128)S(1)}, f32[33,8,128]{2,1,0:T(8,128)S(1)}, u32[]{:S(2)}, u32[]{:S(2)}) collective-permute-start(f32[33,8,128]{2,1,0:T(8,128)S(1)} %get-tuple-element.25), channel_id=1, source_target_pairs={{0,16},{32,48},{64,80},{96,112},{128,144},{160,176},{192,208},{224... | collective-permute-start | bytes 405512 | tf_op jit(solution)/shard_map/ppermute | solution.py:381

commit v12 on v10

--- a/solution.py
+++ b/solution.py
@@ -196,18 +196,15 @@
     return values[0]
 
 
-def route_kernel(owner_ref, index_ref, recv_ref, msg_ref):
-    lane = lax.broadcasted_iota(jnp.int32, (4, 128), 1)
+def route_kernel(chosen_ref, recv_ref, msg_ref):
+    lane = lax.broadcasted_iota(jnp.int32, (SLABS, 128), 1)
     shared = (lane >= 48) & (lane < 64)
-    total = tree([recv_ref[j] for j in range(LAYERS)])
-    common = total[:4]
-    for o in range(SLABS):
-        msg_ref[o] = common
-    row = index_ref[0] // PER_TILE
-    for c in range(TILE_COLS):
-        half = 4 * (c % 2)
-        strip = recv_ref[c // 2, half : half + 4]
-        msg_ref[owner_ref[row, c]] = jnp.where(shared, common, strip)
+    common = tree([recv_ref[j] for j in range(LAYERS)])
+    chosen = chosen_ref[...]
+    for q in range(4):
+        strips = jnp.concatenate([recv_ref[:, q, :], recv_ref[:, 4 + q, :]], axis=0)
+        sent = jnp.dot(chosen, strips, precision=lax.Precision.HIGHEST, preferred_element_type=F32)
+        msg_ref[:, q, :] = jnp.where(shared, common[q : q + 1], sent)
 
 
 def weights(s):
@@ -306,8 +303,14 @@
     )(turn, recv, first, second)
 
 
-def route(owner, index, recv, interpret=False):
-    return call(route_kernel, [SMEM, SMEM, VMEM], [shape(SLABS, 4, 128)], interpret=interpret)(owner, index, recv)
+def route(chosen, recv, interpret=False):
+    return call(route_kernel, [VMEM] * 2, [shape(SLABS, 4, 128)], interpret=interpret)(chosen, recv)
+
+
+def choices(table, index):
+    owners = lax.dynamic_index_in_dim(table, lax.div(index, PER_TILE), 0, keepdims=False)
+    owners = owners.reshape(TILE_COLS // 2, 2).T.reshape(1, TILE_COLS)
+    return (owners == jnp.arange(SLABS, dtype=jnp.int32)[:, None]).astype(F32)
 
 
 def combine(recv, ret, interpret=False):
@@ -334,20 +337,20 @@
 
 def per_device(adjoint_source, conductivity, tile_owner):
     index = lax.axis_index("slab")
-    place = index.reshape(1)
     turn = (index + 1).reshape(1)
     both = jnp.concatenate([conductivity, adjoint_source], axis=0)
     packed, table = pack(turn, both, tile_owner)
     recv = lax.all_to_all(packed, "layer", 0, 0, tiled=True)
     first, second = halo(turn, recv)
-    first, table = lax.optimization_barrier((first, table))
+    first, table, index = lax.optimization_barrier((first, table, index))
     rows = owned_rows(table, index)
+    chosen = choices(table, index)
     first = lax.ppermute(first, "slab", pairing(1))
     second = lax.ppermute(second, "slab", pairing(0))
-    first, second, rows = lax.optimization_barrier((first, second, rows))
+    first, second, rows, chosen = lax.optimization_barrier((first, second, rows, chosen))
     msg, ret = krylov(turn, recv, first, second)
     strips = lax.all_to_all(msg, "layer", 0, 0, tiled=True)
-    outgoing = route(table, place, strips)
+    outgoing = route(chosen, strips)
     received = lax.all_to_all(outgoing, "slab", 0, 0, tiled=True)
     back = lax.all_to_all(combine(received, ret), "layer", 0, 0, tiled=True)
     return finish(rows, received, back)

time: 106 us -> 106 us (level)
  no operation moved by 1% of the time
where the time goes in v12:
time: 106 us
  blocking collectives  90.5 us (85%)
  Pallas kernels  5.04 us (5%)
  waiting for transfers between devices  4.99 us (5%)
  starting transfers between devices  2.59 us (2%)
  other arithmetic  1.5 us (1%)
    all_to_all x1, blocking collectives, per_device(): recv = lax.all_to_all(packed, 'layer', 0, 0, tiled=True)  35.6 us
    all_to_all x1, blocking collectives, per_device(): received = lax.all_to_all(outgoing, 'slab', 0, 0, tiled=True)  27.4 us
    all_to_all x1, blocking collectives, per_device(): back = lax.all_to_all(combine(received, ret), 'layer', 0, 0, tiled=True)  16.4 us
    all_to_all x1, blocking collectives, per_device(): strips = lax.all_to_all(msg, 'layer', 0, 0, tiled=True)  11.1 us
    ppermute x1, waiting for transfers between devices, per_device(): second = lax.ppermute(second, 'slab', pairing(0))  4.99 us
    pallas_call x1, Pallas kernels, krylov(): call(krylov_kernel, [SMEM] + [VMEM] * 3, [shape(LAYERS, 8, 128), shape(LA...  2.79 us
  transfers between devices with their start and end apart: 2, of which 1 were waited for; matrix products, arithmetic and copies ran while one was open for 0% of the time, Pallas kernels for 0%

profile of v12, /device:TPU:1, one launch (start us, length us, event | category | flops | bytes accessed | tf_op | source)
XLA Modules:
  0.0 105.6 jit_solution(14901271595737503799)
XLA Ops:
  0.6 0.0 copy-start
  0.6 1.1 %pad_maximum_fusion.both_ref = f32[2,16,4096]{2,1,0:T(8,128)S(1)} fusion(f32[1,16,4096]{2,1,0:T(8,128)} %param.3, f32[1,16,4096]{2,1,0:T(8,128)} %param.4), kind=kLoop, calls=%fused_computation | loop fusion | flops 131072 | bytes 1048576 | tf_op jit(solution)/shard_map/concatenate | solution.py:341
  1.7 0.0 copy-done
  1.7 0.1 shard_map.50
  1.9 35.6 %all_to_all.20.recv_ref = f32[16,9,8,128]{3,2,1,0:T(8,128)S(1)} all-to-all(f32[16,9,8,128]{3,2,1,0:T(8,128)S(1)} %get-tuple-element.15), channel_id=1, replica_groups=mesh['slab'=64,'layer'=16] {'layer'}, dimensions={0} | all-to-all | bytes 1179648 | tf_op jit(solution)/shard_map/all_to_all | solution.py:343
  37.5 0.1 shard_map.51
  37.6 0.1 compare_reduce_fusion
  37.8 0.2 reduce-window.8
  38.0 0.1 reshape.47
  38.0 0.1 copy.7
  38.1 0.1 eq.39
  38.2 0.7 collective-permute-start
  38.9 1.9 %collective-permute-start.1 = (f32[33,8,128]{2,1,0:T(8,128)S(1)}, f32[33,8,128]{2,1,0:T(8,128)S(1)}, u32[]{:S(2)}, u32[]{:S(2)}) collective-permute-start(f32[33,8,128]{2,1,0:T(8,128)S(1)} %get-tuple-element.19), channel_id=1, source_target_pairs={{0,16},{32,48},{64,80},{96,112},{128,144},{160,176},{192,208},{224... | collective-permute-start | bytes 405512 | tf_op jit(solution)/shard_map/ppermute | solution.py:349
  40.8 0.1 select_reduce_fusion.rows_ref
  41.0 0.0 collective-permute-done.first_ref
  41.0 5.0 %collective-permute-done.1.second_ref = f32[33,8,128]{2,1,0:T(8,128)S(1)} collective-permute-done((f32[33,8,128]{2,1,0:T(8,128)S(1)}, f32[33,8,128]{2,1,0:T(8,128)S(1)}, u32[]{:S(2)}, u32[]{:S(2)}) %collective-permute-start.1) | collective-permute-done | bytes 135200 | tf_op jit(solution)/shard_map/ppermute | solution.py:349
  46.0 2.8 %shard_map.52 = (f32[16,8,128]{2,1,0:T(8,128)S(1)}, f32[16,12,8,128]{3,2,1,0:T(8,128)S(1)}) custom-call(s32[1]{0:T(128)} %bitcast.turn_ref, f32[16,9,8,128]{3,2,1,0:T(8,128)S(1)} %all_to_all.20.recv_ref, f32[33,8,128]{2,1,0:T(8,128)S(1)} %collective-permute-done.first_ref, f32[33,8,128]{2,1,0:T(8,128)S(1)} %collective-permute-done.1.second_ref), custom_call_target="tpu_custom_call" | custom-call | tf_op jit(solution)/shard_map/pallas_call | solution.py:297
  48.7 11.1 %all_to_all.21.recv_ref = f32[16,8,128]{2,1,0:T(8,128)S(1)} all-to-all(f32[16,8,128]{2,1,0:T(8,128)S(1)} %get-tuple-element.26), channel_id=1, replica_groups=mesh['slab'=64,'layer'=16] {'layer'}, dimensions={0} | all-to-all | bytes 131072 | tf_op jit(solution)/shard_map/all_to_all | solution.py:352
  59.9 0.3 shard_map.53
  60.2 27.4 %all_to_all.22.recv_ref = f32[64,4,128]{2,1,0:T(4,128)S(1)} all-to-all(f32[64,4,128]{2,1,0:T(4,128)S(1)} %shard_map.53), channel_id=1, replica_groups=mesh['slab'=64,'layer'=16] {'slab'}, dimensions={0} | all-to-all | bytes 262144 | tf_op jit(solution)/shard_map/all_to_all | solution.py:354
  87.5 0.2 shard_map.54
  87.8 16.4 %all_to_all.23.back_ref = f32[16,4,8,128]{3,2,1,0:T(8,128)S(1)} all-to-all(f32[16,4,8,128]{3,2,1,0:T(8,128)S(1)} %shard_map.54), channel_id=1, replica_groups=mesh['slab'=64,'layer'=16] {'layer'}, dimensions={0} | all-to-all | bytes 524288 | tf_op jit(solution)/shard_map/all_to_all | solution.py:355
  104.1 1.5 %shard_map.55 = (f32[1,16,4096]{2,1,0:T(8,128)}, f32[4,8,128]{2,1,0:T(8,128)}) custom-call(s32[4]{0:T(128)S(1)} %select_reduce_fusion.rows_ref, f32[64,4,128]{2,1,0:T(4,128)S(1)} %all_to_all.22.recv_ref, f32[16,4,8,128]{3,2,1,0:T(8,128)S(1)} %all_to_all.23.back_ref), custom_call_target="tpu_custom_call" | custom-call | tf_op jit(solution)/shard_map/pallas_call | solution.py:322
  (4 shorter events, 0.0 us)
Async XLA Ops:
  0.6 1.1 %copy-start = (s32[8,32]{1,0:T(8,128)S(1)}, s32[8,32]{1,0:T(8,128)}, u32[]{:S(2)}) copy-start(s32[8,32]{1,0:T(8,128)} %owner_ref.1) | copy-start | bytes 3076
  38.2 2.7 %collective-permute-start = (f32[33,8,128]{2,1,0:T(8,128)S(1)}, f32[33,8,128]{2,1,0:T(8,128)S(1)}, u32[]{:S(2)}, u32[]{:S(2)}) collective-permute-start(f32[33,8,128]{2,1,0:T(8,128)S(1)} %get-tuple-element.18), channel_id=1, source_target_pairs={{16,32},{48,64},{80,96},{112,128},{144,160},{176,192},{208,224},{2... | collective-permute-start | bytes 405512 | tf_op jit(solution)/shard_map/ppermute | solution.py:348
  38.9 7.0 %collective-permute-start.1 = (f32[33,8,128]{2,1,0:T(8,128)S(1)}, f32[33,8,128]{2,1,0:T(8,128)S(1)}, u32[]{:S(2)}, u32[]{:S(2)}) collective-permute-start(f32[33,8,128]{2,1,0:T(8,128)S(1)} %get-tuple-element.19), channel_id=1, source_target_pairs={{0,16},{32,48},{64,80},{96,112},{128,144},{160,176},{192,208},{224... | collective-permute-start | bytes 405512 | tf_op jit(solution)/shard_map/ppermute | solution.py:349
